TPU v7x, 32 devices: a whole 2x2x4 slice. The times are simulated.
32 devices in a mesh: dp: 4 (over y, x), expert: 8 (over z, core).
Axes of the slice: x: 2, y: 2, z: 4, core: 2. Of those that a mesh axis runs over, the one named last changes fastest.
Arguments:
- hidden_acts: bfloat16 [4, 8, 1024, 768], P('dp', 'expert'), may hold values from -6 to 6
- out_grads: bfloat16 [4, 8, 1024, 2048], P('dp', 'expert'), may hold values from -0.29882812 to 0.29882812
- row_counts: int32 [4, 8], P('dp', 'expert'), may hold values from 128 to 1024, as said below
- plan_now: int32 [4, 8], replicated, may hold values from 0 to 2, as said below
- plan_next: int32 [4, 8], replicated, may hold values from 0 to 2, as said below
- master: float32 [3, 768, 2048], P(None, 'expert', 'dp'), may hold values from -6 to 6
- moment_one: float32 [3, 768, 2048], P(None, 'expert', 'dp'), may hold values from -6 to 6
- moment_two: float32 [3, 768, 2048], P(None, 'expert', 'dp'), may hold values from 0.01 to 0.3
Outputs:
- master_new: float32 [3, 768, 2048], P(None, 'expert', 'dp')
- moment_one_new: float32 [3, 768, 2048], P(None, 'expert', 'dp')
- moment_two_new: float32 [3, 768, 2048], P(None, 'expert', 'dp')
- replica_weights: bfloat16 [4, 8, 768, 2048], P('dp', 'expert')
Inputs may be any that keep to these rules, and one draw needn't show every extreme that they name: `plan_now`: every expert is named by 1 to 16 devices, and some expert by exactly 16. `plan_next`: every expert is named by 1 to 16 devices, and some expert by exactly 16. `row_counts`: A multiple of 128; rows from it on are padding. Some device has all 1024 rows live.
All inputs are finite; a program needn't handle non-finite values.
Results may differ from a plain program's by a relative error of at most 0.005.
Values may be sent and summed in bfloat16 or wider, within the bound.
No kernel may reach another device: no remote copies, remote signals or barrier semaphores. Data moves between devices by JAX's collectives and lax.ppermute only.
A program may use at most 192 MiB of HBM per device.

v0:
```python
import jax
import jax.numpy as jnp
from jax import lax
from jax.sharding import PartitionSpec as P

beta_one = 0.9
beta_two = 0.999
learn_rate = 0.1
epsilon = 1e-08
first_fix = 1.0 - beta_one**10
second_fix = 1.0 - beta_two**10


def per_device(
    hidden_acts, out_grads, row_counts, plan_now, plan_next, master, moment_one, moment_two
):
    ex_count = lax.axis_size("expert")
    dp_index = lax.axis_index("dp")
    experts = master.shape[0]
    piece_rows = master.shape[1]
    hidden = hidden_acts[0, 0]
    upstream = out_grads[0, 0]
    width = upstream.shape[1]
    row_index = jnp.arange(hidden.shape[0], dtype=jnp.int32)
    row_mask = (row_index < row_counts[0, 0]).astype(hidden.dtype)[:, None]
    partial_value = lax.dot_general(
        hidden * row_mask, upstream, (((0,), (0,)), ((), ())), preferred_element_type=jnp.float32
    ).astype(jnp.bfloat16)
    expert_ids = jnp.arange(experts, dtype=jnp.int32)
    pieces = lax.all_to_all(
        partial_value.reshape(ex_count, piece_rows, width),
        "expert",
        split_axis=0,
        concat_axis=0,
        tiled=True,
    )
    sender_ids = lax.dynamic_index_in_dim(plan_now, dp_index, 0, keepdims=False)
    onehot = (sender_ids[None, :] == expert_ids[:, None]).astype(jnp.bfloat16)
    totals = jnp.einsum("es,srd->erd", onehot, pieces, preferred_element_type=jnp.float32)
    grad_sum = lax.psum_scatter(
        totals.astype(jnp.bfloat16), "dp", scatter_dimension=2, tiled=True
    ).astype(jnp.float32)
    moment_one_new = beta_one * moment_one + (1.0 - beta_one) * grad_sum
    moment_two_new = beta_two * moment_two + (1.0 - beta_two) * grad_sum * grad_sum
    master_new = master - learn_rate * (moment_one_new / first_fix) / (
        jnp.sqrt(moment_two_new / second_fix) + epsilon
    )
    rounded = master_new.astype(jnp.bfloat16)
    full_cols = lax.all_gather(rounded, "dp", axis=2, tiled=True)
    targets = lax.dynamic_index_in_dim(plan_next, dp_index, 0, keepdims=False)
    outgoing = jnp.take(full_cols, targets, axis=0)
    incoming = lax.all_to_all(outgoing, "expert", split_axis=0, concat_axis=0, tiled=True)
    replica = incoming.reshape(ex_count * piece_rows, width)
    return (master_new, moment_one_new, moment_two_new, replica[None, None])


def solution(mesh):
    return jax.shard_map(
        per_device,
        mesh=mesh,
        in_specs=(
            P("dp", "expert", None, None),
            P("dp", "expert", None, None),
            P("dp", "expert"),
            P(),
            P(),
            P(None, "expert", "dp"),
            P(None, "expert", "dp"),
            P(None, "expert", "dp"),
        ),
        out_specs=(
            P(None, "expert", "dp"),
            P(None, "expert", "dp"),
            P(None, "expert", "dp"),
            P("dp", "expert", None, None),
        ),
        check_vma=False,
    )
```

profile of v0, /device:TPU:0, one launch (start us, length us, event | category | flops | bytes accessed | tf_op | source)
XLA Modules:
  0.0 420.7 jit_solution(8020616843771676299)
XLA Ops:
  7.2 0.0 copy-start
  7.9 7.9 %fusion.2 = bf16[768,2048]{1,0:T(8,128)(2,1)} fusion(bf16[1,1,1024,2048]{3,2,1,0:T(8,128)(2,1)} %param.9, bf16[1,1,1024,768]{3,2,1,0:T(8,128)(2,1)} %param.8, bf16[1024]{0:T(1024)(128)(2,1)S(1)} %fusion.15), kind=kOutput, calls=%fused_computation.3 | convolution fusion | flops 3223584768 | bytes 8914944 | tf_op jit(solution)/shard_map/dot_general | solution.py:26
  15.8 6.3 %all-to-all-start = ((bf16[8,96,2048]{2,1,0:T(8,128)(2,1)}), bf16[8,96,2048]{2,1,0:T(8,128)(2,1)S(1)}, u32[]{:S(2)}, u32[]{:S(2)}) async-start(bf16[8,96,2048]{2,1,0:T(8,128)(2,1)} %bitcast.29), calls=%async_computation | async-start | bytes 6291456 | tf_op jit(solution)/shard_map/all_to_all | solution.py:30
  22.1 0.0 reduce-scatter.4.cloned.1.call-start
  22.1 0.0 copy-done
  22.2 71.5 %all-to-all-done = bf16[8,96,2048]{2,1,0:T(8,128)(2,1)S(1)} async-done(((bf16[8,96,2048]{2,1,0:T(8,128)(2,1)}), bf16[8,96,2048]{2,1,0:T(8,128)(2,1)S(1)}, u32[]{:S(2)}, u32[]{:S(2)}) %all-to-all-start) | async-done | bytes 3145760 | tf_op jit(solution)/shard_map/all_to_all | solution.py:30
  93.6 3.5 fusion.7
  97.1 78.7 %copy.29 = bf16[3,96,2048]{0,1,2:T(8,128)(2,1)} copy(bf16[3,96,2048]{2,0,1:T(4,128)(2,1)} %fusion.7) | data formatting | bytes 2359296
  175.8 57.2 %reshape.68 = bf16[2048,288]{1,0:T(8,128)(2,1)} reshape(bf16[2048,96,3]{2,1,0:T(8,128)(2,1)} %bitcast.26) | data formatting | bytes 2359296
  233.1 0.0 reduce-scatter.4.cloned.1.call-update
  233.1 0.2 all-gather.2.cloned.1.call-start
  233.3 29.7 %reduce-scatter.4.cloned.1.call-done = bf16[512,288]{1,0:T(8,128)(2,1)} async-done(((bf16[2048,288]{1,0:T(8,128)(2,1)}), bf16[512,288]{1,0:T(8,128)(2,1)}) %reduce-scatter.4.cloned.1.call-update) | async-done | bytes 294928
  263.1 28.2 %reshape.69 = bf16[512,96,3]{2,1,0:T(8,128)(2,1)} reshape(bf16[512,288]{1,0:T(8,128)(2,1)} %reduce-scatter.4.cloned.1.call-done) | data formatting | bytes 589824
  291.2 0.0 copy-start.2
  291.2 0.0 copy-start.3
  291.2 0.0 copy-start.4
  291.2 13.2 %copy.28 = bf16[3,96,512]{2,1,0:T(8,128)(2,1)S(1)} copy(bf16[3,96,512]{0,1,2:T(8,128)(2,1)} %bitcast.27) | data formatting | bytes 589824 | tf_op jit(solution)/shard_map/reduce_scatter | solution.py:40
  304.5 0.0 copy-done.2
  304.5 0.0 copy-done.3
  304.5 0.0 copy-done.4
  304.5 0.0 copy-start.5
  304.5 1.6 fusion.20
  306.1 0.0 all-gather.2.cloned.1.call-update
  306.1 0.0 copy-done.5
  306.2 27.7 %all-gather.2.cloned.1.call-done = bf16[3,96,2048]{2,1,0:T(8,128)(2,1)} async-done(((bf16[3,96,512]{2,1,0:T(8,128)(2,1)}), bf16[3,96,2048]{2,1,0:T(8,128)(2,1)}) %all-gather.2.cloned.1.call-update) | async-done | bytes 1179664 | tf_op jit(solution)/shard_map/all_gather | solution.py:49
  333.8 2.0 gather_fusion
  335.9 0.4 broadcast_select_fusion
  336.2 75.9 %all_to_all.10 = bf16[8,96,2048]{2,1,0:T(8,128)(2,1)S(1)} all-to-all(bf16[8,96,2048]{2,1,0:T(8,128)(2,1)S(1)} %broadcast_select_fusion), channel_id=1, replica_groups=mesh['dp'=4,'expert'=8] {'expert'}, dimensions={0} | all-to-all | bytes 6291456 | tf_op jit(solution)/shard_map/all_to_all | solution.py:52
  412.2 0.0 copy-start.1
  412.2 1.7 copy.38
  413.9 0.0 copy-done.1
  (5 shorter events, 0.0 us)
Async XLA Ops:
  7.2 15.0 %copy-start = (s32[4,8]{1,0:T(4,128)S(1)}, s32[4,8]{1,0:T(4,128)}, u32[]{:S(2)}) copy-start(s32[4,8]{1,0:T(4,128)} %param.11) | copy-start | bytes 388
  15.8 77.9 %all-to-all-start = ((bf16[8,96,2048]{2,1,0:T(8,128)(2,1)}), bf16[8,96,2048]{2,1,0:T(8,128)(2,1)S(1)}, u32[]{:S(2)}, u32[]{:S(2)}) async-start(bf16[8,96,2048]{2,1,0:T(8,128)(2,1)} %bitcast.29), calls=%async_computation | async-start | bytes 6291456 | tf_op jit(solution)/shard_map/all_to_all | solution.py:30
  22.1 241.0 %reduce-scatter.4.cloned.1.call-start = ((), (), s32[]{:S(2)}) async-start(), calls=%async_computation.4 | async-start | bytes 1966080
  233.1 100.8 %all-gather.2.cloned.1.call-start = ((), (), s32[]{:S(2)}) async-start(), calls=%async_computation.3 | async-start | bytes 1474560 | tf_op jit(solution)/shard_map/all_gather | solution.py:49
  291.2 13.3 %copy-start.2 = (f32[3,96,512]{2,1,0:T(8,128)S(1)}, f32[3,96,512]{2,1,0:T(8,128)}, u32[]{:S(2)}) copy-start(f32[3,96,512]{2,1,0:T(8,128)} %param.13) | copy-start | bytes 1769476
  291.2 13.3 %copy-start.3 = (f32[3,96,512]{2,1,0:T(8,128)S(1)}, f32[3,96,512]{2,1,0:T(8,128)}, u32[]{:S(2)}) copy-start(f32[3,96,512]{2,1,0:T(8,128)} %param.14) | copy-start | bytes 1769476
  291.2 13.3 %copy-start.4 = (f32[3,96,512]{2,1,0:T(8,128)S(1)}, f32[3,96,512]{2,1,0:T(8,128)}, u32[]{:S(2)}) copy-start(f32[3,96,512]{2,1,0:T(8,128)} %param.15) | copy-start | bytes 1769476
  304.5 1.6 copy-start.5
  412.2 1.7 copy-start.1
Sparse Core Ops, SparseCore 0:
  233.2 29.8 reduce-scatter.3
  306.2 27.5 all-gather.1
where the time goes:
time: 422 us; the launch traced here: 421 us
  local copies, waits for them, and re-layouts  181 us (43%)
  waiting for transfers between devices  129 us (31%)
  blocking collectives  75.9 us (18%)
  between operations  14.8 us (4%)
  matrix products  11.4 us (3%)
  starting transfers between devices  6.58 us (2%)
    unnamed x16, local copies, waits for them, and re-layouts  166 us
    all_to_all x1, blocking collectives, per_device(): lax.all_to_all(outgoing, 'expert', split_axis=0, concat_axis=0, tiled=True)  75.9 us
    all_to_all x1, waiting for transfers between devices, per_device(): lax.all_to_all(partial_value.reshape(ex_count, piece_rows, width), 'exper...  71.5 us
    unnamed x3, waiting for transfers between devices  29.8 us
    all_gather x1, waiting for transfers between devices, per_device(): full_cols = lax.all_gather(rounded, 'dp', axis=2, tiled=True)  27.7 us
    reduce_scatter x1, local copies, waits for them, and re-layouts, per_device(): lax.psum_scatter(totals.astype(jnp.bfloat16), 'dp', scatter_dimension=2,...  13.2 us
  transfers between devices with their start and end apart: 3, of which 3 were waited for; matrix products, arithmetic and copies ran while one was open for 0% of the time, Pallas kernels for 0%

commit v1 on v0

--- a/solution.py
+++ b/solution.py
@@ -1,6 +1,10 @@
+import functools
+
 import jax
 import jax.numpy as jnp
 from jax import lax
+from jax.experimental import pallas as pl
+from jax.experimental.pallas import tpu as pltpu
 from jax.sharding import PartitionSpec as P
 
 beta_one = 0.9
@@ -10,8 +14,187 @@
 first_fix = 1.0 - beta_one**10
 second_fix = 1.0 - beta_two**10
 
-
-def per_device(
+AXES = ("dp", "expert")
+
+
+def adam(grad_sum, master, moment_one, moment_two):
+    moment_one_new = beta_one * moment_one + (1.0 - beta_one) * grad_sum
+    moment_two_new = beta_two * moment_two + (1.0 - beta_two) * grad_sum * grad_sum
+    master_new = master - learn_rate * (moment_one_new / first_fix) / (
+        jnp.sqrt(moment_two_new / second_fix) + epsilon
+    )
+    return master_new, moment_one_new, moment_two_new
+
+
+def matmul_kernel(place, hidden_ref, upstream_ref, keep_ref, send_ref, turned):
+    planes, unused, rows, unused = keep_ref.shape
+
+    @pl.when(pl.program_id(0) == 0)
+    def turn():
+        hidden = hidden_ref[...]
+        live = lax.broadcasted_iota(jnp.int32, hidden.shape, 0) < place[3]
+        turned[...] = jnp.where(live, hidden, jnp.zeros_like(hidden)).T
+
+    product = jnp.dot(turned[...], upstream_ref[...], preferred_element_type=jnp.float32)
+    product = product.astype(jnp.bfloat16)
+    even_core = place[2] == 0
+    for plane in range(planes):
+        even = product[2 * plane * rows : (2 * plane + 1) * rows]
+        odd = product[(2 * plane + 1) * rows : (2 * plane + 2) * rows]
+        ahead = lax.rem(plane - place[1] + planes, planes)
+        keep_ref[ahead, 0] = jnp.where(even_core, even, odd)
+        send_ref[ahead, 0] = jnp.where(even_core, odd, even)
+
+
+def partial_blocks(place, hidden, upstream, groups, planes):
+    tokens, inner = hidden.shape
+    width = upstream.shape[1]
+    cols = width // groups
+    rows = inner // (2 * planes)
+    out = jax.ShapeDtypeStruct((planes, groups, rows, cols), jnp.bfloat16)
+    out_spec = pl.BlockSpec((planes, 1, rows, cols), lambda j, place: (0, j, 0, 0))
+    return pl.pallas_call(
+        matmul_kernel,
+        grid_spec=pltpu.PrefetchScalarGridSpec(
+            num_scalar_prefetch=1,
+            grid=(groups,),
+            in_specs=[
+                pl.BlockSpec((tokens, inner), lambda j, place: (0, 0)),
+                pl.BlockSpec((tokens, cols), lambda j, place: (0, place[0] ^ j)),
+            ],
+            out_specs=[out_spec, out_spec],
+            scratch_shapes=[pltpu.VMEM((inner, tokens), jnp.bfloat16)],
+        ),
+        out_shape=[out, out],
+        compiler_params=pltpu.CompilerParams(vmem_limit_bytes=40 * 2**20),
+        cost_estimate=pl.CostEstimate(
+            flops=2 * tokens * inner * width,
+            bytes_accessed=2 * (tokens * inner + tokens * width + inner * width),
+            transcendentals=0,
+        ),
+        name="partial_blocks",
+    )(place, hidden, upstream)
+
+
+def assemble_kernel(groups, planes, place, *refs):
+    mine = refs[: planes * groups]
+    other = refs[planes * groups : planes * groups + planes]
+    out_ref = refs[-2]
+    sems = refs[-1]
+    rows, cols = mine[0].shape[1:]
+    copies = []
+    for s in range(planes):
+        plane = lax.rem(place[1] - s + planes, planes)
+        for i in range(2):
+            row = pl.multiple_of((2 * plane + (place[2] ^ i)) * rows, rows)
+            for j in range(groups):
+                col = pl.multiple_of((place[0] ^ j) * cols, cols)
+                src = mine[s * groups + j].at[0] if i == 0 else other[s].at[j]
+                copies.append(
+                    pltpu.make_async_copy(
+                        src, out_ref.at[pl.ds(row, rows), pl.ds(col, cols)], sems.at[len(copies)]
+                    )
+                )
+    for copy in copies:
+        copy.start()
+    for copy in copies:
+        copy.wait()
+
+
+def assemble(place, mine, other, groups, planes):
+    rows, cols = mine[0].shape[1:]
+    return pl.pallas_call(
+        functools.partial(assemble_kernel, groups, planes),
+        in_specs=[pl.BlockSpec(memory_space=pltpu.SMEM)]
+        + [pl.BlockSpec(memory_space=pl.ANY)] * (len(mine) + len(other)),
+        out_specs=pl.BlockSpec(memory_space=pl.ANY),
+        scratch_shapes=[pltpu.SemaphoreType.DMA((2 * planes * groups,))],
+        out_shape=jax.ShapeDtypeStruct((2 * planes * rows, groups * cols), jnp.bfloat16),
+        cost_estimate=pl.CostEstimate(
+            flops=0, bytes_accessed=8 * planes * rows * groups * cols, transcendentals=0
+        ),
+        name="assemble",
+    )(place, *mine, *other)
+
+
+def per_device_planes(
+    hidden_acts, out_grads, row_counts, plan_now, plan_next, master, moment_one, moment_two
+):
+    groups = lax.axis_size("dp")
+    owners = lax.axis_size("expert")
+    planes = owners // 2
+    group = lax.axis_index("dp")
+    owner = lax.axis_index("expert")
+    plane, core = owner // 2, owner % 2
+    experts = master.shape[0]
+    place = jnp.stack([group, plane, core, row_counts[0, 0]]).astype(jnp.int32)
+
+    everyone = range(groups * owners)
+    to_core = [(d, d ^ 1) for d in everyone]
+    to_group = [[(d, d ^ (j * owners)) for d in everyone] for j in range(groups)]
+    to_plane = [
+        [(d, d // owners * owners + (d % owners + 2 * s) % owners) for d in everyone] for s in range(planes)
+    ]
+    order = sorted(range(planes), key=lambda s: -min(s, planes - s))
+
+    near_groups = jnp.stack([group ^ j for j in range(groups)])
+    near_owners = jnp.stack([owner, owner ^ 1])
+    now = plan_now[near_groups][:, near_owners]
+    later = plan_next[near_groups][:, near_owners]
+
+    keep, send = partial_blocks(place, hidden_acts[0, 0], out_grads[0, 0], groups, planes)
+    held = lax.ppermute(send, AXES, to_core)
+
+    arrived = {}
+    own_sum = None
+    for s in order:
+        sums = [jnp.float32(0.0)] * experts
+        for j in range(groups):
+            block = jnp.stack([keep[s, j], held[s, j]])
+            if j:
+                block = lax.ppermute(block, AXES, to_group[j])
+            block = block.astype(jnp.float32)
+            for i in range(2):
+                sums = [
+                    sums[e] + jnp.where(now[j, i] == e, block[i], jnp.float32(0.0)) for e in range(experts)
+                ]
+        total = jnp.stack(sums)
+        if s:
+            arrived[s] = lax.ppermute(total.astype(jnp.bfloat16), AXES, to_plane[s])
+        else:
+            own_sum = total
+    grad_sum = own_sum
+    for s in range(1, planes):
+        grad_sum = grad_sum + arrived[s].astype(jnp.float32)
+
+    master_new, moment_one_new, moment_two_new = adam(grad_sum, master, moment_one, moment_two)
+    rounded = master_new.astype(jnp.bfloat16)
+
+    mine = {}
+    other = {}
+    for s in order[::-1]:
+        shard = lax.ppermute(rounded, AXES, to_plane[s]) if s else rounded
+        passed_on = []
+        for j in range(groups):
+            block = jnp.stack(
+                [lax.dynamic_index_in_dim(shard, later[j, i], 0, keepdims=False) for i in range(2)]
+            )
+            if j:
+                block = lax.ppermute(block, AXES, to_group[j])
+            mine[s, j] = block
+            passed_on.append(block[1])
+        other[s] = lax.ppermute(jnp.stack(passed_on), AXES, to_core)
+    replica = assemble(
+        place,
+        [mine[s, j] for s in range(planes) for j in range(groups)],
+        [other[s] for s in range(planes)],
+        groups,
+        planes,
+    )
+    return (master_new, moment_one_new, moment_two_new, replica[None, None])
+
+
+def per_device_whole(
     hidden_acts, out_grads, row_counts, plan_now, plan_next, master, moment_one, moment_two
 ):
     ex_count = lax.axis_size("expert")
@@ -40,11 +223,7 @@
     grad_sum = lax.psum_scatter(
         totals.astype(jnp.bfloat16), "dp", scatter_dimension=2, tiled=True
     ).astype(jnp.float32)
-    moment_one_new = beta_one * moment_one + (1.0 - beta_one) * grad_sum
-    moment_two_new = beta_two * moment_two + (1.0 - beta_two) * grad_sum * grad_sum
-    master_new = master - learn_rate * (moment_one_new / first_fix) / (
-        jnp.sqrt(moment_two_new / second_fix) + epsilon
-    )
+    master_new, moment_one_new, moment_two_new = adam(grad_sum, master, moment_one, moment_two)
     rounded = master_new.astype(jnp.bfloat16)
     full_cols = lax.all_gather(rounded, "dp", axis=2, tiled=True)
     targets = lax.dynamic_index_in_dim(plan_next, dp_index, 0, keepdims=False)
@@ -52,6 +231,16 @@
     incoming = lax.all_to_all(outgoing, "expert", split_axis=0, concat_axis=0, tiled=True)
     replica = incoming.reshape(ex_count * piece_rows, width)
     return (master_new, moment_one_new, moment_two_new, replica[None, None])
+
+
+def per_device(hidden_acts, out_grads, row_counts, plan_now, plan_next, master, *moments):
+    groups = lax.axis_size("dp")
+    owners = lax.axis_size("expert")
+    experts, rows, cols = master.shape
+    few = experts <= 2 * groups and owners <= 8
+    even = owners % 2 == 0 and groups & (groups - 1) == 0 and rows % 16 == 0 and cols % 128 == 0
+    body = per_device_planes if few and even else per_device_whole
+    return body(hidden_acts, out_grads, row_counts, plan_now, plan_next, master, *moments)
 
 
 def solution(mesh):

time: 422 us -> 272 us (0.64)
  local copies, waits for them, and re-layouts: 181 us -> 11.2 us
  Pallas kernels: 0 us -> 103 us
  blocking collectives: 75.9 us -> 0 us
  waiting for transfers between devices: 129 us -> 68.9 us
  starting transfers between devices: 6.58 us -> 47.4 us
  between operations: 14.8 us -> 31.9 us
  matrix products: 11.4 us -> 0 us
  other arithmetic: 1.98 us -> 8.04 us
    unnamed x16 -> x48, local copies, waits for them, and re-layouts: 166 us -> 5.41 us
    pallas_call x0 -> x2, Pallas kernels: none -> 103 us  [the longest x1 97.3 us: assemble(): pl.pallas_call(functools.partial(assemble_kernel, groups, planes), in_spe...]
    all_to_all x1 -> x0, blocking collectives: 75.9 us -> none  [per_device(): lax.all_to_all(outgoing, 'expert', split_axis=0, concat_axis=0, tiled=True)]
    all_to_all x1 -> x0, waiting for transfers between devices: 71.5 us -> none  [per_device(): lax.all_to_all(partial_value.reshape(ex_count, piece_rows, width), 'exper...]
    ppermute x0 -> x35, waiting for transfers between devices: none -> 68.9 us  [the longest x24 31.1 us: per_device_planes(): block = lax.ppermute(block, AXES, to_group[j])]
    ppermute x0 -> x35, starting transfers between devices: none -> 47.4 us  [the longest x24 34.9 us: per_device_planes(): block = lax.ppermute(block, AXES, to_group[j])]
    unnamed x3 -> x0, waiting for transfers between devices: 29.8 us -> none
    all_gather x1 -> x0, waiting for transfers between devices: 27.7 us -> none  [per_device(): full_cols = lax.all_gather(rounded, 'dp', axis=2, tiled=True)]
  transfers between devices with their start and end apart: 3 -> 35, of which waited for: 3 -> 17; matrix products, arithmetic and copies ran while one was open for 0% -> 4% of each run, Pallas kernels for 0% -> 0%
where the time goes in v1:
time: 272 us; the launch traced here: 270 us
  Pallas kernels  103 us (38%)
  waiting for transfers between devices  68.9 us (25%)
  starting transfers between devices  47.4 us (17%)
  between operations  31.9 us (12%)
  local copies, waits for them, and re-layouts  11.2 us (4%)
  other arithmetic  8.04 us (3%)
    pallas_call x1, Pallas kernels, assemble(): pl.pallas_call(functools.partial(assemble_kernel, groups, planes), in_spe...  97.3 us
    ppermute x24, starting transfers between devices, per_device_planes(): block = lax.ppermute(block, AXES, to_group[j])  34.9 us
    ppermute x24, waiting for transfers between devices, per_device_planes(): block = lax.ppermute(block, AXES, to_group[j])  31.1 us
    ppermute x3, waiting for transfers between devices, per_device_planes(): arrived[s] = lax.ppermute(total.astype(jnp.bfloat16), AXES, to_plane[s])  22.1 us
    ppermute x3, waiting for transfers between devices, per_device_planes(): shard = lax.ppermute(rounded, AXES, to_plane[s]) if s else rounded  15.7 us
    ppermute x3, starting transfers between devices, per_device_planes(): shard = lax.ppermute(rounded, AXES, to_plane[s]) if s else rounded  7.01 us
    pallas_call x1, Pallas kernels, partial_blocks(): pl.pallas_call(matmul_kernel, grid_spec=pltpu.PrefetchScalarGridSpec(num_...  5.62 us
  transfers between devices with their start and end apart: 35, of which 17 were waited for; matrix products, arithmetic and copies ran while one was open for 4% of the time, Pallas kernels for 0%

profile of v1, /device:TPU:0, one launch (start us, length us, event | category | flops | bytes accessed | tf_op | source)
XLA Modules:
  0.0 270.3 jit_solution(14407202117294507058)
XLA Ops:
  1.4 2.2 copy-done.2
  3.6 1.4 copy-done.3
  5.0 5.6 %partial_blocks.1 = (bf16[4,4,96,512]{3,2,1,0:T(8,128)(2,1)S(1)}, bf16[4,4,96,512]{3,2,1,0:T(8,128)(2,1)S(1)}) custom-call(s32[4]{0:T(128)S(1)} %pad_add_fusion.place, bf16[1024,768]{1,0:T(8,128)(2,1)S(1)} %bitcast.117, bf16[1024,2048]{1,0:T(8,128)(2,1)S(1)} %bitcast.116), custom_call_target="tpu_custom_call" | custom-call | flops 3221225472 | bytes 8912896 | tf_op jit(solution)/shard_map/partial_blocks/pallas_call | solution.py:56
  10.6 0.5 collective-permute-start
  11.2 0.6 gather_fusion.2
  12.0 0.6 gather_fusion.3
  12.5 0.7 fusion.7
  22.9 0.6 gather_fusion
  23.6 0.6 gather_fusion.1
  24.1 0.7 fusion.8
  44.9 1.6 slice_bitcast_fusion.15
  46.5 2.6 collective-permute-start.4
  49.1 1.6 collective-permute-start.5
  50.7 0.6 collective-permute-start.12
  51.5 3.0 %collective-permute-start.14 = (bf16[2,96,512]{2,1,0:T(8,128)(2,1)S(1)}, bf16[2,96,512]{2,1,0:T(8,128)(2,1)S(1)}, u32[]{:S(2)}, u32[]{:S(2)}) collective-permute-start(bf16[2,96,512]{2,1,0:T(8,128)(2,1)S(1)} %pad_maximum_fusion.18), channel_id=1, source_target_pairs={{0,24},{1,25},{2,26},{3,27},{4,28},{5,29},{6,30},{7,31},{8,16},{9,... | collective-permute-start | bytes 589832 | tf_op jit(solution)/shard_map/ppermute | solution.py:155
  54.9 1.9 collective-permute-start.1
  56.9 1.5 collective-permute-start.2
  58.5 0.6 collective-permute-done.12
  59.1 2.9 %collective-permute-start.3 = (bf16[2,96,512]{2,1,0:T(8,128)(2,1)S(1)}, bf16[2,96,512]{2,1,0:T(8,128)(2,1)S(1)}, u32[]{:S(2)}, u32[]{:S(2)}) collective-permute-start(bf16[2,96,512]{2,1,0:T(8,128)(2,1)S(1)} %pad_maximum_fusion.9), channel_id=1, source_target_pairs={{0,24},{1,25},{2,26},{3,27},{4,28},{5,29},{6,30},{7,31},{8,16},{9,... | collective-permute-start | bytes 589832 | tf_op jit(solution)/shard_map/ppermute | solution.py:155
  62.0 3.3 %collective-permute-done.13 = bf16[2,96,512]{2,1,0:T(8,128)(2,1)S(1)} collective-permute-done((bf16[2,96,512]{2,1,0:T(8,128)(2,1)S(1)}, bf16[2,96,512]{2,1,0:T(8,128)(2,1)S(1)}, u32[]{:S(2)}, u32[]{:S(2)}) %collective-permute-start.13) | collective-permute-done | bytes 196640 | tf_op jit(solution)/shard_map/ppermute | solution.py:155
  65.4 1.5 collective-permute-start.6
  66.9 1.6 collective-permute-start.8
  68.5 0.2 add_convert_fusion
  68.7 8.7 %collective-permute-done.6 = bf16[2,96,512]{2,1,0:T(8,128)(2,1)S(1)} collective-permute-done((bf16[2,96,512]{2,1,0:T(8,128)(2,1)S(1)}, bf16[2,96,512]{2,1,0:T(8,128)(2,1)S(1)}, u32[]{:S(2)}, u32[]{:S(2)}) %collective-permute-start.6) | collective-permute-done | bytes 196640 | tf_op jit(solution)/shard_map/ppermute | solution.py:155
  77.5 0.2 add_convert_fusion.6
  77.7 0.2 add_convert_fusion.2
  78.1 2.0 collective-permute-done.8
  80.0 2.6 collective-permute-start.10
  82.9 0.6 collective-permute-done.9
  83.8 4.0 %collective-permute-done.10 = bf16[2,96,512]{2,1,0:T(8,128)(2,1)S(1)} collective-permute-done((bf16[2,96,512]{2,1,0:T(8,128)(2,1)S(1)}, bf16[2,96,512]{2,1,0:T(8,128)(2,1)S(1)}, u32[]{:S(2)}, u32[]{:S(2)}) %collective-permute-start.10) | collective-permute-done | bytes 196640 | tf_op jit(solution)/shard_map/ppermute | solution.py:155
  88.4 3.7 %collective-permute-start.15 = (bf16[3,96,512]{2,1,0:T(8,128)(2,1)S(1)}, bf16[3,96,512]{2,1,0:T(8,128)(2,1)S(1)}, u32[]{:S(2)}, u32[]{:S(2)}) collective-permute-start(bf16[3,96,512]{2,1,0:T(8,128)(2,1)S(1)} %pad_maximum_fusion.6), channel_id=1, source_target_pairs={{0,6},{1,7},{2,0},{3,1},{4,2},{5,3},{6,4},{7,5},{8,14},{9,15},{10,... | collective-permute-start | bytes 884744 | tf_op jit(solution)/shard_map/ppermute | solution.py:163
  92.2 1.0 collective-permute-start.7
  94.0 5.6 %collective-permute-done.15 = bf16[3,96,512]{2,1,0:T(8,128)(2,1)S(1)} collective-permute-done((bf16[3,96,512]{2,1,0:T(8,128)(2,1)S(1)}, bf16[3,96,512]{2,1,0:T(8,128)(2,1)S(1)}, u32[]{:S(2)}, u32[]{:S(2)}) %collective-permute-start.15) | collective-permute-done | bytes 294944 | tf_op jit(solution)/shard_map/ppermute | solution.py:163
  99.6 16.5 %collective-permute-done.11 = bf16[3,96,512]{2,1,0:T(8,128)(2,1)S(1)} collective-permute-done((bf16[3,96,512]{2,1,0:T(8,128)(2,1)S(1)}, bf16[3,96,512]{2,1,0:T(8,128)(2,1)S(1)}, u32[]{:S(2)}, u32[]{:S(2)}) %collective-permute-start.11) | collective-permute-done | bytes 294944 | tf_op jit(solution)/shard_map/ppermute | solution.py:163
  116.1 1.6 fusion.5
  117.8 1.6 collective-permute-start.16
  119.4 1.5 collective-permute-start.17
  120.9 0.6 collective-permute-start.18
  121.5 1.0 collective-permute-start.19
  122.5 2.9 %collective-permute-start.27 = (bf16[3,96,512]{2,1,0:T(8,128)(2,1)S(1)}, bf16[3,96,512]{2,1,0:T(8,128)(2,1)S(1)}, u32[]{:S(2)}, u32[]{:S(2)}) collective-permute-start(bf16[3,96,512]{2,1,0:T(8,128)(2,1)S(1)} %get-tuple-element.8), channel_id=1, source_target_pairs={{0,6},{1,7},{2,0},{3,1},{4,2},{5,3},{6,4},{7,5},{8,14},{9,15},{10,... | collective-permute-start | bytes 884744 | tf_op jit(solution)/shard_map/ppermute | solution.py:176
  125.4 3.2 %collective-permute-start.23 = (bf16[3,96,512]{2,1,0:T(8,128)(2,1)S(1)}, bf16[3,96,512]{2,1,0:T(8,128)(2,1)S(1)}, u32[]{:S(2)}, u32[]{:S(2)}) collective-permute-start(bf16[3,96,512]{2,1,0:T(8,128)(2,1)S(1)} %get-tuple-element.8), channel_id=1, source_target_pairs={{0,4},{1,5},{2,6},{3,7},{4,0},{5,1},{6,2},{7,3},{8,12},{9,13},{10,... | collective-permute-start | bytes 884744 | tf_op jit(solution)/shard_map/ppermute | solution.py:176
  128.7 4.7 %collective-permute-done.19 = bf16[3,96,512]{2,1,0:T(8,128)(2,1)S(1)} collective-permute-done((bf16[3,96,512]{2,1,0:T(8,128)(2,1)S(1)}, bf16[3,96,512]{2,1,0:T(8,128)(2,1)S(1)}, u32[]{:S(2)}, u32[]{:S(2)}) %collective-permute-start.19) | collective-permute-done | bytes 294944 | tf_op jit(solution)/shard_map/ppermute | solution.py:176
  133.5 1.6 collective-permute-start.20
  135.1 1.5 collective-permute-start.21
  136.6 0.6 collective-permute-start.22
  137.2 11.0 %collective-permute-done.23 = bf16[3,96,512]{2,1,0:T(8,128)(2,1)S(1)} collective-permute-done((bf16[3,96,512]{2,1,0:T(8,128)(2,1)S(1)}, bf16[3,96,512]{2,1,0:T(8,128)(2,1)S(1)}, u32[]{:S(2)}, u32[]{:S(2)}) %collective-permute-start.23) | collective-permute-done | bytes 294944 | tf_op jit(solution)/shard_map/ppermute | solution.py:176
  148.3 1.6 collective-permute-start.24
  149.9 1.6 collective-permute-start.25
  151.6 0.5 collective-permute-start.26
  152.4 1.6 collective-permute-start.28
  154.0 1.8 collective-permute-done.24.refs_9_
  155.7 1.6 collective-permute-start.29
  157.4 2.0 collective-permute-done.25.refs_10_
  159.4 0.7 collective-permute-start.30
  160.1 0.9 collective-permute-done.26.refs_11_
  161.1 3.0 %collective-permute-done.28.refs_13_ = bf16[2,96,512]{2,1,0:T(8,128)(2,1)S(1)} collective-permute-done((bf16[2,96,512]{2,1,0:T(8,128)(2,1)S(1)}, bf16[2,96,512]{2,1,0:T(8,128)(2,1)S(1)}, u32[]{:S(2)}, u32[]{:S(2)}) %collective-permute-start.28) | collective-permute-done | bytes 196640 | tf_op jit(solution)/shard_map/ppermute | solution.py:183
  164.2 4.0 %collective-permute-done.29.refs_14_ = bf16[2,96,512]{2,1,0:T(8,128)(2,1)S(1)} collective-permute-done((bf16[2,96,512]{2,1,0:T(8,128)(2,1)S(1)}, bf16[2,96,512]{2,1,0:T(8,128)(2,1)S(1)}, u32[]{:S(2)}, u32[]{:S(2)}) %collective-permute-start.29) | collective-permute-done | bytes 196640 | tf_op jit(solution)/shard_map/ppermute | solution.py:183
  168.4 0.7 pad_maximum_fusion.19.refs_0_
  169.1 0.7 pad_maximum_fusion.23.refs_4_
  169.8 0.7 pad_maximum_fusion.27.refs_8_
  170.5 0.7 pad_maximum_fusion.31.refs_12_
  171.3 0.7 copy-done.19
  172.2 0.7 copy-done.22
  173.0 97.3 %assemble.1 = bf16[768,2048]{1,0:T(8,128)(2,1)} custom-call(s32[4]{0:T(128)} %copy-done.1, bf16[2,96,512]{2,1,0:T(8,128)(2,1)} %pad_maximum_fusion.19.refs_0_, bf16[2,96,512]{2,1,0:T(8,128)(2,1)} %copy-done.7, bf16[2,96,512]{2,1,0:T(8,128)(2,1)} %copy-done.8, bf16[2,96,512]{2,1,0:T(8,128)(2,1)} %copy-done.9, bf16[2,96,512]{2,1,0:T(8,128)(2,1)} %pad_maximum_fusion.23.refs_4_, ...), custom_call_target="tpu_custom_call" | custom-call | bytes 6291456 | tf_op jit(solution)/shard_map/assemble/pallas_call | solution.py:106
  (150 shorter events, 4.7 us)
Async XLA Ops:
  0.6 10.6 %copy-start = (s32[4,8]{1,0:T(4,128)S(1)}, s32[4,8]{1,0:T(4,128)}, u32[]{:S(2)}) copy-start(s32[4,8]{1,0:T(4,128)} %param.12) | copy-start | bytes 388
  1.4 9.2 %copy-start.1 = (s32[4]{0:T(128)}, s32[4]{0:T(128)S(1)}, u32[]{:S(2)}) copy-start(s32[4]{0:T(128)S(1)} %pad_add_fusion.place) | copy-start | bytes 52
  1.4 2.2 copy-start.2
  3.6 1.4 copy-start.3
  5.0 17.9 %copy-start.23 = (s32[4,8]{1,0:T(4,128)S(1)}, s32[4,8]{1,0:T(4,128)}, u32[]{:S(2)}) copy-start(s32[4,8]{1,0:T(4,128)} %param.11) | copy-start | bytes 388
  10.6 34.3 %collective-permute-start = (bf16[4,4,96,512]{3,2,1,0:T(8,128)(2,1)S(1)}, bf16[4,4,96,512]{3,2,1,0:T(8,128)(2,1)}, u32[]{:S(2)}, u32[]{:S(2)}) collective-permute-start(bf16[4,4,96,512]{3,2,1,0:T(8,128)(2,1)S(1)} %get-tuple-element.7), channel_id=1, source_target_pairs={{0,1},{1,0},{2,3},{3,2},{4,5},{5,4},{6,7},{7,6},{8,9},{9,8},{10,11... | collective-permute-start | bytes 4718600 | tf_op jit(solution)/shard_map/ppermute | solution.py:146
  46.5 8.3 %collective-permute-start.4 = (bf16[2,96,512]{2,1,0:T(8,128)(2,1)S(1)}, bf16[2,96,512]{2,1,0:T(8,128)(2,1)S(1)}, u32[]{:S(2)}, u32[]{:S(2)}) collective-permute-start(bf16[2,96,512]{2,1,0:T(8,128)(2,1)S(1)} %pad_maximum_fusion.10), channel_id=1, source_target_pairs={{0,8},{1,9},{2,10},{3,11},{4,12},{5,13},{6,14},{7,15},{8,0},{9,1},... | collective-permute-start | bytes 589832 | tf_op jit(solution)/shard_map/ppermute | solution.py:155
  49.1 7.8 %collective-permute-start.5 = (bf16[2,96,512]{2,1,0:T(8,128)(2,1)S(1)}, bf16[2,96,512]{2,1,0:T(8,128)(2,1)S(1)}, u32[]{:S(2)}, u32[]{:S(2)}) collective-permute-start(bf16[2,96,512]{2,1,0:T(8,128)(2,1)S(1)} %pad_maximum_fusion.11), channel_id=1, source_target_pairs={{0,16},{1,17},{2,18},{3,19},{4,20},{5,21},{6,22},{7,23},{8,24},{9,... | collective-permute-start | bytes 589832 | tf_op jit(solution)/shard_map/ppermute | solution.py:155
  50.7 8.3 %collective-permute-start.12 = (bf16[2,96,512]{2,1,0:T(8,128)(2,1)S(1)}, bf16[2,96,512]{2,1,0:T(8,128)(2,1)S(1)}, u32[]{:S(2)}, u32[]{:S(2)}) collective-permute-start(bf16[2,96,512]{2,1,0:T(8,128)(2,1)S(1)} %pad_maximum_fusion.16), channel_id=1, source_target_pairs={{0,8},{1,9},{2,10},{3,11},{4,12},{5,13},{6,14},{7,15},{8,0},{9,1},... | collective-permute-start | bytes 589832 | tf_op jit(solution)/shard_map/ppermute | solution.py:155
  51.4 14.0 %collective-permute-start.13 = (bf16[2,96,512]{2,1,0:T(8,128)(2,1)S(1)}, bf16[2,96,512]{2,1,0:T(8,128)(2,1)S(1)}, u32[]{:S(2)}, u32[]{:S(2)}) collective-permute-start(bf16[2,96,512]{2,1,0:T(8,128)(2,1)S(1)} %pad_maximum_fusion.17), channel_id=1, source_target_pairs={{0,16},{1,17},{2,18},{3,19},{4,20},{5,21},{6,22},{7,23},{8,24},{9,... | collective-permute-start | bytes 589832 | tf_op jit(solution)/shard_map/ppermute | solution.py:155
  51.5 15.4 %collective-permute-start.14 = (bf16[2,96,512]{2,1,0:T(8,128)(2,1)S(1)}, bf16[2,96,512]{2,1,0:T(8,128)(2,1)S(1)}, u32[]{:S(2)}, u32[]{:S(2)}) collective-permute-start(bf16[2,96,512]{2,1,0:T(8,128)(2,1)S(1)} %pad_maximum_fusion.18), channel_id=1, source_target_pairs={{0,24},{1,25},{2,26},{3,27},{4,28},{5,29},{6,30},{7,31},{8,16},{9,... | collective-permute-start | bytes 589832 | tf_op jit(solution)/shard_map/ppermute | solution.py:155
  54.9 37.4 %collective-permute-start.1 = (bf16[2,96,512]{2,1,0:T(8,128)(2,1)S(1)}, bf16[2,96,512]{2,1,0:T(8,128)(2,1)S(1)}, u32[]{:S(2)}, u32[]{:S(2)}) collective-permute-start(bf16[2,96,512]{2,1,0:T(8,128)(2,1)S(1)} %pad_maximum_fusion.7), channel_id=1, source_target_pairs={{0,8},{1,9},{2,10},{3,11},{4,12},{5,13},{6,14},{7,15},{8,0},{9,1},... | collective-permute-start | bytes 589832 | tf_op jit(solution)/shard_map/ppermute | solution.py:155
  56.9 36.4 %collective-permute-start.2 = (bf16[2,96,512]{2,1,0:T(8,128)(2,1)S(1)}, bf16[2,96,512]{2,1,0:T(8,128)(2,1)S(1)}, u32[]{:S(2)}, u32[]{:S(2)}) collective-permute-start(bf16[2,96,512]{2,1,0:T(8,128)(2,1)S(1)} %pad_maximum_fusion.8), channel_id=1, source_target_pairs={{0,16},{1,17},{2,18},{3,19},{4,20},{5,21},{6,22},{7,23},{8,24},{9,... | collective-permute-start | bytes 589832 | tf_op jit(solution)/shard_map/ppermute | solution.py:155
  59.1 34.3 %collective-permute-start.3 = (bf16[2,96,512]{2,1,0:T(8,128)(2,1)S(1)}, bf16[2,96,512]{2,1,0:T(8,128)(2,1)S(1)}, u32[]{:S(2)}, u32[]{:S(2)}) collective-permute-start(bf16[2,96,512]{2,1,0:T(8,128)(2,1)S(1)} %pad_maximum_fusion.9), channel_id=1, source_target_pairs={{0,24},{1,25},{2,26},{3,27},{4,28},{5,29},{6,30},{7,31},{8,16},{9,... | collective-permute-start | bytes 589832 | tf_op jit(solution)/shard_map/ppermute | solution.py:155
  65.4 12.1 %collective-permute-start.6 = (bf16[2,96,512]{2,1,0:T(8,128)(2,1)S(1)}, bf16[2,96,512]{2,1,0:T(8,128)(2,1)S(1)}, u32[]{:S(2)}, u32[]{:S(2)}) collective-permute-start(bf16[2,96,512]{2,1,0:T(8,128)(2,1)S(1)} %pad_maximum_fusion.12), channel_id=1, source_target_pairs={{0,24},{1,25},{2,26},{3,27},{4,28},{5,29},{6,30},{7,31},{8,16},{9,... | collective-permute-start | bytes 589832 | tf_op jit(solution)/shard_map/ppermute | solution.py:155
  66.9 13.1 %collective-permute-start.8 = (bf16[2,96,512]{2,1,0:T(8,128)(2,1)S(1)}, bf16[2,96,512]{2,1,0:T(8,128)(2,1)S(1)}, u32[]{:S(2)}, u32[]{:S(2)}) collective-permute-start(bf16[2,96,512]{2,1,0:T(8,128)(2,1)S(1)} %pad_maximum_fusion.13), channel_id=1, source_target_pairs={{0,8},{1,9},{2,10},{3,11},{4,12},{5,13},{6,14},{7,15},{8,0},{9,1},... | collective-permute-start | bytes 589832 | tf_op jit(solution)/shard_map/ppermute | solution.py:155
  77.4 6.1 %collective-permute-start.9 = (bf16[2,96,512]{2,1,0:T(8,128)(2,1)S(1)}, bf16[2,96,512]{2,1,0:T(8,128)(2,1)S(1)}, u32[]{:S(2)}, u32[]{:S(2)}) collective-permute-start(bf16[2,96,512]{2,1,0:T(8,128)(2,1)S(1)} %pad_maximum_fusion.14), channel_id=1, source_target_pairs={{0,16},{1,17},{2,18},{3,19},{4,20},{5,21},{6,22},{7,23},{8,24},{9,... | collective-permute-start | bytes 589832 | tf_op jit(solution)/shard_map/ppermute | solution.py:155
  80.0 7.7 %collective-permute-start.10 = (bf16[2,96,512]{2,1,0:T(8,128)(2,1)S(1)}, bf16[2,96,512]{2,1,0:T(8,128)(2,1)S(1)}, u32[]{:S(2)}, u32[]{:S(2)}) collective-permute-start(bf16[2,96,512]{2,1,0:T(8,128)(2,1)S(1)} %pad_maximum_fusion.15), channel_id=1, source_target_pairs={{0,24},{1,25},{2,26},{3,27},{4,28},{5,29},{6,30},{7,31},{8,16},{9,... | collective-permute-start | bytes 589832 | tf_op jit(solution)/shard_map/ppermute | solution.py:155
  88.4 11.2 %collective-permute-start.15 = (bf16[3,96,512]{2,1,0:T(8,128)(2,1)S(1)}, bf16[3,96,512]{2,1,0:T(8,128)(2,1)S(1)}, u32[]{:S(2)}, u32[]{:S(2)}) collective-permute-start(bf16[3,96,512]{2,1,0:T(8,128)(2,1)S(1)} %pad_maximum_fusion.6), channel_id=1, source_target_pairs={{0,6},{1,7},{2,0},{3,1},{4,2},{5,3},{6,4},{7,5},{8,14},{9,15},{10,... | collective-permute-start | bytes 884744 | tf_op jit(solution)/shard_map/ppermute | solution.py:163
  92.1 24.0 %collective-permute-start.11 = (bf16[3,96,512]{2,1,0:T(8,128)(2,1)S(1)}, bf16[3,96,512]{2,1,0:T(8,128)(2,1)S(1)}, u32[]{:S(2)}, u32[]{:S(2)}) collective-permute-start(bf16[3,96,512]{2,1,0:T(8,128)(2,1)S(1)} %pad_maximum_fusion.5), channel_id=1, source_target_pairs={{0,4},{1,5},{2,6},{3,7},{4,0},{5,1},{6,2},{7,3},{8,12},{9,13},{10,... | collective-permute-start | bytes 884744 | tf_op jit(solution)/shard_map/ppermute | solution.py:163
  92.2 23.9 %collective-permute-start.7 = (bf16[3,96,512]{2,1,0:T(8,128)(2,1)S(1)}, bf16[3,96,512]{2,1,0:T(8,128)(2,1)S(1)}, u32[]{:S(2)}, u32[]{:S(2)}) collective-permute-start(bf16[3,96,512]{2,1,0:T(8,128)(2,1)S(1)} %pad_maximum_fusion.4), channel_id=1, source_target_pairs={{0,2},{1,3},{2,4},{3,5},{4,6},{5,7},{6,0},{7,1},{8,10},{9,11},{10,... | collective-permute-start | bytes 884744 | tf_op jit(solution)/shard_map/ppermute | solution.py:163
  93.6 22.5 %copy-start.4 = (f32[3,96,512]{2,1,0:T(8,128)S(1)}, f32[3,96,512]{2,1,0:T(8,128)}, u32[]{:S(2)}) copy-start(f32[3,96,512]{2,1,0:T(8,128)} %param.13) | copy-start | bytes 1769476
  93.6 22.5 %copy-start.5 = (f32[3,96,512]{2,1,0:T(8,128)S(1)}, f32[3,96,512]{2,1,0:T(8,128)}, u32[]{:S(2)}) copy-start(f32[3,96,512]{2,1,0:T(8,128)} %param.14) | copy-start | bytes 1769476
  93.6 22.5 %copy-start.6 = (f32[3,96,512]{2,1,0:T(8,128)S(1)}, f32[3,96,512]{2,1,0:T(8,128)}, u32[]{:S(2)}) copy-start(f32[3,96,512]{2,1,0:T(8,128)} %param.15) | copy-start | bytes 1769476
  117.8 7.6 %collective-permute-start.16 = (bf16[2,96,512]{2,1,0:T(8,128)(2,1)S(1)}, bf16[2,96,512]{2,1,0:T(8,128)(2,1)S(1)}, u32[]{:S(2)}, u32[]{:S(2)}) collective-permute-start(bf16[2,96,512]{2,1,0:T(8,128)(2,1)S(1)} %pad_maximum_fusion.20), channel_id=1, source_target_pairs={{0,8},{1,9},{2,10},{3,11},{4,12},{5,13},{6,14},{7,15},{8,0},{9,1},... | collective-permute-start | bytes 589832 | tf_op jit(solution)/shard_map/ppermute | solution.py:183
  119.4 9.2 %collective-permute-start.17 = (bf16[2,96,512]{2,1,0:T(8,128)(2,1)S(1)}, bf16[2,96,512]{2,1,0:T(8,128)(2,1)S(1)}, u32[]{:S(2)}, u32[]{:S(2)}) collective-permute-start(bf16[2,96,512]{2,1,0:T(8,128)(2,1)S(1)} %pad_maximum_fusion.21), channel_id=1, source_target_pairs={{0,16},{1,17},{2,18},{3,19},{4,20},{5,21},{6,22},{7,23},{8,24},{9,... | collective-permute-start | bytes 589832 | tf_op jit(solution)/shard_map/ppermute | solution.py:183
  120.9 7.7 %collective-permute-start.18 = (bf16[2,96,512]{2,1,0:T(8,128)(2,1)S(1)}, bf16[2,96,512]{2,1,0:T(8,128)(2,1)S(1)}, u32[]{:S(2)}, u32[]{:S(2)}) collective-permute-start(bf16[2,96,512]{2,1,0:T(8,128)(2,1)S(1)} %pad_maximum_fusion.22), channel_id=1, source_target_pairs={{0,24},{1,25},{2,26},{3,27},{4,28},{5,29},{6,30},{7,31},{8,16},{9,... | collective-permute-start | bytes 589832 | tf_op jit(solution)/shard_map/ppermute | solution.py:183
  121.5 11.8 %collective-permute-start.19 = (bf16[3,96,512]{2,1,0:T(8,128)(2,1)S(1)}, bf16[3,96,512]{2,1,0:T(8,128)(2,1)S(1)}, u32[]{:S(2)}, u32[]{:S(2)}) collective-permute-start(bf16[3,96,512]{2,1,0:T(8,128)(2,1)S(1)} %get-tuple-element.8), channel_id=1, source_target_pairs={{0,2},{1,3},{2,4},{3,5},{4,6},{5,7},{6,0},{7,1},{8,10},{9,11},{10,... | collective-permute-start | bytes 884744 | tf_op jit(solution)/shard_map/ppermute | solution.py:176
  122.5 27.4 %collective-permute-start.27 = (bf16[3,96,512]{2,1,0:T(8,128)(2,1)S(1)}, bf16[3,96,512]{2,1,0:T(8,128)(2,1)S(1)}, u32[]{:S(2)}, u32[]{:S(2)}) collective-permute-start(bf16[3,96,512]{2,1,0:T(8,128)(2,1)S(1)} %get-tuple-element.8), channel_id=1, source_target_pairs={{0,6},{1,7},{2,0},{3,1},{4,2},{5,3},{6,4},{7,5},{8,14},{9,15},{10,... | collective-permute-start | bytes 884744 | tf_op jit(solution)/shard_map/ppermute | solution.py:176
  125.4 8.1 %copy-start.7 = (bf16[2,96,512]{2,1,0:T(8,128)(2,1)}, bf16[2,96,512]{2,1,0:T(8,128)(2,1)S(1)}, u32[]{:S(2)}) copy-start(bf16[2,96,512]{2,1,0:T(8,128)(2,1)S(1)} %collective-permute-done.16.refs_1_) | copy-start | bytes 589828
  125.4 22.8 %collective-permute-start.23 = (bf16[3,96,512]{2,1,0:T(8,128)(2,1)S(1)}, bf16[3,96,512]{2,1,0:T(8,128)(2,1)S(1)}, u32[]{:S(2)}, u32[]{:S(2)}) collective-permute-start(bf16[3,96,512]{2,1,0:T(8,128)(2,1)S(1)} %get-tuple-element.8), channel_id=1, source_target_pairs={{0,4},{1,5},{2,6},{3,7},{4,0},{5,1},{6,2},{7,3},{8,12},{9,13},{10,... | collective-permute-start | bytes 884744 | tf_op jit(solution)/shard_map/ppermute | solution.py:176
  128.6 4.9 %copy-start.8 = (bf16[2,96,512]{2,1,0:T(8,128)(2,1)}, bf16[2,96,512]{2,1,0:T(8,128)(2,1)S(1)}, u32[]{:S(2)}) copy-start(bf16[2,96,512]{2,1,0:T(8,128)(2,1)S(1)} %collective-permute-done.17.refs_2_) | copy-start | bytes 589828
  128.6 6.5 %copy-start.9 = (bf16[2,96,512]{2,1,0:T(8,128)(2,1)}, bf16[2,96,512]{2,1,0:T(8,128)(2,1)S(1)}, u32[]{:S(2)}) copy-start(bf16[2,96,512]{2,1,0:T(8,128)(2,1)S(1)} %collective-permute-done.18.refs_3_) | copy-start | bytes 589828
  133.5 18.1 %collective-permute-start.20 = (bf16[2,96,512]{2,1,0:T(8,128)(2,1)S(1)}, bf16[2,96,512]{2,1,0:T(8,128)(2,1)S(1)}, u32[]{:S(2)}, u32[]{:S(2)}) collective-permute-start(bf16[2,96,512]{2,1,0:T(8,128)(2,1)S(1)} %pad_maximum_fusion.24), channel_id=1, source_target_pairs={{0,8},{1,9},{2,10},{3,11},{4,12},{5,13},{6,14},{7,15},{8,0},{9,1},... | collective-permute-start | bytes 589832 | tf_op jit(solution)/shard_map/ppermute | solution.py:183
  135.1 17.2 %collective-permute-start.21 = (bf16[2,96,512]{2,1,0:T(8,128)(2,1)S(1)}, bf16[2,96,512]{2,1,0:T(8,128)(2,1)S(1)}, u32[]{:S(2)}, u32[]{:S(2)}) collective-permute-start(bf16[2,96,512]{2,1,0:T(8,128)(2,1)S(1)} %pad_maximum_fusion.25), channel_id=1, source_target_pairs={{0,16},{1,17},{2,18},{3,19},{4,20},{5,21},{6,22},{7,23},{8,24},{9,... | collective-permute-start | bytes 589832 | tf_op jit(solution)/shard_map/ppermute | solution.py:183
  136.6 15.7 %collective-permute-start.22 = (bf16[2,96,512]{2,1,0:T(8,128)(2,1)S(1)}, bf16[2,96,512]{2,1,0:T(8,128)(2,1)S(1)}, u32[]{:S(2)}, u32[]{:S(2)}) collective-permute-start(bf16[2,96,512]{2,1,0:T(8,128)(2,1)S(1)} %pad_maximum_fusion.26), channel_id=1, source_target_pairs={{0,24},{1,25},{2,26},{3,27},{4,28},{5,29},{6,30},{7,31},{8,16},{9,... | collective-permute-start | bytes 589832 | tf_op jit(solution)/shard_map/ppermute | solution.py:183
  148.3 7.4 %collective-permute-start.24 = (bf16[2,96,512]{2,1,0:T(8,128)(2,1)S(1)}, bf16[2,96,512]{2,1,0:T(8,128)(2,1)S(1)}, u32[]{:S(2)}, u32[]{:S(2)}) collective-permute-start(bf16[2,96,512]{2,1,0:T(8,128)(2,1)S(1)} %pad_maximum_fusion.28), channel_id=1, source_target_pairs={{0,8},{1,9},{2,10},{3,11},{4,12},{5,13},{6,14},{7,15},{8,0},{9,1},... | collective-permute-start | bytes 589832 | tf_op jit(solution)/shard_map/ppermute | solution.py:183
  149.9 9.4 %collective-permute-start.25 = (bf16[2,96,512]{2,1,0:T(8,128)(2,1)S(1)}, bf16[2,96,512]{2,1,0:T(8,128)(2,1)S(1)}, u32[]{:S(2)}, u32[]{:S(2)}) collective-permute-start(bf16[2,96,512]{2,1,0:T(8,128)(2,1)S(1)} %pad_maximum_fusion.29), channel_id=1, source_target_pairs={{0,16},{1,17},{2,18},{3,19},{4,20},{5,21},{6,22},{7,23},{8,24},{9,... | collective-permute-start | bytes 589832 | tf_op jit(solution)/shard_map/ppermute | solution.py:183
  151.6 9.5 %copy-start.10 = (bf16[2,96,512]{2,1,0:T(8,128)(2,1)}, bf16[2,96,512]{2,1,0:T(8,128)(2,1)S(1)}, u32[]{:S(2)}) copy-start(bf16[2,96,512]{2,1,0:T(8,128)(2,1)S(1)} %collective-permute-done.20.refs_5_) | copy-start | bytes 589828
  151.6 9.4 %collective-permute-start.26 = (bf16[2,96,512]{2,1,0:T(8,128)(2,1)S(1)}, bf16[2,96,512]{2,1,0:T(8,128)(2,1)S(1)}, u32[]{:S(2)}, u32[]{:S(2)}) collective-permute-start(bf16[2,96,512]{2,1,0:T(8,128)(2,1)S(1)} %pad_maximum_fusion.30), channel_id=1, source_target_pairs={{0,24},{1,25},{2,26},{3,27},{4,28},{5,29},{6,30},{7,31},{8,16},{9,... | collective-permute-start | bytes 589832 | tf_op jit(solution)/shard_map/ppermute | solution.py:183
  152.2 16.0 %copy-start.11 = (bf16[2,96,512]{2,1,0:T(8,128)(2,1)}, bf16[2,96,512]{2,1,0:T(8,128)(2,1)S(1)}, u32[]{:S(2)}) copy-start(bf16[2,96,512]{2,1,0:T(8,128)(2,1)S(1)} %collective-permute-done.21.refs_6_) | copy-start | bytes 589828
  152.2 18.9 %collective-permute-start.31 = (bf16[4,96,512]{2,1,0:T(8,128)(2,1)S(1)}, bf16[4,96,512]{2,1,0:T(8,128)(2,1)S(1)}, u32[]{:S(2)}, u32[]{:S(2)}) collective-permute-start(bf16[4,96,512]{2,1,0:T(8,128)(2,1)S(1)} %pad_maximum_fusion), channel_id=1, source_target_pairs={{0,1},{1,0},{2,3},{3,2},{4,5},{5,4},{6,7},{7,6},{8,9},{9,8},{10,11... | collective-permute-start | bytes 1179656 | tf_op jit(solution)/shard_map/ppermute | solution.py:186
  152.3 15.9 %copy-start.12 = (bf16[2,96,512]{2,1,0:T(8,128)(2,1)}, bf16[2,96,512]{2,1,0:T(8,128)(2,1)S(1)}, u32[]{:S(2)}) copy-start(bf16[2,96,512]{2,1,0:T(8,128)(2,1)S(1)} %collective-permute-done.22.refs_7_) | copy-start | bytes 589828
  152.4 11.8 %collective-permute-start.28 = (bf16[2,96,512]{2,1,0:T(8,128)(2,1)S(1)}, bf16[2,96,512]{2,1,0:T(8,128)(2,1)S(1)}, u32[]{:S(2)}, u32[]{:S(2)}) collective-permute-start(bf16[2,96,512]{2,1,0:T(8,128)(2,1)S(1)} %pad_maximum_fusion.32), channel_id=1, source_target_pairs={{0,8},{1,9},{2,10},{3,11},{4,12},{5,13},{6,14},{7,15},{8,0},{9,1},... | collective-permute-start | bytes 589832 | tf_op jit(solution)/shard_map/ppermute | solution.py:183
  155.7 12.6 %copy-start.13 = (bf16[2,96,512]{2,1,0:T(8,128)(2,1)}, bf16[2,96,512]{2,1,0:T(8,128)(2,1)S(1)}, u32[]{:S(2)}) copy-start(bf16[2,96,512]{2,1,0:T(8,128)(2,1)S(1)} %collective-permute-done.24.refs_9_) | copy-start | bytes 589828
  155.7 12.5 %collective-permute-start.29 = (bf16[2,96,512]{2,1,0:T(8,128)(2,1)S(1)}, bf16[2,96,512]{2,1,0:T(8,128)(2,1)S(1)}, u32[]{:S(2)}, u32[]{:S(2)}) collective-permute-start(bf16[2,96,512]{2,1,0:T(8,128)(2,1)S(1)} %pad_maximum_fusion.33), channel_id=1, source_target_pairs={{0,16},{1,17},{2,18},{3,19},{4,20},{5,21},{6,22},{7,23},{8,24},{9,... | collective-permute-start | bytes 589832 | tf_op jit(solution)/shard_map/ppermute | solution.py:183
  159.4 8.9 %copy-start.14 = (bf16[2,96,512]{2,1,0:T(8,128)(2,1)}, bf16[2,96,512]{2,1,0:T(8,128)(2,1)S(1)}, u32[]{:S(2)}) copy-start(bf16[2,96,512]{2,1,0:T(8,128)(2,1)S(1)} %collective-permute-done.25.refs_10_) | copy-start | bytes 589828
  159.4 8.8 %collective-permute-start.30 = (bf16[2,96,512]{2,1,0:T(8,128)(2,1)S(1)}, bf16[2,96,512]{2,1,0:T(8,128)(2,1)S(1)}, u32[]{:S(2)}, u32[]{:S(2)}) collective-permute-start(bf16[2,96,512]{2,1,0:T(8,128)(2,1)S(1)} %pad_maximum_fusion.34), channel_id=1, source_target_pairs={{0,24},{1,25},{2,26},{3,27},{4,28},{5,29},{6,30},{7,31},{8,16},{9,... | collective-permute-start | bytes 589832 | tf_op jit(solution)/shard_map/ppermute | solution.py:183
  161.0 8.8 %copy-start.15 = (bf16[2,96,512]{2,1,0:T(8,128)(2,1)}, bf16[2,96,512]{2,1,0:T(8,128)(2,1)S(1)}, u32[]{:S(2)}) copy-start(bf16[2,96,512]{2,1,0:T(8,128)(2,1)S(1)} %collective-permute-done.26.refs_11_) | copy-start | bytes 589828
  161.0 10.2 %collective-permute-start.32 = (bf16[4,96,512]{2,1,0:T(8,128)(2,1)S(1)}, bf16[4,96,512]{2,1,0:T(8,128)(2,1)S(1)}, u32[]{:S(2)}, u32[]{:S(2)}) collective-permute-start(bf16[4,96,512]{2,1,0:T(8,128)(2,1)S(1)} %pad_maximum_fusion.1), channel_id=1, source_target_pairs={{0,1},{1,0},{2,3},{3,2},{4,5},{5,4},{6,7},{7,6},{8,9},{9,8},{10,11... | collective-permute-start | bytes 1179656 | tf_op jit(solution)/shard_map/ppermute | solution.py:186
  164.1 7.1 %copy-start.16 = (bf16[2,96,512]{2,1,0:T(8,128)(2,1)}, bf16[2,96,512]{2,1,0:T(8,128)(2,1)S(1)}, u32[]{:S(2)}) copy-start(bf16[2,96,512]{2,1,0:T(8,128)(2,1)S(1)} %collective-permute-done.28.refs_13_) | copy-start | bytes 589828
  164.1 7.1 %collective-permute-start.33 = (bf16[4,96,512]{2,1,0:T(8,128)(2,1)S(1)}, bf16[4,96,512]{2,1,0:T(8,128)(2,1)S(1)}, u32[]{:S(2)}, u32[]{:S(2)}) collective-permute-start(bf16[4,96,512]{2,1,0:T(8,128)(2,1)S(1)} %pad_maximum_fusion.2), channel_id=1, source_target_pairs={{0,1},{1,0},{2,3},{3,2},{4,5},{5,4},{6,7},{7,6},{8,9},{9,8},{10,11... | collective-permute-start | bytes 1179656 | tf_op jit(solution)/shard_map/ppermute | solution.py:186
  168.2 3.1 %copy-start.17 = (bf16[2,96,512]{2,1,0:T(8,128)(2,1)}, bf16[2,96,512]{2,1,0:T(8,128)(2,1)S(1)}, u32[]{:S(2)}) copy-start(bf16[2,96,512]{2,1,0:T(8,128)(2,1)S(1)} %collective-permute-done.29.refs_14_) | copy-start | bytes 589828
  168.2 3.1 %copy-start.18 = (bf16[2,96,512]{2,1,0:T(8,128)(2,1)}, bf16[2,96,512]{2,1,0:T(8,128)(2,1)S(1)}, u32[]{:S(2)}) copy-start(bf16[2,96,512]{2,1,0:T(8,128)(2,1)S(1)} %collective-permute-done.30.refs_15_) | copy-start | bytes 589828
  168.3 2.9 %collective-permute-start.34 = (bf16[4,96,512]{2,1,0:T(8,128)(2,1)S(1)}, bf16[4,96,512]{2,1,0:T(8,128)(2,1)S(1)}, u32[]{:S(2)}, u32[]{:S(2)}) collective-permute-start(bf16[4,96,512]{2,1,0:T(8,128)(2,1)S(1)} %pad_maximum_fusion.3), channel_id=1, source_target_pairs={{0,1},{1,0},{2,3},{3,2},{4,5},{5,4},{6,7},{7,6},{8,9},{9,8},{10,11... | collective-permute-start | bytes 1179656 | tf_op jit(solution)/shard_map/ppermute | solution.py:186
  171.2 0.8 copy-start.19
  171.2 0.9 copy-start.20
  171.2 1.0 copy-start.21
  172.2 0.7 copy-start.22

commit v2 on v1

--- a/solution.py
+++ b/solution.py
@@ -1,5 +1,3 @@
-import functools
-
 import jax
 import jax.numpy as jnp
 from jax import lax
@@ -26,14 +24,21 @@
     return master_new, moment_one_new, moment_two_new
 
 
-def matmul_kernel(place, hidden_ref, upstream_ref, keep_ref, send_ref, turned):
+def matmul_kernel(place, now_ref, next_ref, hidden_ref, upstream_ref, keep_ref, send_ref, chosen_ref, turned):
     planes, unused, rows, unused = keep_ref.shape
+    experts = chosen_ref.shape[2]
 
     @pl.when(pl.program_id(0) == 0)
     def turn():
         hidden = hidden_ref[...]
         live = lax.broadcasted_iota(jnp.int32, hidden.shape, 0) < place[3]
         turned[...] = jnp.where(live, hidden, jnp.zeros_like(hidden)).T
+        shape = chosen_ref.shape[2:]
+        names = lax.broadcasted_iota(jnp.int32, shape, 0)
+        for n, plan_ref in enumerate((now_ref, next_ref)):
+            for near in range(chosen_ref.shape[1]):
+                named = plan_ref[place[0] ^ (near // 2), 2 * place[1] + (place[2] ^ (near % 2))]
+                chosen_ref[n, near] = jnp.where(names == named, 1.0, 0.0)
 
     product = jnp.dot(turned[...], upstream_ref[...], preferred_element_type=jnp.float32)
     product = product.astype(jnp.bfloat16)
@@ -46,75 +51,46 @@
         send_ref[ahead, 0] = jnp.where(even_core, odd, even)
 
 
-def partial_blocks(place, hidden, upstream, groups, planes):
+def partial_blocks(place, plan_now, plan_next, hidden, upstream, experts):
+    groups, owners = plan_now.shape
+    planes = owners // 2
     tokens, inner = hidden.shape
     width = upstream.shape[1]
     cols = width // groups
-    rows = inner // (2 * planes)
+    rows = inner // owners
     out = jax.ShapeDtypeStruct((planes, groups, rows, cols), jnp.bfloat16)
+    chosen = jax.ShapeDtypeStruct((2, 2 * groups, experts, cols), jnp.float32)
     out_spec = pl.BlockSpec((planes, 1, rows, cols), lambda j, place: (0, j, 0, 0))
+    smem = pl.BlockSpec(memory_space=pltpu.SMEM)
     return pl.pallas_call(
         matmul_kernel,
         grid_spec=pltpu.PrefetchScalarGridSpec(
             num_scalar_prefetch=1,
             grid=(groups,),
             in_specs=[
+                smem,
+                smem,
                 pl.BlockSpec((tokens, inner), lambda j, place: (0, 0)),
                 pl.BlockSpec((tokens, cols), lambda j, place: (0, place[0] ^ j)),
             ],
-            out_specs=[out_spec, out_spec],
+            out_specs=[out_spec, out_spec, pl.BlockSpec(chosen.shape, lambda j, place: (0, 0, 0, 0))],
             scratch_shapes=[pltpu.VMEM((inner, tokens), jnp.bfloat16)],
         ),
-        out_shape=[out, out],
-        compiler_params=pltpu.CompilerParams(vmem_limit_bytes=40 * 2**20),
+        out_shape=[out, out, chosen],
+        compiler_params=pltpu.CompilerParams(vmem_limit_bytes=60 * 2**20),
         cost_estimate=pl.CostEstimate(
             flops=2 * tokens * inner * width,
             bytes_accessed=2 * (tokens * inner + tokens * width + inner * width),
             transcendentals=0,
         ),
         name="partial_blocks",
-    )(place, hidden, upstream)
-
-
-def assemble_kernel(groups, planes, place, *refs):
-    mine = refs[: planes * groups]
-    other = refs[planes * groups : planes * groups + planes]
-    out_ref = refs[-2]
-    sems = refs[-1]
-    rows, cols = mine[0].shape[1:]
-    copies = []
-    for s in range(planes):
-        plane = lax.rem(place[1] - s + planes, planes)
-        for i in range(2):
-            row = pl.multiple_of((2 * plane + (place[2] ^ i)) * rows, rows)
-            for j in range(groups):
-                col = pl.multiple_of((place[0] ^ j) * cols, cols)
-                src = mine[s * groups + j].at[0] if i == 0 else other[s].at[j]
-                copies.append(
-                    pltpu.make_async_copy(
-                        src, out_ref.at[pl.ds(row, rows), pl.ds(col, cols)], sems.at[len(copies)]
-                    )
-                )
-    for copy in copies:
-        copy.start()
-    for copy in copies:
-        copy.wait()
-
-
-def assemble(place, mine, other, groups, planes):
-    rows, cols = mine[0].shape[1:]
-    return pl.pallas_call(
-        functools.partial(assemble_kernel, groups, planes),
-        in_specs=[pl.BlockSpec(memory_space=pltpu.SMEM)]
-        + [pl.BlockSpec(memory_space=pl.ANY)] * (len(mine) + len(other)),
-        out_specs=pl.BlockSpec(memory_space=pl.ANY),
-        scratch_shapes=[pltpu.SemaphoreType.DMA((2 * planes * groups,))],
-        out_shape=jax.ShapeDtypeStruct((2 * planes * rows, groups * cols), jnp.bfloat16),
-        cost_estimate=pl.CostEstimate(
-            flops=0, bytes_accessed=8 * planes * rows * groups * cols, transcendentals=0
-        ),
-        name="assemble",
-    )(place, *mine, *other)
+    )(place, plan_now, plan_next, hidden, upstream)
+
+
+def after(values, token):
+    if token is None:
+        return values
+    return list(lax.optimization_barrier((*values, token))[:-1])
 
 
 def per_device_planes(
@@ -126,7 +102,7 @@
     group = lax.axis_index("dp")
     owner = lax.axis_index("expert")
     plane, core = owner // 2, owner % 2
-    experts = master.shape[0]
+    experts, rows, cols = master.shape
     place = jnp.stack([group, plane, core, row_counts[0, 0]]).astype(jnp.int32)
 
     everyone = range(groups * owners)
@@ -137,60 +113,53 @@
     ]
     order = sorted(range(planes), key=lambda s: -min(s, planes - s))
 
-    near_groups = jnp.stack([group ^ j for j in range(groups)])
-    near_owners = jnp.stack([owner, owner ^ 1])
-    now = plan_now[near_groups][:, near_owners]
-    later = plan_next[near_groups][:, near_owners]
-
-    keep, send = partial_blocks(place, hidden_acts[0, 0], out_grads[0, 0], groups, planes)
+    keep, send, chosen = partial_blocks(
+        place, plan_now, plan_next, hidden_acts[0, 0], out_grads[0, 0], experts
+    )
+    now, later = chosen[0], chosen[1]
     held = lax.ppermute(send, AXES, to_core)
 
-    arrived = {}
-    own_sum = None
-    for s in order:
-        sums = [jnp.float32(0.0)] * experts
+    sums = []
+    arrived = []
+    for n, s in enumerate(order):
+        messages = [jnp.stack([keep[s, j], held[s, j]]) for j in range(groups)]
+        messages = after(messages, sums[n - 2] if n >= 2 else None)
+        total = jnp.zeros((experts, rows, cols), jnp.float32)
         for j in range(groups):
-            block = jnp.stack([keep[s, j], held[s, j]])
-            if j:
-                block = lax.ppermute(block, AXES, to_group[j])
-            block = block.astype(jnp.float32)
+            block = lax.ppermute(messages[j], AXES, to_group[j]) if j else messages[j]
             for i in range(2):
-                sums = [
-                    sums[e] + jnp.where(now[j, i] == e, block[i], jnp.float32(0.0)) for e in range(experts)
-                ]
-        total = jnp.stack(sums)
+                total = total + now[2 * j + i][:, None] * block[i].astype(jnp.float32)
         if s:
-            arrived[s] = lax.ppermute(total.astype(jnp.bfloat16), AXES, to_plane[s])
-        else:
-            own_sum = total
-    grad_sum = own_sum
-    for s in range(1, planes):
-        grad_sum = grad_sum + arrived[s].astype(jnp.float32)
+            sums.append(total.astype(jnp.bfloat16))
+            arrived.append(lax.ppermute(sums[-1], AXES, to_plane[s]))
+    grad_sum = total
+    for shard in arrived:
+        grad_sum = grad_sum + shard.astype(jnp.float32)
 
     master_new, moment_one_new, moment_two_new = adam(grad_sum, master, moment_one, moment_two)
     rounded = master_new.astype(jnp.bfloat16)
 
-    mine = {}
-    other = {}
+    def in_order(blocks):
+        for bit in range(groups.bit_length() - 1):
+            swap = (group >> bit) % 2 == 1
+            blocks = [jnp.where(swap, blocks[m ^ (1 << bit)], blocks[m]) for m in range(groups)]
+        return jnp.concatenate(blocks, axis=-1)
+
+    replica = jnp.zeros((planes, 2, rows, groups * cols), jnp.bfloat16)
     for s in order[::-1]:
-        shard = lax.ppermute(rounded, AXES, to_plane[s]) if s else rounded
-        passed_on = []
+        shard = (lax.ppermute(rounded, AXES, to_plane[s]) if s else rounded).astype(jnp.float32)
+        blocks = []
         for j in range(groups):
             block = jnp.stack(
-                [lax.dynamic_index_in_dim(shard, later[j, i], 0, keepdims=False) for i in range(2)]
+                [jnp.sum(later[2 * j + i][:, None] * shard, axis=0).astype(jnp.bfloat16) for i in range(2)]
             )
-            if j:
-                block = lax.ppermute(block, AXES, to_group[j])
-            mine[s, j] = block
-            passed_on.append(block[1])
-        other[s] = lax.ppermute(jnp.stack(passed_on), AXES, to_core)
-    replica = assemble(
-        place,
-        [mine[s, j] for s in range(planes) for j in range(groups)],
-        [other[s] for s in range(planes)],
-        groups,
-        planes,
-    )
+            blocks.append(lax.ppermute(block, AXES, to_group[j]) if j else block)
+        mine = in_order([block[0] for block in blocks])
+        other = lax.ppermute(jnp.stack([block[1] for block in blocks]), AXES, to_core)
+        other = in_order([other[j] for j in range(groups)])
+        both = jnp.stack([jnp.where(core == 0, mine, other), jnp.where(core == 0, other, mine)])
+        replica = lax.dynamic_update_index_in_dim(replica, both, (plane - s) % planes, 0)
+    replica = replica.reshape(2 * planes * rows, groups * cols)
     return (master_new, moment_one_new, moment_two_new, replica[None, None])
 
 

time: 272 us -> 130 us (0.48)
  Pallas kernels: 103 us -> 8.49 us
  between operations: 31.9 us -> 1.93 us
  waiting for transfers between devices: 68.9 us -> 57.7 us
  local copies, waits for them, and re-layouts: 11.2 us -> 2.94 us
    pallas_call x1 -> x0, Pallas kernels: 97.3 us -> none  [assemble(): pl.pallas_call(functools.partial(assemble_kernel, groups, planes), in_spe...]
    ppermute x34, waiting for transfers between devices: 68.9 us -> 57 us  [the longest x12 27.2 us: per_device_planes(): block = lax.ppermute(messages[j], AXES, to_group[j]) if j else messages[j]]
    unnamed x48 -> x8, local copies, waits for them, and re-layouts: 5.41 us -> 1.68 us
    pallas_call x1, Pallas kernels: 5.62 us -> 8.49 us  [partial_blocks(): pl.pallas_call(matmul_kernel, grid_spec=pltpu.PrefetchScalarGridSpec(num_...]
  transfers between devices with their start and end apart: 35 -> 35, of which waited for: 17 -> 21; matrix products, arithmetic and copies ran while one was open for 4% -> 5% of each run, Pallas kernels for 0% -> 0%
where the time goes in v2:
time: 130 us; the launch traced here: 129 us
  waiting for transfers between devices  57.7 us (44%)
  starting transfers between devices  48.9 us (38%)
  other arithmetic  9.28 us (7%)
  Pallas kernels  8.49 us (7%)
  local copies, waits for them, and re-layouts  2.94 us (2%)
  between operations  1.93 us (1%)
    ppermute x12, waiting for transfers between devices, per_device_planes(): block = lax.ppermute(messages[j], AXES, to_group[j]) if j else messages[j]  27.2 us
    ppermute x12, starting transfers between devices, per_device_planes(): block = lax.ppermute(messages[j], AXES, to_group[j]) if j else messages[j]  19.8 us
    ppermute x3, waiting for transfers between devices, per_device_planes(): lax.ppermute(rounded, AXES, to_plane[s])  14.2 us
    ppermute x12, starting transfers between devices, per_device_planes(): blocks.append(lax.ppermute(block, AXES, to_group[j]) if j else block)  13.5 us
    ppermute x12, waiting for transfers between devices, per_device_planes(): blocks.append(lax.ppermute(block, AXES, to_group[j]) if j else block)  10.2 us
    ppermute x3, starting transfers between devices, per_device_planes(): lax.ppermute(rounded, AXES, to_plane[s])  10.1 us
    pallas_call x1, Pallas kernels, partial_blocks(): pl.pallas_call(matmul_kernel, grid_spec=pltpu.PrefetchScalarGridSpec(num_...  8.49 us
    ppermute x3, waiting for transfers between devices, per_device_planes(): arrived.append(lax.ppermute(sums[-1], AXES, to_plane[s]))  4.37 us
  transfers between devices with their start and end apart: 35, of which 21 were waited for; matrix products, arithmetic and copies ran while one was open for 5% of the time, Pallas kernels for 0%

profile of v2, /device:TPU:0, one launch (start us, length us, event | category | flops | bytes accessed | tf_op | source)
XLA Modules:
  0.0 129.3 jit_solution(3345511574627448785)
XLA Ops:
  1.3 0.6 pad_add_fusion.place
  1.9 8.5 %partial_blocks.1 = (bf16[4,4,96,512]{3,2,1,0:T(8,128)(2,1)}, bf16[4,4,96,512]{3,2,1,0:T(8,128)(2,1)}, f32[2,8,3,512]{3,2,1,0:T(4,128)}) custom-call(s32[4]{0:T(128)} %pad_add_fusion.place, s32[4,8]{1,0:T(4,128)} %now_ref.1, s32[4,8]{1,0:T(4,128)} %next_ref.1, bf16[1024,768]{1,0:T(8,128)(2,1)} %bitcast.394, bf16[1024,2048]{1,0:T(8,128)(2,1)} %bitcast.393), custom_call_target="tpu_custom_call" | custom-call | flops 3221225472 | bytes 8912896 | tf_op jit(solution)/shard_map/partial_blocks/pallas_call | solution.py:65
  10.4 0.5 collective-permute-start
  10.9 0.9 slice_bitcast_fusion.61
  11.8 1.6 %slice_bitcast_fusion.50 = (bf16[1,96,512]{2,1,0:T(8,128)(2,1)S(1)}, bf16[1,96,512]{2,1,0:T(8,128)(2,1)S(1)}, bf16[1,96,512]{2,1,0:T(8,128)(2,1)S(1)}, bf16[1,96...) fusion(bf16[4,4,96,512]{3,2,1,0:T(8,128)(2,1)} %get-tuple-eleme, ...), kind=kLoop, calls=%fused_computation.244 | loop fusion | flops 98304 | bytes 3342336 | tf_op jit(solution)/shard_map/stack;squeeze | solution.py:125
  13.4 0.7 collective-permute-done
  14.1 0.2 slice_bitcast_fusion.36
  14.3 2.9 %collective-permute-start.1 = (bf16[2,96,512]{2,1,0:T(8,128)(2,1)S(1)}, bf16[2,96,512]{2,1,0:T(8,128)(2,1)S(1)}, u32[]{:S(2)}, u32[]{:S(2)}) collective-permute-start(bf16[2,96,512]{2,1,0:T(8,128)(2,1)S(1)} %pad_maximum_fusion.16), channel_id=1, source_target_pairs={{0,8},{1,9},{2,10},{3,11},{4,12},{5,13},{6,14},{7,15},{8,0},{9,1},... | collective-permute-start | bytes 589832 | tf_op jit(solution)/shard_map/ppermute | solution.py:129
  17.3 1.6 %collective-permute-start.2 = (bf16[2,96,512]{2,1,0:T(8,128)(2,1)S(1)}, bf16[2,96,512]{2,1,0:T(8,128)(2,1)S(1)}, u32[]{:S(2)}, u32[]{:S(2)}) collective-permute-start(bf16[2,96,512]{2,1,0:T(8,128)(2,1)S(1)} %pad_maximum_fusion.17), channel_id=1, source_target_pairs={{0,16},{1,17},{2,18},{3,19},{4,20},{5,21},{6,22},{7,23},{8,24},{9,... | collective-permute-start | bytes 589832 | tf_op jit(solution)/shard_map/ppermute | solution.py:129
  19.0 2.0 %collective-permute-start.7 = (bf16[2,96,512]{2,1,0:T(8,128)(2,1)S(1)}, bf16[2,96,512]{2,1,0:T(8,128)(2,1)S(1)}, u32[]{:S(2)}, u32[]{:S(2)}) collective-permute-start(bf16[2,96,512]{2,1,0:T(8,128)(2,1)S(1)} %pad_maximum_fusion.19), channel_id=1, source_target_pairs={{0,8},{1,9},{2,10},{3,11},{4,12},{5,13},{6,14},{7,15},{8,0},{9,1},... | collective-permute-start | bytes 589832 | tf_op jit(solution)/shard_map/ppermute | solution.py:129
  21.0 1.6 %collective-permute-start.8 = (bf16[2,96,512]{2,1,0:T(8,128)(2,1)S(1)}, bf16[2,96,512]{2,1,0:T(8,128)(2,1)S(1)}, u32[]{:S(2)}, u32[]{:S(2)}) collective-permute-start(bf16[2,96,512]{2,1,0:T(8,128)(2,1)S(1)} %pad_maximum_fusion.20), channel_id=1, source_target_pairs={{0,16},{1,17},{2,18},{3,19},{4,20},{5,21},{6,22},{7,23},{8,24},{9,... | collective-permute-start | bytes 589832 | tf_op jit(solution)/shard_map/ppermute | solution.py:129
  23.0 3.0 %collective-permute-start.9 = (bf16[2,96,512]{2,1,0:T(8,128)(2,1)S(1)}, bf16[2,96,512]{2,1,0:T(8,128)(2,1)S(1)}, u32[]{:S(2)}, u32[]{:S(2)}) collective-permute-start(bf16[2,96,512]{2,1,0:T(8,128)(2,1)S(1)} %pad_maximum_fusion.21), channel_id=1, source_target_pairs={{0,24},{1,25},{2,26},{3,27},{4,28},{5,29},{6,30},{7,31},{8,16},{9,... | collective-permute-start | bytes 589832 | tf_op jit(solution)/shard_map/ppermute | solution.py:129
  26.0 3.3 %collective-permute-done.2 = bf16[2,96,512]{2,1,0:T(8,128)(2,1)S(1)} collective-permute-done((bf16[2,96,512]{2,1,0:T(8,128)(2,1)S(1)}, bf16[2,96,512]{2,1,0:T(8,128)(2,1)S(1)}, u32[]{:S(2)}, u32[]{:S(2)}) %collective-permute-start.2) | collective-permute-done | bytes 196640 | tf_op jit(solution)/shard_map/ppermute | solution.py:129
  29.5 0.3 add_convert_fusion.2
  29.8 1.6 %collective-permute-start.11 = (bf16[3,96,512]{2,1,0:T(8,128)(2,1)S(1)}, bf16[3,96,512]{2,1,0:T(8,128)(2,1)S(1)}, u32[]{:S(2)}, u32[]{:S(2)}) collective-permute-start(bf16[3,96,512]{2,1,0:T(8,128)(2,1)S(1)} %add_convert_fusion.2), channel_id=1, source_target_pairs={{0,2},{1,3},{2,4},{3,5},{4,6},{5,7},{6,0},{7,1},{8,10},{9,11},{10,... | collective-permute-start | bytes 884744 | tf_op jit(solution)/shard_map/ppermute | solution.py:134
  31.4 0.8 collective-permute-start.4
  32.3 1.3 %collective-permute-start.5 = (bf16[2,96,512]{2,1,0:T(8,128)(2,1)S(1)}, bf16[2,96,512]{2,1,0:T(8,128)(2,1)S(1)}, u32[]{:S(2)}, u32[]{:S(2)}) collective-permute-start(bf16[2,96,512]{2,1,0:T(8,128)(2,1)S(1)} %get-tuple-element.20), channel_id=1, source_target_pairs={{0,16},{1,17},{2,18},{3,19},{4,20},{5,21},{6,22},{7,23},{8,24},{9,... | collective-permute-start | bytes 589832 | tf_op jit(solution)/shard_map/ppermute | solution.py:129
  33.6 3.2 %collective-permute-done.8 = bf16[2,96,512]{2,1,0:T(8,128)(2,1)S(1)} collective-permute-done((bf16[2,96,512]{2,1,0:T(8,128)(2,1)S(1)}, bf16[2,96,512]{2,1,0:T(8,128)(2,1)S(1)}, u32[]{:S(2)}, u32[]{:S(2)}) %collective-permute-start.8) | collective-permute-done | bytes 196640 | tf_op jit(solution)/shard_map/ppermute | solution.py:129
  36.9 0.3 collective-permute-done.9
  37.2 0.3 add_convert_fusion.1
  37.6 2.7 %collective-permute-start.10 = (bf16[3,96,512]{2,1,0:T(8,128)(2,1)S(1)}, bf16[3,96,512]{2,1,0:T(8,128)(2,1)S(1)}, u32[]{:S(2)}, u32[]{:S(2)}) collective-permute-start(bf16[3,96,512]{2,1,0:T(8,128)(2,1)S(1)} %add_convert_fusion.1), channel_id=1, source_target_pairs={{0,4},{1,5},{2,6},{3,7},{4,0},{5,1},{6,2},{7,3},{8,12},{9,13},{10,... | collective-permute-start | bytes 884744 | tf_op jit(solution)/shard_map/ppermute | solution.py:134
  40.2 1.5 %collective-permute-start.12 = (bf16[2,96,512]{2,1,0:T(8,128)(2,1)S(1)}, bf16[2,96,512]{2,1,0:T(8,128)(2,1)S(1)}, u32[]{:S(2)}, u32[]{:S(2)}) collective-permute-start(bf16[2,96,512]{2,1,0:T(8,128)(2,1)S(1)} %get-tuple-element.23), channel_id=1, source_target_pairs={{0,8},{1,9},{2,10},{3,11},{4,12},{5,13},{6,14},{7,15},{8,0},{9,1},... | collective-permute-start | bytes 589832 | tf_op jit(solution)/shard_map/ppermute | solution.py:129
  41.8 4.1 %collective-permute-done.12 = bf16[2,96,512]{2,1,0:T(8,128)(2,1)S(1)} collective-permute-done((bf16[2,96,512]{2,1,0:T(8,128)(2,1)S(1)}, bf16[2,96,512]{2,1,0:T(8,128)(2,1)S(1)}, u32[]{:S(2)}, u32[]{:S(2)}) %collective-permute-start.12) | collective-permute-done | bytes 196640 | tf_op jit(solution)/shard_map/ppermute | solution.py:129
  45.9 2.1 %collective-permute-start.13 = (bf16[2,96,512]{2,1,0:T(8,128)(2,1)S(1)}, bf16[2,96,512]{2,1,0:T(8,128)(2,1)S(1)}, u32[]{:S(2)}, u32[]{:S(2)}) collective-permute-start(bf16[2,96,512]{2,1,0:T(8,128)(2,1)S(1)} %get-tuple-element.24), channel_id=1, source_target_pairs={{0,16},{1,17},{2,18},{3,19},{4,20},{5,21},{6,22},{7,23},{8,24},{9,... | collective-permute-start | bytes 589832 | tf_op jit(solution)/shard_map/ppermute | solution.py:129
  48.1 5.7 %collective-permute-done.13 = bf16[2,96,512]{2,1,0:T(8,128)(2,1)S(1)} collective-permute-done((bf16[2,96,512]{2,1,0:T(8,128)(2,1)S(1)}, bf16[2,96,512]{2,1,0:T(8,128)(2,1)S(1)}, u32[]{:S(2)}, u32[]{:S(2)}) %collective-permute-start.13) | collective-permute-done | bytes 196640 | tf_op jit(solution)/shard_map/ppermute | solution.py:129
  53.8 1.5 %collective-permute-start.14 = (bf16[2,96,512]{2,1,0:T(8,128)(2,1)S(1)}, bf16[2,96,512]{2,1,0:T(8,128)(2,1)S(1)}, u32[]{:S(2)}, u32[]{:S(2)}) collective-permute-start(bf16[2,96,512]{2,1,0:T(8,128)(2,1)S(1)} %get-tuple-element.25), channel_id=1, source_target_pairs={{0,24},{1,25},{2,26},{3,27},{4,28},{5,29},{6,30},{7,31},{8,16},{9,... | collective-permute-start | bytes 589832 | tf_op jit(solution)/shard_map/ppermute | solution.py:129
  55.3 5.7 %collective-permute-done.14 = bf16[2,96,512]{2,1,0:T(8,128)(2,1)S(1)} collective-permute-done((bf16[2,96,512]{2,1,0:T(8,128)(2,1)S(1)}, bf16[2,96,512]{2,1,0:T(8,128)(2,1)S(1)}, u32[]{:S(2)}, u32[]{:S(2)}) %collective-permute-start.14) | collective-permute-done | bytes 196640 | tf_op jit(solution)/shard_map/ppermute | solution.py:129
  61.0 1.4 %collective-permute-start.6 = (bf16[2,96,512]{2,1,0:T(8,128)(2,1)S(1)}, bf16[2,96,512]{2,1,0:T(8,128)(2,1)S(1)}, u32[]{:S(2)}, u32[]{:S(2)}) collective-permute-start(bf16[2,96,512]{2,1,0:T(8,128)(2,1)S(1)} %get-tuple-element.21), channel_id=1, source_target_pairs={{0,24},{1,25},{2,26},{3,27},{4,28},{5,29},{6,30},{7,31},{8,16},{9,... | collective-permute-start | bytes 589832 | tf_op jit(solution)/shard_map/ppermute | solution.py:129
  62.5 0.3 add_convert_fusion
  63.0 4.6 %collective-permute-done.6 = bf16[2,96,512]{2,1,0:T(8,128)(2,1)S(1)} collective-permute-done((bf16[2,96,512]{2,1,0:T(8,128)(2,1)S(1)}, bf16[2,96,512]{2,1,0:T(8,128)(2,1)S(1)}, u32[]{:S(2)}, u32[]{:S(2)}) %collective-permute-start.6) | collective-permute-done | bytes 196640 | tf_op jit(solution)/shard_map/ppermute | solution.py:129
  67.7 4.4 %collective-permute-done.15 = bf16[3,96,512]{2,1,0:T(8,128)(2,1)S(1)} collective-permute-done((bf16[3,96,512]{2,1,0:T(8,128)(2,1)S(1)}, bf16[3,96,512]{2,1,0:T(8,128)(2,1)S(1)}, u32[]{:S(2)}, u32[]{:S(2)}) %collective-permute-start.15) | collective-permute-done | bytes 294944 | tf_op jit(solution)/shard_map/ppermute | solution.py:134
  72.0 1.8 %fusion.63 = (bf16[3,96,512]{2,1,0:T(8,128)(2,1)S(1)}, f32[3,96,512]{2,1,0:T(8,128)}, f32[3,96,512]{2,1,0:T(8,128)}, f32[3,96,512]{2,1,0:T(8,128)}) fusion(f32[3,96,512]{2,1,0:T(8,128)S(1)} %copy-done.1, f32[3,96,512]{2,1,0:T(8,128)S(1)} %copy-done.2, f32[3,96,512]{2,1,0:T(8,128)S(1)} %copy-done.3, bf16[3,96,512]{2,1,0:T(8,128)(2,1)S(1)} %collective-permute-done.15, ...), kind=kLoop, calls=%fused_computation.321 | loop fusion | flops 5013504 | bytes 6340608 | tf_op jit(solution)/shard_map/convert_element_type | solution.py:140
  73.9 8.6 %collective-permute-start.25 = (bf16[3,96,512]{2,1,0:T(8,128)(2,1)S(1)}, bf16[3,96,512]{2,1,0:T(8,128)(2,1)S(1)}, u32[]{:S(2)}, u32[]{:S(2)}) collective-permute-start(bf16[3,96,512]{2,1,0:T(8,128)(2,1)S(1)} %get-tuple-element.98), channel_id=1, source_target_pairs={{0,2},{1,3},{2,4},{3,5},{4,6},{5,7},{6,0},{7,1},{8,10},{9,11},{10,... | collective-permute-start | bytes 884744 | tf_op jit(solution)/shard_map/ppermute | solution.py:150
  82.5 1.5 %collective-permute-start.30 = (bf16[3,96,512]{2,1,0:T(8,128)(2,1)S(1)}, bf16[3,96,512]{2,1,0:T(8,128)(2,1)S(1)}, u32[]{:S(2)}, u32[]{:S(2)}) collective-permute-start(bf16[3,96,512]{2,1,0:T(8,128)(2,1)S(1)} %get-tuple-element.98), channel_id=1, source_target_pairs={{0,4},{1,5},{2,6},{3,7},{4,0},{5,1},{6,2},{7,3},{8,12},{9,13},{10,... | collective-permute-start | bytes 884744 | tf_op jit(solution)/shard_map/ppermute | solution.py:150
  83.9 3.2 %collective-permute-done.20 = bf16[3,96,512]{2,1,0:T(8,128)(2,1)S(1)} collective-permute-done((bf16[3,96,512]{2,1,0:T(8,128)(2,1)S(1)}, bf16[3,96,512]{2,1,0:T(8,128)(2,1)S(1)}, u32[]{:S(2)}, u32[]{:S(2)}) %collective-permute-start.20) | collective-permute-done | bytes 294944 | tf_op jit(solution)/shard_map/ppermute | solution.py:150
  87.2 3.7 %collective-permute-done.25 = bf16[3,96,512]{2,1,0:T(8,128)(2,1)S(1)} collective-permute-done((bf16[3,96,512]{2,1,0:T(8,128)(2,1)S(1)}, bf16[3,96,512]{2,1,0:T(8,128)(2,1)S(1)}, u32[]{:S(2)}, u32[]{:S(2)}) %collective-permute-start.25) | collective-permute-done | bytes 294944 | tf_op jit(solution)/shard_map/ppermute | solution.py:150
  90.9 7.2 %collective-permute-done.30 = bf16[3,96,512]{2,1,0:T(8,128)(2,1)S(1)} collective-permute-done((bf16[3,96,512]{2,1,0:T(8,128)(2,1)S(1)}, bf16[3,96,512]{2,1,0:T(8,128)(2,1)S(1)}, u32[]{:S(2)}, u32[]{:S(2)}) %collective-permute-start.30) | collective-permute-done | bytes 294944 | tf_op jit(solution)/shard_map/ppermute | solution.py:150
  98.1 1.5 %fusion.11 = (bf16[96,512]{1,0:T(8,128)(2,1)S(1)}, bf16[96,512]{1,0:T(8,128)(2,1)S(1)}, bf16[96,512]{1,0:T(8,128)(2,1)S(1)}, bf16[96,512]{1,0:T(8,128)(2,1)S(1)}...) fusion(bf16[3,96,512]{2,1,0:T(8,128)(2,1)S(1)} %get-tuple-eleme, ...), kind=kLoop, calls=%fused_computation.48 | loop fusion | flops 8454144 | bytes 4374528 | tf_op jit(solution)/shard_map/reduce_sum | solution.py:154
  99.7 1.2 collective-permute-start.33
  100.9 2.0 %collective-permute-start.31 = (bf16[2,96,512]{2,1,0:T(8,128)(2,1)S(1)}, bf16[2,96,512]{2,1,0:T(8,128)(2,1)S(1)}, u32[]{:S(2)}, u32[]{:S(2)}) collective-permute-start(bf16[2,96,512]{2,1,0:T(8,128)(2,1)S(1)} %pad_maximum_fusion.35), channel_id=1, source_target_pairs={{0,24},{1,25},{2,26},{3,27},{4,28},{5,29},{6,30},{7,31},{8,16},{9,... | collective-permute-start | bytes 589832 | tf_op jit(solution)/shard_map/ppermute | solution.py:156
  103.0 0.5 collective-permute-start.32
  103.4 1.2 collective-permute-start.28
  104.7 2.0 %collective-permute-start.26 = (bf16[2,96,512]{2,1,0:T(8,128)(2,1)S(1)}, bf16[2,96,512]{2,1,0:T(8,128)(2,1)S(1)}, u32[]{:S(2)}, u32[]{:S(2)}) collective-permute-start(bf16[2,96,512]{2,1,0:T(8,128)(2,1)S(1)} %pad_maximum_fusion.32), channel_id=1, source_target_pairs={{0,24},{1,25},{2,26},{3,27},{4,28},{5,29},{6,30},{7,31},{8,16},{9,... | collective-permute-start | bytes 589832 | tf_op jit(solution)/shard_map/ppermute | solution.py:156
  106.9 0.5 collective-permute-start.27
  107.4 1.3 %collective-permute-done.31 = bf16[2,96,512]{2,1,0:T(8,128)(2,1)S(1)} collective-permute-done((bf16[2,96,512]{2,1,0:T(8,128)(2,1)S(1)}, bf16[2,96,512]{2,1,0:T(8,128)(2,1)S(1)}, u32[]{:S(2)}, u32[]{:S(2)}) %collective-permute-start.31) | collective-permute-done | bytes 196640 | tf_op jit(solution)/shard_map/ppermute | solution.py:156
  108.7 0.5 collective-permute-start.23
  109.2 1.5 %collective-permute-done.32 = bf16[2,96,512]{2,1,0:T(8,128)(2,1)S(1)} collective-permute-done((bf16[2,96,512]{2,1,0:T(8,128)(2,1)S(1)}, bf16[2,96,512]{2,1,0:T(8,128)(2,1)S(1)}, u32[]{:S(2)}, u32[]{:S(2)}) %collective-permute-start.32) | collective-permute-done | bytes 196640 | tf_op jit(solution)/shard_map/ppermute | solution.py:156
  110.7 1.0 collective-permute-start.21
  111.8 1.5 %collective-permute-start.18 = (bf16[2,96,512]{2,1,0:T(8,128)(2,1)S(1)}, bf16[2,96,512]{2,1,0:T(8,128)(2,1)S(1)}, u32[]{:S(2)}, u32[]{:S(2)}) collective-permute-start(bf16[2,96,512]{2,1,0:T(8,128)(2,1)S(1)} %pad_maximum_fusion.28), channel_id=1, source_target_pairs={{0,8},{1,9},{2,10},{3,11},{4,12},{5,13},{6,14},{7,15},{8,0},{9,1},... | collective-permute-start | bytes 589832 | tf_op jit(solution)/shard_map/ppermute | solution.py:156
  113.3 1.1 collective-permute-start.16
  114.4 0.5 collective-permute-done.27
  114.9 1.0 collective-permute-start.17
  116.1 2.8 %collective-permute-done.18 = bf16[2,96,512]{2,1,0:T(8,128)(2,1)S(1)} collective-permute-done((bf16[2,96,512]{2,1,0:T(8,128)(2,1)S(1)}, bf16[2,96,512]{2,1,0:T(8,128)(2,1)S(1)}, u32[]{:S(2)}, u32[]{:S(2)}) %collective-permute-start.18) | collective-permute-done | bytes 196640 | tf_op jit(solution)/shard_map/ppermute | solution.py:156
  118.9 1.1 collective-permute-start.22
  119.9 1.6 %collective-permute-done.16 = bf16[2,96,512]{2,1,0:T(8,128)(2,1)S(1)} collective-permute-done((bf16[2,96,512]{2,1,0:T(8,128)(2,1)S(1)}, bf16[2,96,512]{2,1,0:T(8,128)(2,1)S(1)}, u32[]{:S(2)}, u32[]{:S(2)}) %collective-permute-start.16) | collective-permute-done | bytes 196640 | tf_op jit(solution)/shard_map/ppermute | solution.py:156
  121.6 1.1 collective-permute-done.17
  122.9 0.6 collective-permute-start.19
  123.4 1.4 %collective-permute-done.22 = bf16[2,96,512]{2,1,0:T(8,128)(2,1)S(1)} collective-permute-done((bf16[2,96,512]{2,1,0:T(8,128)(2,1)S(1)}, bf16[2,96,512]{2,1,0:T(8,128)(2,1)S(1)}, u32[]{:S(2)}, u32[]{:S(2)}) %collective-permute-start.22) | collective-permute-done | bytes 196640 | tf_op jit(solution)/shard_map/ppermute | solution.py:156
  125.1 0.2 broadcast_select_fusion.7
  125.2 0.4 broadcast_in_dim.14
  125.7 1.0 collective-permute-done.24
  126.8 0.2 broadcast_select_fusion.5
  127.1 0.2 broadcast_select_fusion.3
  127.6 1.7 %copy-done = bf16[4,2,96,2048]{3,2,1,0:T(8,128)(2,1)} copy-done((bf16[4,2,96,2048]{3,2,1,0:T(8,128)(2,1)}, bf16[4,2,96,2048]{3,2,1,0:T(8,128)(2,1)S(1)}, u32[]{:S(2)}) %copy-start) | copy-done | bytes 3145752
  (85 shorter events, 2.5 us)
Async XLA Ops:
  10.4 3.8 %collective-permute-start = (bf16[4,4,96,512]{3,2,1,0:T(8,128)(2,1)}, bf16[4,4,96,512]{3,2,1,0:T(8,128)(2,1)S(1)}, u32[]{:S(2)}, u32[]{:S(2)}) collective-permute-start(bf16[4,4,96,512]{3,2,1,0:T(8,128)(2,1)} %get-tuple-element.17), channel_id=1, source_target_pairs={{0,1},{1,0},{2,3},{3,2},{4,5},{5,4},{6,7},{7,6},{8,9},{9,8},{10,11... | collective-permute-start | bytes 4718600 | tf_op jit(solution)/shard_map/ppermute | solution.py:120
  14.3 8.6 %collective-permute-start.1 = (bf16[2,96,512]{2,1,0:T(8,128)(2,1)S(1)}, bf16[2,96,512]{2,1,0:T(8,128)(2,1)S(1)}, u32[]{:S(2)}, u32[]{:S(2)}) collective-permute-start(bf16[2,96,512]{2,1,0:T(8,128)(2,1)S(1)} %pad_maximum_fusion.16), channel_id=1, source_target_pairs={{0,8},{1,9},{2,10},{3,11},{4,12},{5,13},{6,14},{7,15},{8,0},{9,1},... | collective-permute-start | bytes 589832 | tf_op jit(solution)/shard_map/ppermute | solution.py:129
  17.3 12.1 %collective-permute-start.2 = (bf16[2,96,512]{2,1,0:T(8,128)(2,1)S(1)}, bf16[2,96,512]{2,1,0:T(8,128)(2,1)S(1)}, u32[]{:S(2)}, u32[]{:S(2)}) collective-permute-start(bf16[2,96,512]{2,1,0:T(8,128)(2,1)S(1)} %pad_maximum_fusion.17), channel_id=1, source_target_pairs={{0,16},{1,17},{2,18},{3,19},{4,20},{5,21},{6,22},{7,23},{8,24},{9,... | collective-permute-start | bytes 589832 | tf_op jit(solution)/shard_map/ppermute | solution.py:129
  18.9 10.5 %collective-permute-start.3 = (bf16[2,96,512]{2,1,0:T(8,128)(2,1)S(1)}, bf16[2,96,512]{2,1,0:T(8,128)(2,1)S(1)}, u32[]{:S(2)}, u32[]{:S(2)}) collective-permute-start(bf16[2,96,512]{2,1,0:T(8,128)(2,1)S(1)} %pad_maximum_fusion.18), channel_id=1, source_target_pairs={{0,24},{1,25},{2,26},{3,27},{4,28},{5,29},{6,30},{7,31},{8,16},{9,... | collective-permute-start | bytes 589832 | tf_op jit(solution)/shard_map/ppermute | solution.py:129
  19.0 13.3 %collective-permute-start.7 = (bf16[2,96,512]{2,1,0:T(8,128)(2,1)S(1)}, bf16[2,96,512]{2,1,0:T(8,128)(2,1)S(1)}, u32[]{:S(2)}, u32[]{:S(2)}) collective-permute-start(bf16[2,96,512]{2,1,0:T(8,128)(2,1)S(1)} %pad_maximum_fusion.19), channel_id=1, source_target_pairs={{0,8},{1,9},{2,10},{3,11},{4,12},{5,13},{6,14},{7,15},{8,0},{9,1},... | collective-permute-start | bytes 589832 | tf_op jit(solution)/shard_map/ppermute | solution.py:129
  21.0 15.8 %collective-permute-start.8 = (bf16[2,96,512]{2,1,0:T(8,128)(2,1)S(1)}, bf16[2,96,512]{2,1,0:T(8,128)(2,1)S(1)}, u32[]{:S(2)}, u32[]{:S(2)}) collective-permute-start(bf16[2,96,512]{2,1,0:T(8,128)(2,1)S(1)} %pad_maximum_fusion.20), channel_id=1, source_target_pairs={{0,16},{1,17},{2,18},{3,19},{4,20},{5,21},{6,22},{7,23},{8,24},{9,... | collective-permute-start | bytes 589832 | tf_op jit(solution)/shard_map/ppermute | solution.py:129
  23.0 14.3 %collective-permute-start.9 = (bf16[2,96,512]{2,1,0:T(8,128)(2,1)S(1)}, bf16[2,96,512]{2,1,0:T(8,128)(2,1)S(1)}, u32[]{:S(2)}, u32[]{:S(2)}) collective-permute-start(bf16[2,96,512]{2,1,0:T(8,128)(2,1)S(1)} %pad_maximum_fusion.21), channel_id=1, source_target_pairs={{0,24},{1,25},{2,26},{3,27},{4,28},{5,29},{6,30},{7,31},{8,16},{9,... | collective-permute-start | bytes 589832 | tf_op jit(solution)/shard_map/ppermute | solution.py:129
  29.8 37.9 %collective-permute-start.11 = (bf16[3,96,512]{2,1,0:T(8,128)(2,1)S(1)}, bf16[3,96,512]{2,1,0:T(8,128)(2,1)S(1)}, u32[]{:S(2)}, u32[]{:S(2)}) collective-permute-start(bf16[3,96,512]{2,1,0:T(8,128)(2,1)S(1)} %add_convert_fusion.2), channel_id=1, source_target_pairs={{0,2},{1,3},{2,4},{3,5},{4,6},{5,7},{6,0},{7,1},{8,10},{9,11},{10,... | collective-permute-start | bytes 884744 | tf_op jit(solution)/shard_map/ppermute | solution.py:134
  31.4 31.5 %collective-permute-start.4 = (bf16[2,96,512]{2,1,0:T(8,128)(2,1)S(1)}, bf16[2,96,512]{2,1,0:T(8,128)(2,1)S(1)}, u32[]{:S(2)}, u32[]{:S(2)}) collective-permute-start(bf16[2,96,512]{2,1,0:T(8,128)(2,1)S(1)} %get-tuple-element.19), channel_id=1, source_target_pairs={{0,8},{1,9},{2,10},{3,11},{4,12},{5,13},{6,14},{7,15},{8,0},{9,1},... | collective-permute-start | bytes 589832 | tf_op jit(solution)/shard_map/ppermute | solution.py:129
  32.3 30.7 %collective-permute-start.5 = (bf16[2,96,512]{2,1,0:T(8,128)(2,1)S(1)}, bf16[2,96,512]{2,1,0:T(8,128)(2,1)S(1)}, u32[]{:S(2)}, u32[]{:S(2)}) collective-permute-start(bf16[2,96,512]{2,1,0:T(8,128)(2,1)S(1)} %get-tuple-element.20), channel_id=1, source_target_pairs={{0,16},{1,17},{2,18},{3,19},{4,20},{5,21},{6,22},{7,23},{8,24},{9,... | collective-permute-start | bytes 589832 | tf_op jit(solution)/shard_map/ppermute | solution.py:129
  37.6 30.1 %collective-permute-start.10 = (bf16[3,96,512]{2,1,0:T(8,128)(2,1)S(1)}, bf16[3,96,512]{2,1,0:T(8,128)(2,1)S(1)}, u32[]{:S(2)}, u32[]{:S(2)}) collective-permute-start(bf16[3,96,512]{2,1,0:T(8,128)(2,1)S(1)} %add_convert_fusion.1), channel_id=1, source_target_pairs={{0,4},{1,5},{2,6},{3,7},{4,0},{5,1},{6,2},{7,3},{8,12},{9,13},{10,... | collective-permute-start | bytes 884744 | tf_op jit(solution)/shard_map/ppermute | solution.py:134
  40.2 5.7 %collective-permute-start.12 = (bf16[2,96,512]{2,1,0:T(8,128)(2,1)S(1)}, bf16[2,96,512]{2,1,0:T(8,128)(2,1)S(1)}, u32[]{:S(2)}, u32[]{:S(2)}) collective-permute-start(bf16[2,96,512]{2,1,0:T(8,128)(2,1)S(1)} %get-tuple-element.23), channel_id=1, source_target_pairs={{0,8},{1,9},{2,10},{3,11},{4,12},{5,13},{6,14},{7,15},{8,0},{9,1},... | collective-permute-start | bytes 589832 | tf_op jit(solution)/shard_map/ppermute | solution.py:129
  45.9 7.9 %collective-permute-start.13 = (bf16[2,96,512]{2,1,0:T(8,128)(2,1)S(1)}, bf16[2,96,512]{2,1,0:T(8,128)(2,1)S(1)}, u32[]{:S(2)}, u32[]{:S(2)}) collective-permute-start(bf16[2,96,512]{2,1,0:T(8,128)(2,1)S(1)} %get-tuple-element.24), channel_id=1, source_target_pairs={{0,16},{1,17},{2,18},{3,19},{4,20},{5,21},{6,22},{7,23},{8,24},{9,... | collective-permute-start | bytes 589832 | tf_op jit(solution)/shard_map/ppermute | solution.py:129
  53.8 7.2 %collective-permute-start.14 = (bf16[2,96,512]{2,1,0:T(8,128)(2,1)S(1)}, bf16[2,96,512]{2,1,0:T(8,128)(2,1)S(1)}, u32[]{:S(2)}, u32[]{:S(2)}) collective-permute-start(bf16[2,96,512]{2,1,0:T(8,128)(2,1)S(1)} %get-tuple-element.25), channel_id=1, source_target_pairs={{0,24},{1,25},{2,26},{3,27},{4,28},{5,29},{6,30},{7,31},{8,16},{9,... | collective-permute-start | bytes 589832 | tf_op jit(solution)/shard_map/ppermute | solution.py:129
  61.0 6.6 %collective-permute-start.6 = (bf16[2,96,512]{2,1,0:T(8,128)(2,1)S(1)}, bf16[2,96,512]{2,1,0:T(8,128)(2,1)S(1)}, u32[]{:S(2)}, u32[]{:S(2)}) collective-permute-start(bf16[2,96,512]{2,1,0:T(8,128)(2,1)S(1)} %get-tuple-element.21), channel_id=1, source_target_pairs={{0,24},{1,25},{2,26},{3,27},{4,28},{5,29},{6,30},{7,31},{8,16},{9,... | collective-permute-start | bytes 589832 | tf_op jit(solution)/shard_map/ppermute | solution.py:129
  62.5 9.5 %copy-start.1 = (f32[3,96,512]{2,1,0:T(8,128)S(1)}, f32[3,96,512]{2,1,0:T(8,128)}, u32[]{:S(2)}) copy-start(f32[3,96,512]{2,1,0:T(8,128)} %param.13) | copy-start | bytes 1769476
  62.5 9.5 %copy-start.2 = (f32[3,96,512]{2,1,0:T(8,128)S(1)}, f32[3,96,512]{2,1,0:T(8,128)}, u32[]{:S(2)}) copy-start(f32[3,96,512]{2,1,0:T(8,128)} %param.14) | copy-start | bytes 1769476
  62.5 9.5 %copy-start.3 = (f32[3,96,512]{2,1,0:T(8,128)S(1)}, f32[3,96,512]{2,1,0:T(8,128)}, u32[]{:S(2)}) copy-start(f32[3,96,512]{2,1,0:T(8,128)} %param.15) | copy-start | bytes 1769476
  62.9 9.2 %collective-permute-start.15 = (bf16[3,96,512]{2,1,0:T(8,128)(2,1)S(1)}, bf16[3,96,512]{2,1,0:T(8,128)(2,1)S(1)}, u32[]{:S(2)}, u32[]{:S(2)}) collective-permute-start(bf16[3,96,512]{2,1,0:T(8,128)(2,1)S(1)} %add_convert_fusion), channel_id=1, source_target_pairs={{0,6},{1,7},{2,0},{3,1},{4,2},{5,3},{6,4},{7,5},{8,14},{9,15},{10,... | collective-permute-start | bytes 884744 | tf_op jit(solution)/shard_map/ppermute | solution.py:134
  73.9 13.3 %collective-permute-start.20 = (bf16[3,96,512]{2,1,0:T(8,128)(2,1)S(1)}, bf16[3,96,512]{2,1,0:T(8,128)(2,1)S(1)}, u32[]{:S(2)}, u32[]{:S(2)}) collective-permute-start(bf16[3,96,512]{2,1,0:T(8,128)(2,1)S(1)} %get-tuple-element.98), channel_id=1, source_target_pairs={{0,6},{1,7},{2,0},{3,1},{4,2},{5,3},{6,4},{7,5},{8,14},{9,15},{10,... | collective-permute-start | bytes 884744 | tf_op jit(solution)/shard_map/ppermute | solution.py:150
  73.9 17.0 %collective-permute-start.25 = (bf16[3,96,512]{2,1,0:T(8,128)(2,1)S(1)}, bf16[3,96,512]{2,1,0:T(8,128)(2,1)S(1)}, u32[]{:S(2)}, u32[]{:S(2)}) collective-permute-start(bf16[3,96,512]{2,1,0:T(8,128)(2,1)S(1)} %get-tuple-element.98), channel_id=1, source_target_pairs={{0,2},{1,3},{2,4},{3,5},{4,6},{5,7},{6,0},{7,1},{8,10},{9,11},{10,... | collective-permute-start | bytes 884744 | tf_op jit(solution)/shard_map/ppermute | solution.py:150
  82.5 15.6 %collective-permute-start.30 = (bf16[3,96,512]{2,1,0:T(8,128)(2,1)S(1)}, bf16[3,96,512]{2,1,0:T(8,128)(2,1)S(1)}, u32[]{:S(2)}, u32[]{:S(2)}) collective-permute-start(bf16[3,96,512]{2,1,0:T(8,128)(2,1)S(1)} %get-tuple-element.98), channel_id=1, source_target_pairs={{0,4},{1,5},{2,6},{3,7},{4,0},{5,1},{6,2},{7,3},{8,12},{9,13},{10,... | collective-permute-start | bytes 884744 | tf_op jit(solution)/shard_map/ppermute | solution.py:150
  99.7 7.2 %collective-permute-start.33 = (bf16[2,96,512]{2,1,0:T(8,128)(2,1)S(1)}, bf16[2,96,512]{2,1,0:T(8,128)(2,1)S(1)}, u32[]{:S(2)}, u32[]{:S(2)}) collective-permute-start(bf16[2,96,512]{2,1,0:T(8,128)(2,1)S(1)} %pad_maximum_fusion.37), channel_id=1, source_target_pairs={{0,8},{1,9},{2,10},{3,11},{4,12},{5,13},{6,14},{7,15},{8,0},{9,1},... | collective-permute-start | bytes 589832 | tf_op jit(solution)/shard_map/ppermute | solution.py:156
  100.9 7.8 %collective-permute-start.31 = (bf16[2,96,512]{2,1,0:T(8,128)(2,1)S(1)}, bf16[2,96,512]{2,1,0:T(8,128)(2,1)S(1)}, u32[]{:S(2)}, u32[]{:S(2)}) collective-permute-start(bf16[2,96,512]{2,1,0:T(8,128)(2,1)S(1)} %pad_maximum_fusion.35), channel_id=1, source_target_pairs={{0,24},{1,25},{2,26},{3,27},{4,28},{5,29},{6,30},{7,31},{8,16},{9,... | collective-permute-start | bytes 589832 | tf_op jit(solution)/shard_map/ppermute | solution.py:156
  103.0 7.7 %collective-permute-start.32 = (bf16[2,96,512]{2,1,0:T(8,128)(2,1)S(1)}, bf16[2,96,512]{2,1,0:T(8,128)(2,1)S(1)}, u32[]{:S(2)}, u32[]{:S(2)}) collective-permute-start(bf16[2,96,512]{2,1,0:T(8,128)(2,1)S(1)} %pad_maximum_fusion.36), channel_id=1, source_target_pairs={{0,16},{1,17},{2,18},{3,19},{4,20},{5,21},{6,22},{7,23},{8,24},{9,... | collective-permute-start | bytes 589832 | tf_op jit(solution)/shard_map/ppermute | solution.py:156
  103.4 8.3 %collective-permute-start.28 = (bf16[2,96,512]{2,1,0:T(8,128)(2,1)S(1)}, bf16[2,96,512]{2,1,0:T(8,128)(2,1)S(1)}, u32[]{:S(2)}, u32[]{:S(2)}) collective-permute-start(bf16[2,96,512]{2,1,0:T(8,128)(2,1)S(1)} %pad_maximum_fusion.34), channel_id=1, source_target_pairs={{0,8},{1,9},{2,10},{3,11},{4,12},{5,13},{6,14},{7,15},{8,0},{9,1},... | collective-permute-start | bytes 589832 | tf_op jit(solution)/shard_map/ppermute | solution.py:156
  104.7 8.6 %collective-permute-start.26 = (bf16[2,96,512]{2,1,0:T(8,128)(2,1)S(1)}, bf16[2,96,512]{2,1,0:T(8,128)(2,1)S(1)}, u32[]{:S(2)}, u32[]{:S(2)}) collective-permute-start(bf16[2,96,512]{2,1,0:T(8,128)(2,1)S(1)} %pad_maximum_fusion.32), channel_id=1, source_target_pairs={{0,24},{1,25},{2,26},{3,27},{4,28},{5,29},{6,30},{7,31},{8,16},{9,... | collective-permute-start | bytes 589832 | tf_op jit(solution)/shard_map/ppermute | solution.py:156
  106.9 8.0 %collective-permute-start.27 = (bf16[2,96,512]{2,1,0:T(8,128)(2,1)S(1)}, bf16[2,96,512]{2,1,0:T(8,128)(2,1)S(1)}, u32[]{:S(2)}, u32[]{:S(2)}) collective-permute-start(bf16[2,96,512]{2,1,0:T(8,128)(2,1)S(1)} %pad_maximum_fusion.33), channel_id=1, source_target_pairs={{0,16},{1,17},{2,18},{3,19},{4,20},{5,21},{6,22},{7,23},{8,24},{9,... | collective-permute-start | bytes 589832 | tf_op jit(solution)/shard_map/ppermute | solution.py:156
  108.7 14.2 %collective-permute-start.23 = (bf16[2,96,512]{2,1,0:T(8,128)(2,1)S(1)}, bf16[2,96,512]{2,1,0:T(8,128)(2,1)S(1)}, u32[]{:S(2)}, u32[]{:S(2)}) collective-permute-start(bf16[2,96,512]{2,1,0:T(8,128)(2,1)S(1)} %pad_maximum_fusion.31), channel_id=1, source_target_pairs={{0,8},{1,9},{2,10},{3,11},{4,12},{5,13},{6,14},{7,15},{8,0},{9,1},... | collective-permute-start | bytes 589832 | tf_op jit(solution)/shard_map/ppermute | solution.py:156
  110.7 12.7 %collective-permute-start.21 = (bf16[2,96,512]{2,1,0:T(8,128)(2,1)S(1)}, bf16[2,96,512]{2,1,0:T(8,128)(2,1)S(1)}, u32[]{:S(2)}, u32[]{:S(2)}) collective-permute-start(bf16[2,96,512]{2,1,0:T(8,128)(2,1)S(1)} %pad_maximum_fusion.29), channel_id=1, source_target_pairs={{0,24},{1,25},{2,26},{3,27},{4,28},{5,29},{6,30},{7,31},{8,16},{9,... | collective-permute-start | bytes 589832 | tf_op jit(solution)/shard_map/ppermute | solution.py:156
  111.8 7.1 %collective-permute-start.18 = (bf16[2,96,512]{2,1,0:T(8,128)(2,1)S(1)}, bf16[2,96,512]{2,1,0:T(8,128)(2,1)S(1)}, u32[]{:S(2)}, u32[]{:S(2)}) collective-permute-start(bf16[2,96,512]{2,1,0:T(8,128)(2,1)S(1)} %pad_maximum_fusion.28), channel_id=1, source_target_pairs={{0,8},{1,9},{2,10},{3,11},{4,12},{5,13},{6,14},{7,15},{8,0},{9,1},... | collective-permute-start | bytes 589832 | tf_op jit(solution)/shard_map/ppermute | solution.py:156
  113.3 8.3 %collective-permute-start.16 = (bf16[2,96,512]{2,1,0:T(8,128)(2,1)S(1)}, bf16[2,96,512]{2,1,0:T(8,128)(2,1)S(1)}, u32[]{:S(2)}, u32[]{:S(2)}) collective-permute-start(bf16[2,96,512]{2,1,0:T(8,128)(2,1)S(1)} %pad_maximum_fusion.26), channel_id=1, source_target_pairs={{0,24},{1,25},{2,26},{3,27},{4,28},{5,29},{6,30},{7,31},{8,16},{9,... | collective-permute-start | bytes 589832 | tf_op jit(solution)/shard_map/ppermute | solution.py:156
  114.9 7.8 %collective-permute-start.17 = (bf16[2,96,512]{2,1,0:T(8,128)(2,1)S(1)}, bf16[2,96,512]{2,1,0:T(8,128)(2,1)S(1)}, u32[]{:S(2)}, u32[]{:S(2)}) collective-permute-start(bf16[2,96,512]{2,1,0:T(8,128)(2,1)S(1)} %pad_maximum_fusion.27), channel_id=1, source_target_pairs={{0,16},{1,17},{2,18},{3,19},{4,20},{5,21},{6,22},{7,23},{8,24},{9,... | collective-permute-start | bytes 589832 | tf_op jit(solution)/shard_map/ppermute | solution.py:156
  118.9 5.9 %collective-permute-start.22 = (bf16[2,96,512]{2,1,0:T(8,128)(2,1)S(1)}, bf16[2,96,512]{2,1,0:T(8,128)(2,1)S(1)}, u32[]{:S(2)}, u32[]{:S(2)}) collective-permute-start(bf16[2,96,512]{2,1,0:T(8,128)(2,1)S(1)} %pad_maximum_fusion.30), channel_id=1, source_target_pairs={{0,16},{1,17},{2,18},{3,19},{4,20},{5,21},{6,22},{7,23},{8,24},{9,... | collective-permute-start | bytes 589832 | tf_op jit(solution)/shard_map/ppermute | solution.py:156
  121.6 5.7 %collective-permute-start.34 = (bf16[4,96,512]{2,1,0:T(8,128)(2,1)S(1)}, bf16[4,96,512]{2,1,0:T(8,128)(2,1)S(1)}, u32[]{:S(2)}, u32[]{:S(2)}) collective-permute-start(bf16[4,96,512]{2,1,0:T(8,128)(2,1)S(1)} %pad_maximum_fusion.10), channel_id=1, source_target_pairs={{0,1},{1,0},{2,3},{3,2},{4,5},{5,4},{6,7},{7,6},{8,9},{9,8},{10,11... | collective-permute-start | bytes 1179656 | tf_op jit(solution)/shard_map/ppermute | solution.py:158
  122.7 4.3 %collective-permute-start.29 = (bf16[4,96,512]{2,1,0:T(8,128)(2,1)S(1)}, bf16[4,96,512]{2,1,0:T(8,128)(2,1)S(1)}, u32[]{:S(2)}, u32[]{:S(2)}) collective-permute-start(bf16[4,96,512]{2,1,0:T(8,128)(2,1)S(1)} %pad_maximum_fusion.7), channel_id=1, source_target_pairs={{0,1},{1,0},{2,3},{3,2},{4,5},{5,4},{6,7},{7,6},{8,9},{9,8},{10,11... | collective-permute-start | bytes 1179656 | tf_op jit(solution)/shard_map/ppermute | solution.py:158
  122.9 2.2 %collective-permute-start.19 = (bf16[4,96,512]{2,1,0:T(8,128)(2,1)S(1)}, bf16[4,96,512]{2,1,0:T(8,128)(2,1)S(1)}, u32[]{:S(2)}, u32[]{:S(2)}) collective-permute-start(bf16[4,96,512]{2,1,0:T(8,128)(2,1)S(1)} %pad_maximum_fusion.1), channel_id=1, source_target_pairs={{0,1},{1,0},{2,3},{3,2},{4,5},{5,4},{6,7},{7,6},{8,9},{9,8},{10,11... | collective-permute-start | bytes 1179656 | tf_op jit(solution)/shard_map/ppermute | solution.py:158
  125.0 1.8 %collective-permute-start.24 = (bf16[4,96,512]{2,1,0:T(8,128)(2,1)S(1)}, bf16[4,96,512]{2,1,0:T(8,128)(2,1)S(1)}, u32[]{:S(2)}, u32[]{:S(2)}) collective-permute-start(bf16[4,96,512]{2,1,0:T(8,128)(2,1)S(1)} %pad_maximum_fusion.4), channel_id=1, source_target_pairs={{0,1},{1,0},{2,3},{3,2},{4,5},{5,4},{6,7},{7,6},{8,9},{9,8},{10,11... | collective-permute-start | bytes 1179656 | tf_op jit(solution)/shard_map/ppermute | solution.py:158
  127.6 1.7 %copy-start = (bf16[4,2,96,2048]{3,2,1,0:T(8,128)(2,1)}, bf16[4,2,96,2048]{3,2,1,0:T(8,128)(2,1)S(1)}, u32[]{:S(2)}) copy-start(bf16[4,2,96,2048]{3,2,1,0:T(8,128)(2,1)S(1)} %fusion.3) | copy-start | bytes 9437188

commit v3 on v0

--- a/solution.py
+++ b/solution.py
@@ -1,6 +1,8 @@
 import jax
 import jax.numpy as jnp
 from jax import lax
+from jax.experimental import pallas as pl
+from jax.experimental.pallas import tpu as pltpu
 from jax.sharding import PartitionSpec as P
 
 beta_one = 0.9
@@ -10,8 +12,324 @@
 first_fix = 1.0 - beta_one**10
 second_fix = 1.0 - beta_two**10
 
-
-def per_device(
+AXES = ("dp", "expert")
+
+
+def adam(grad_sum, master, moment_one, moment_two):
+    moment_one_new = beta_one * moment_one + (1.0 - beta_one) * grad_sum
+    moment_two_new = beta_two * moment_two + (1.0 - beta_two) * grad_sum * grad_sum
+    master_new = master - learn_rate * (moment_one_new / first_fix) / (
+        jnp.sqrt(moment_two_new / second_fix) + epsilon
+    )
+    return master_new, moment_one_new, moment_two_new
+
+
+def plane_order(planes):
+    return sorted(range(planes), key=lambda s: -min(s, planes - s))
+
+
+def store_blocks(product, even_core, rows, at, j, keep_ref, send_ref):
+    even, odd = product[:rows], product[rows:]
+    keep_ref[at, j] = jnp.where(even_core, even, odd).astype(keep_ref.dtype)
+    send_ref[at, j] = jnp.where(even_core, odd, even).astype(send_ref.dtype)
+
+
+def first_kernel(
+    count_ref, now_hbm, next_hbm, hidden_hbm, upstream_hbm, turned_ref, upstream_ref, keep_ref, send_ref,
+    chosen_ref, hidden_ref, now_ref, next_ref, sems, small_sems,
+):
+    tokens, inner = hidden_ref.shape
+    groups, rows, cols = keep_ref.shape[1:]
+    planes = inner // (2 * rows)
+    parts = sems.shape[1]
+    part = tokens // parts
+    group, owner = lax.axis_index("dp"), lax.axis_index("expert")
+    plane, core = owner >> 1, owner & 1
+
+    smalls = [
+        pltpu.make_async_copy(source, target, small_sems.at[n])
+        for n, (source, target) in enumerate(((now_hbm, now_ref), (next_hbm, next_ref)))
+    ]
+    for copy in smalls:
+        copy.start()
+    copies = []
+    for n in range(parts):
+        at = pl.ds(n * part, part)
+        copies.append(
+            [
+                pltpu.make_async_copy(hidden_hbm.at[at], hidden_ref.at[at], sems.at[0, n]),
+                pltpu.make_async_copy(upstream_hbm.at[at], upstream_ref.at[at], sems.at[1, n]),
+            ]
+        )
+    for kind in range(2):
+        for copy in copies:
+            copy[kind].start()
+
+    for copy in smalls:
+        copy.wait()
+    names = lax.broadcasted_iota(jnp.int32, chosen_ref.shape[2:], 0)
+    for n, plan_ref in enumerate((now_ref, next_ref)):
+        for near in range(2 * groups):
+            named = plan_ref[group ^ (near // 2), 2 * plane + (core ^ (near % 2))]
+            chosen_ref[n, near] = jnp.where(names == named, 1.0, 0.0)
+
+    for n in range(parts):
+        copies[n][0].wait()
+        hidden = hidden_ref[n * part : (n + 1) * part]
+        live = lax.broadcasted_iota(jnp.int32, hidden.shape, 0) < count_ref[0, 0] - n * part
+        hidden = jnp.where(live, hidden, jnp.zeros_like(hidden)).T
+        for m, s in enumerate(plane_order(planes)):
+            for p in range(planes):
+
+                @pl.when(lax.rem(plane + s, planes) == p)
+                def put():
+                    turned_ref[2 * rows * m : 2 * rows * (m + 1), n * part : (n + 1) * part] = hidden[
+                        2 * rows * p : 2 * rows * (p + 1)
+                    ]
+    for n in range(parts):
+        copies[n][1].wait()
+
+    def columns(j, carry):
+        at = pl.ds(pl.multiple_of((group ^ j) * cols, cols), cols)
+        product = jnp.dot(
+            turned_ref[: 2 * rows], upstream_ref[:, at], preferred_element_type=jnp.float32
+        )
+        store_blocks(product, core == 0, rows, 0, j, keep_ref, send_ref)
+        return carry
+
+    lax.fori_loop(0, groups, columns, 0)
+
+
+def rest_kernel(turned_ref, upstream_ref, keep_ref, send_ref):
+    rest, groups, rows, cols = keep_ref.shape
+    group, core = lax.axis_index("dp"), lax.axis_index("expert") & 1
+
+    def columns(j, carry):
+        at = pl.ds(pl.multiple_of((group ^ j) * cols, cols), cols)
+        product = jnp.dot(
+            turned_ref[2 * rows :], upstream_ref[:, at], preferred_element_type=jnp.float32
+        )
+        for n in range(rest):
+            part = product[2 * rows * n : 2 * rows * (n + 1)]
+            store_blocks(part, core == 0, rows, n, j, keep_ref, send_ref)
+        return carry
+
+    lax.fori_loop(0, groups, columns, 0)
+
+
+def first_blocks(counts, plan_now, plan_next, hidden, upstream, experts):
+    groups, owners = plan_now.shape
+    planes = owners // 2
+    plan_now, plan_next, hidden, upstream = [
+        pltpu.with_memory_space_constraint(array, pltpu.HBM)
+        for array in (plan_now, plan_next, hidden, upstream)
+    ]
+    tokens, inner = hidden.shape
+    width = upstream.shape[1]
+    cols = width // groups
+    rows = inner // owners
+    parts = 4 if tokens % 512 == 0 else 1
+    hbm = pl.BlockSpec(memory_space=pltpu.HBM)
+    vmem = pl.BlockSpec(memory_space=pltpu.VMEM)
+
+    def blocks(n):
+        return jax.ShapeDtypeStruct((n, groups, rows, cols), jnp.bfloat16)
+
+    turned, copied, keep, send, chosen = pl.pallas_call(
+        first_kernel,
+        in_specs=[pl.BlockSpec(memory_space=pltpu.SMEM)] + [hbm] * 4,
+        out_specs=[vmem] * 5,
+        out_shape=[
+            jax.ShapeDtypeStruct((inner, tokens), jnp.bfloat16),
+            jax.ShapeDtypeStruct((tokens, width), jnp.bfloat16),
+            blocks(1),
+            blocks(1),
+            jax.ShapeDtypeStruct((2, 2 * groups, experts, cols), jnp.float32),
+        ],
+        scratch_shapes=[
+            pltpu.VMEM((tokens, inner), jnp.bfloat16),
+            pltpu.SMEM(plan_now.shape, jnp.int32),
+            pltpu.SMEM(plan_next.shape, jnp.int32),
+            pltpu.SemaphoreType.DMA((2, parts)),
+            pltpu.SemaphoreType.DMA((2,)),
+        ],
+        compiler_params=pltpu.CompilerParams(vmem_limit_bytes=24 * 2**20),
+        cost_estimate=pl.CostEstimate(
+            flops=4 * tokens * rows * width,
+            bytes_accessed=2 * (tokens * inner + tokens * width),
+            transcendentals=0,
+        ),
+        name="first_blocks",
+    )(counts, plan_now, plan_next, hidden, upstream)
+    return turned, copied, keep, send, chosen
+
+
+def rest_blocks(turned, upstream, groups, planes):
+    tokens, width = upstream.shape
+    inner = turned.shape[0]
+    cols = width // groups
+    rows = inner // (2 * planes)
+    vmem = pl.BlockSpec(memory_space=pltpu.VMEM)
+    out = jax.ShapeDtypeStruct((planes - 1, groups, rows, cols), jnp.bfloat16)
+    return pl.pallas_call(
+        rest_kernel,
+        in_specs=[vmem, vmem],
+        out_specs=[vmem, vmem],
+        out_shape=[out, out],
+        compiler_params=pltpu.CompilerParams(vmem_limit_bytes=24 * 2**20),
+        cost_estimate=pl.CostEstimate(
+            flops=2 * tokens * (inner - 2 * rows) * width,
+            bytes_accessed=2 * (inner - 2 * rows) * width,
+            transcendentals=0,
+        ),
+        name="rest_blocks",
+    )(turned, upstream)
+
+
+class Mail:
+    def __init__(self):
+        self.arrived = {}
+
+    def send(self, name, value, pairs, after=()):
+        self.arrived[name] = lax.ppermute(self.hold(value, after), AXES, pairs)
+
+    def hold(self, value, after):
+        if after:
+            value, *there = lax.optimization_barrier((value, *[self.arrived[n] for n in after]))
+            self.arrived.update(zip(after, there))
+        return value
+
+    def __getitem__(self, name):
+        return self.arrived[name]
+
+
+def per_device_planes(
+    hidden_acts, out_grads, row_counts, plan_now, plan_next, master, moment_one, moment_two
+):
+    groups = lax.axis_size("dp")
+    owners = lax.axis_size("expert")
+    planes = owners // 2
+    group = lax.axis_index("dp")
+    owner = lax.axis_index("expert")
+    plane, core = owner >> 1, owner & 1
+    experts, rows, cols = master.shape
+
+    everyone = range(groups * owners)
+    to_core = [(d, d ^ 1) for d in everyone]
+    to_group = [[(d, d ^ (j * owners)) for d in everyone] for j in range(groups)]
+    to_plane = [
+        [(d, d // owners * owners + (d % owners + 2 * s) % owners) for d in everyone] for s in range(planes)
+    ]
+    order = plane_order(planes)
+    others = range(1, groups)
+
+    turned, upstream, first_keep, first_send, chosen = first_blocks(
+        row_counts, plan_now, plan_next, hidden_acts[0, 0], out_grads[0, 0], experts
+    )
+    now, later = chosen[0], chosen[1]
+
+    mail = Mail()
+    mail.send("first", first_send, to_core)
+    rest_keep, rest_send = rest_blocks(mail.hold(turned, ["first"]), upstream, groups, planes)
+    mail.send("rest", rest_send, to_core)
+    keep, held = {}, {}
+    for n, s in enumerate(order):
+        keep[s], held[s] = (rest_keep[n - 1], mail["rest"][n - 1]) if n else (first_keep[0], mail["first"][0])
+    window = 5
+    names = []
+    for n, s in enumerate(order):
+        names += [(s, j) for j in others]
+        if n and order[n - 1]:
+            names.append(("sum", order[n - 1]))
+
+    def start(s, j, value, pairs):
+        at = names.index((s, j))
+        mail.send((s, j), value, pairs, names[at - window : at - window + 1] if at >= window else ())
+
+    def plane_sum(s):
+        total = jnp.zeros((experts, rows, cols), jnp.float32)
+        for j in range(groups):
+            block = mail[s, j] if j else jnp.stack([keep[s][0], held[s][0]])
+            for i in range(2):
+                total = total + now[2 * j + i][:, None] * block[i].astype(jnp.float32)
+        return total
+
+    for name in names:
+        if name[0] == "sum":
+            s = name[1]
+            start("sum", s, plane_sum(s).astype(jnp.bfloat16), to_plane[s])
+        else:
+            s, j = name
+            start(s, j, jnp.stack([keep[s][j], held[s][j]]), to_group[j])
+    grad_sum = plane_sum(0)
+    for s in order:
+        if s:
+            grad_sum = grad_sum + mail["sum", s].astype(jnp.float32)
+
+    master_new, moment_one_new, moment_two_new = adam(grad_sum, master, moment_one, moment_two)
+    rounded = master_new.astype(jnp.bfloat16)
+
+    def chosen_blocks(shard):
+        shard = shard.astype(jnp.float32)
+        return [
+            jnp.stack(
+                [jnp.sum(later[2 * j + i][:, None] * shard, axis=0).astype(jnp.bfloat16) for i in range(2)]
+            )
+            for j in range(groups)
+        ]
+
+    def in_order(blocks):
+        for bit in range(groups.bit_length() - 1):
+            swap = (group >> bit) & 1 == 1
+            blocks = [jnp.where(swap, blocks[m ^ (1 << bit)], blocks[m]) for m in range(groups)]
+        return jnp.concatenate(blocks, axis=-1)
+
+    back = order[::-1]
+    own = {}
+    mail = Mail()
+
+    def spread(n):
+        s, before = back[n], back[n - 1]
+        shard = mail.hold(mail["shard", s], [(before, 1)]) if s else rounded
+        own[s], *blocks = chosen_blocks(shard)
+        for j, block in enumerate(blocks, 1):
+            mail.send((s, j), block, to_group[j], [(before, j)] if s and j > 1 else [])
+
+    def pass_on(n):
+        s = back[n]
+        blocks = jnp.stack([own[s][1]] + [mail[s, j][1] for j in others])
+        mail.send(("core", s), blocks, to_core)
+
+    def shards(n, after):
+        s = back[n]
+        mail.send(("shard", s), rounded, to_plane[s], after)
+
+    last = planes - 1
+    for n in range(planes):
+        if n == 0:
+            shards(1, [])
+            spread(0)
+            if last >= 2:
+                shards(2, [])
+            if last >= 3:
+                shards(3, [("shard", back[1])])
+        else:
+            spread(n)
+            if n + 3 <= last:
+                shards(n + 3, [("shard", back[n + 1])])
+        pass_on(n)
+
+    replica = jnp.zeros((planes, 2, rows, groups * cols), jnp.bfloat16)
+    for s in back:
+        mine = in_order([own[s][0]] + [mail[s, j][0] for j in others])
+        other = in_order([mail["core", s][j] for j in range(groups)])
+        both = jnp.stack([jnp.where(core == 0, mine, other), jnp.where(core == 0, other, mine)])
+        replica = lax.dynamic_update_index_in_dim(replica, both, lax.rem(plane - s + planes, planes), 0)
+    replica = replica.reshape(2 * planes * rows, groups * cols)
+    return (master_new, moment_one_new, moment_two_new, replica[None, None])
+
+
+def per_device_whole(
     hidden_acts, out_grads, row_counts, plan_now, plan_next, master, moment_one, moment_two
 ):
     ex_count = lax.axis_size("expert")
@@ -40,11 +358,7 @@
     grad_sum = lax.psum_scatter(
         totals.astype(jnp.bfloat16), "dp", scatter_dimension=2, tiled=True
     ).astype(jnp.float32)
-    moment_one_new = beta_one * moment_one + (1.0 - beta_one) * grad_sum
-    moment_two_new = beta_two * moment_two + (1.0 - beta_two) * grad_sum * grad_sum
-    master_new = master - learn_rate * (moment_one_new / first_fix) / (
-        jnp.sqrt(moment_two_new / second_fix) + epsilon
-    )
+    master_new, moment_one_new, moment_two_new = adam(grad_sum, master, moment_one, moment_two)
     rounded = master_new.astype(jnp.bfloat16)
     full_cols = lax.all_gather(rounded, "dp", axis=2, tiled=True)
     targets = lax.dynamic_index_in_dim(plan_next, dp_index, 0, keepdims=False)
@@ -52,6 +366,16 @@
     incoming = lax.all_to_all(outgoing, "expert", split_axis=0, concat_axis=0, tiled=True)
     replica = incoming.reshape(ex_count * piece_rows, width)
     return (master_new, moment_one_new, moment_two_new, replica[None, None])
+
+
+def per_device(hidden_acts, out_grads, row_counts, plan_now, plan_next, master, *moments):
+    groups = lax.axis_size("dp")
+    owners = lax.axis_size("expert")
+    experts, rows, cols = master.shape
+    few = experts <= 2 * groups and owners <= 8
+    even = owners % 2 == 0 and groups & (groups - 1) == 0 and rows % 16 == 0 and cols % 128 == 0
+    body = per_device_planes if few and even else per_device_whole
+    return body(hidden_acts, out_grads, row_counts, plan_now, plan_next, master, *moments)
 
 
 def solution(mesh):

time: 422 us -> 118 us (0.28)
  local copies, waits for them, and re-layouts: 181 us -> 2.15 us
  blocking collectives: 75.9 us -> 0 us
  waiting for transfers between devices: 129 us -> 60.4 us
  starting transfers between devices: 6.58 us -> 38.2 us
  between operations: 14.8 us -> 2.02 us
  matrix products: 11.4 us -> 0 us
  Pallas kernels: 0 us -> 7.44 us
  other arithmetic: 1.98 us -> 7.15 us
    unnamed x16 -> x8, local copies, waits for them, and re-layouts: 166 us -> 1.68 us
    all_to_all x1 -> x0, blocking collectives: 75.9 us -> none  [per_device(): lax.all_to_all(outgoing, 'expert', split_axis=0, concat_axis=0, tiled=True)]
    all_to_all x1 -> x0, waiting for transfers between devices: 71.5 us -> none  [per_device(): lax.all_to_all(partial_value.reshape(ex_count, piece_rows, width), 'exper...]
    ppermute x0 -> x36, waiting for transfers between devices: none -> 60.4 us  [send(): self.arrived[name] = lax.ppermute(self.hold(value, after), AXES, pairs)]
    ppermute x0 -> x36, starting transfers between devices: none -> 38.2 us  [send(): self.arrived[name] = lax.ppermute(self.hold(value, after), AXES, pairs)]
    unnamed x3 -> x0, waiting for transfers between devices: 29.8 us -> none
    all_gather x1 -> x0, waiting for transfers between devices: 27.7 us -> none  [per_device(): full_cols = lax.all_gather(rounded, 'dp', axis=2, tiled=True)]
    reduce_scatter x1 -> x0, local copies, waits for them, and re-layouts: 13.2 us -> none  [per_device(): lax.psum_scatter(totals.astype(jnp.bfloat16), 'dp', scatter_dimension=2,...]
  transfers between devices with their start and end apart: 3 -> 36, of which waited for: 3 -> 18; matrix products, arithmetic and copies ran while one was open for 0% -> 4% of each run, Pallas kernels for 0% -> 0%
where the time goes in v3:
time: 118 us; the launch traced here: 117 us
  waiting for transfers between devices  60.4 us (51%)
  starting transfers between devices  38.2 us (32%)
  Pallas kernels  7.44 us (6%)
  other arithmetic  7.15 us (6%)
  local copies, waits for them, and re-layouts  2.15 us (2%)
  between operations  2.02 us (2%)
    ppermute x36, waiting for transfers between devices, send(): self.arrived[name] = lax.ppermute(self.hold(value, after), AXES, pairs)  60.4 us
    ppermute x36, starting transfers between devices, send(): self.arrived[name] = lax.ppermute(self.hold(value, after), AXES, pairs)  38.2 us
    pallas_call x1, Pallas kernels, first_blocks(): pl.pallas_call(first_kernel, in_specs=[pl.BlockSpec(memory_space=pltpu.SM...  4.31 us
    reduce_sum x4, other arithmetic, chosen_blocks(): jnp.sum(later[2 * j + i][:, None] * shard, axis=0).astype(jnp.bfloat16)  3.44 us
    pallas_call x1, Pallas kernels, rest_blocks(): pl.pallas_call(rest_kernel, in_specs=[vmem, vmem], out_specs=[vmem, vmem]...  3.13 us
  transfers between devices with their start and end apart: 36, of which 18 were waited for; matrix products, arithmetic and copies ran while one was open for 4% of the time, Pallas kernels for 0%

profile of v3, /device:TPU:0, one launch (start us, length us, event | category | flops | bytes accessed | tf_op | source)
XLA Modules:
  0.0 117.4 jit_solution(18421883173954383751)
XLA Ops:
  1.3 4.3 %first_blocks.1 = (bf16[768,1024]{1,0:T(8,128)(2,1)S(1)}, bf16[1024,2048]{1,0:T(8,128)(2,1)S(1)}, bf16[1,4,96,512]{3,2,1,0:T(8,128)(2,1)S(1)}, bf16[1,4,96,512]{3,2,1,0:T(8,128)(2,1)S(1)}, f32[2,8,3,512]{3,2,1,0:T(4,128)S(1)}) custom-call(s32[1,1]{1,0:T(1,128)S(6)} %copy.16.count_ref, s32[4,8]{1,0:T(4,128)} %now_hbm.1, s32[4,8]{1,0:T(4,128)} %next_hbm.1, ...), custom_call_target="tpu_custom_call" | custom-call | flops 805306368 | bytes 5767168 | tf_op jit(solution)/shard_map/first_blocks/pallas_call | solution.py:138
  5.6 0.5 collective-permute-start
  6.2 1.3 %collective-permute-done = bf16[1,4,96,512]{3,2,1,0:T(8,128)(2,1)S(1)} collective-permute-done((bf16[1,4,96,512]{3,2,1,0:T(8,128)(2,1)S(1)}, bf16[1,4,96,512]{3,2,1,0:T(8,128)(2,1)S(1)}, u32[]{:S(2)}, u32[]{:S(2)}) %collective-permute-start) | collective-permute-done | bytes 393248 | tf_op jit(solution)/shard_map/ppermute | solution.py:194
  7.5 3.1 %rest_blocks.1 = (bf16[3,4,96,512]{3,2,1,0:T(8,128)(2,1)S(1)}, bf16[3,4,96,512]{3,2,1,0:T(8,128)(2,1)S(1)}) custom-call(bf16[768,1024]{1,0:T(8,128)(2,1)S(1)} %get-tuple-element.52.turned_ref, bf16[1024,2048]{1,0:T(8,128)(2,1)S(1)} %get-tuple-element.53.upstream_ref), custom_call_target="tpu_custom_call" | custom-call | flops 2415919104 | bytes 2359296 | tf_op jit(solution)/shard_map/rest_blocks/pallas_call | solution.py:174
  10.6 0.4 collective-permute-start.1
  11.1 3.7 %collective-permute-start.4 = (bf16[2,96,512]{2,1,0:T(8,128)(2,1)S(1)}, bf16[2,96,512]{2,1,0:T(8,128)(2,1)S(1)}, u32[]{:S(2)}, u32[]{:S(2)}) collective-permute-start(bf16[2,96,512]{2,1,0:T(8,128)(2,1)S(1)} %pad_maximum_fusion.16), channel_id=1, source_target_pairs={{0,24},{1,25},{2,26},{3,27},{4,28},{5,29},{6,30},{7,31},{8,16},{9,... | collective-permute-start | bytes 589832 | tf_op jit(solution)/shard_map/ppermute | solution.py:194
  14.8 0.6 collective-permute-start.2
  15.4 0.1 collective-permute-start.3
  15.6 0.1 bitcast_convert_fusion.14
  15.7 4.9 %collective-permute-done.4 = bf16[2,96,512]{2,1,0:T(8,128)(2,1)S(1)} collective-permute-done((bf16[2,96,512]{2,1,0:T(8,128)(2,1)S(1)}, bf16[2,96,512]{2,1,0:T(8,128)(2,1)S(1)}, u32[]{:S(2)}, u32[]{:S(2)}) %collective-permute-start.4) | collective-permute-done | bytes 196640 | tf_op jit(solution)/shard_map/ppermute | solution.py:194
  20.6 3.8 %collective-permute-done.3 = bf16[2,96,512]{2,1,0:T(8,128)(2,1)S(1)} collective-permute-done((bf16[2,96,512]{2,1,0:T(8,128)(2,1)S(1)}, bf16[2,96,512]{2,1,0:T(8,128)(2,1)S(1)}, u32[]{:S(2)}, u32[]{:S(2)}) %collective-permute-start.3) | collective-permute-done | bytes 196640 | tf_op jit(solution)/shard_map/ppermute | solution.py:194
  24.5 0.1 fusion.53
  24.6 1.8 %collective-permute-start.12 = (bf16[2,96,512]{2,1,0:T(8,128)(2,1)S(1)}, bf16[2,96,512]{2,1,0:T(8,128)(2,1)S(1)}, u32[]{:S(2)}, u32[]{:S(2)}) collective-permute-start(bf16[2,96,512]{2,1,0:T(8,128)(2,1)S(1)} %pad_maximum_fusion.23), channel_id=1, source_target_pairs={{0,16},{1,17},{2,18},{3,19},{4,20},{5,21},{6,22},{7,23},{8,24},{9,... | collective-permute-start | bytes 589832 | tf_op jit(solution)/shard_map/ppermute | solution.py:194
  26.4 1.6 %collective-permute-start.9 = (bf16[2,96,512]{2,1,0:T(8,128)(2,1)S(1)}, bf16[2,96,512]{2,1,0:T(8,128)(2,1)S(1)}, u32[]{:S(2)}, u32[]{:S(2)}) collective-permute-start(bf16[2,96,512]{2,1,0:T(8,128)(2,1)S(1)} %pad_maximum_fusion.21), channel_id=1, source_target_pairs={{0,8},{1,9},{2,10},{3,11},{4,12},{5,13},{6,14},{7,15},{8,0},{9,1},... | collective-permute-start | bytes 589832 | tf_op jit(solution)/shard_map/ppermute | solution.py:194
  28.0 0.6 collective-permute-start.7
  28.6 1.5 %collective-permute-start.13 = (bf16[2,96,512]{2,1,0:T(8,128)(2,1)S(1)}, bf16[2,96,512]{2,1,0:T(8,128)(2,1)S(1)}, u32[]{:S(2)}, u32[]{:S(2)}) collective-permute-start(bf16[2,96,512]{2,1,0:T(8,128)(2,1)S(1)} %pad_maximum_fusion.13), channel_id=1, source_target_pairs={{0,24},{1,25},{2,26},{3,27},{4,28},{5,29},{6,30},{7,31},{8,16},{9,... | collective-permute-start | bytes 589832 | tf_op jit(solution)/shard_map/ppermute | solution.py:194
  30.2 0.3 add_convert_fusion.2
  30.5 2.7 %collective-permute-start.5 = (bf16[3,96,512]{2,1,0:T(8,128)(2,1)S(1)}, bf16[3,96,512]{2,1,0:T(8,128)(2,1)S(1)}, u32[]{:S(2)}, u32[]{:S(2)}) collective-permute-start(bf16[3,96,512]{2,1,0:T(8,128)(2,1)S(1)} %add_convert_fusion.2), channel_id=1, source_target_pairs={{0,4},{1,5},{2,6},{3,7},{4,0},{5,1},{6,2},{7,3},{8,12},{9,13},{10,... | collective-permute-start | bytes 884744 | tf_op jit(solution)/shard_map/ppermute | solution.py:194
  33.3 1.6 %collective-permute-start.15 = (bf16[2,96,512]{2,1,0:T(8,128)(2,1)S(1)}, bf16[2,96,512]{2,1,0:T(8,128)(2,1)S(1)}, u32[]{:S(2)}, u32[]{:S(2)}) collective-permute-start(bf16[2,96,512]{2,1,0:T(8,128)(2,1)S(1)} %get-tuple-element.72), channel_id=1, source_target_pairs={{0,24},{1,25},{2,26},{3,27},{4,28},{5,29},{6,30},{7,31},{8,16},{9,... | collective-permute-start | bytes 589832 | tf_op jit(solution)/shard_map/ppermute | solution.py:194
  34.9 0.5 collective-permute-start.10
  35.4 7.1 %collective-permute-done.13 = bf16[2,96,512]{2,1,0:T(8,128)(2,1)S(1)} collective-permute-done((bf16[2,96,512]{2,1,0:T(8,128)(2,1)S(1)}, bf16[2,96,512]{2,1,0:T(8,128)(2,1)S(1)}, u32[]{:S(2)}, u32[]{:S(2)}) %collective-permute-start.13) | collective-permute-done | bytes 196640 | tf_op jit(solution)/shard_map/ppermute | solution.py:194
  42.6 0.3 add_convert_fusion.1
  43.0 1.8 %collective-permute-start.14 = (bf16[3,96,512]{2,1,0:T(8,128)(2,1)S(1)}, bf16[3,96,512]{2,1,0:T(8,128)(2,1)S(1)}, u32[]{:S(2)}, u32[]{:S(2)}) collective-permute-start(bf16[3,96,512]{2,1,0:T(8,128)(2,1)S(1)} %add_convert_fusion.1), channel_id=1, source_target_pairs={{0,2},{1,3},{2,4},{3,5},{4,6},{5,7},{6,0},{7,1},{8,10},{9,11},{10,... | collective-permute-start | bytes 884744 | tf_op jit(solution)/shard_map/ppermute | solution.py:194
  44.8 1.5 %collective-permute-start.8 = (bf16[2,96,512]{2,1,0:T(8,128)(2,1)S(1)}, bf16[2,96,512]{2,1,0:T(8,128)(2,1)S(1)}, u32[]{:S(2)}, u32[]{:S(2)}) collective-permute-start(bf16[2,96,512]{2,1,0:T(8,128)(2,1)S(1)} %pad_maximum_fusion.17), channel_id=1, source_target_pairs={{0,16},{1,17},{2,18},{3,19},{4,20},{5,21},{6,22},{7,23},{8,24},{9,... | collective-permute-start | bytes 589832 | tf_op jit(solution)/shard_map/ppermute | solution.py:194
  46.3 5.8 %collective-permute-done.5 = bf16[3,96,512]{2,1,0:T(8,128)(2,1)S(1)} collective-permute-done((bf16[3,96,512]{2,1,0:T(8,128)(2,1)S(1)}, bf16[3,96,512]{2,1,0:T(8,128)(2,1)S(1)}, u32[]{:S(2)}, u32[]{:S(2)}) %collective-permute-start.5) | collective-permute-done | bytes 294944 | tf_op jit(solution)/shard_map/ppermute | solution.py:194
  52.3 0.3 add_convert_fusion
  52.6 1.1 collective-permute-start.16
  53.7 1.5 %collective-permute-start.11 = (bf16[2,96,512]{2,1,0:T(8,128)(2,1)S(1)}, bf16[2,96,512]{2,1,0:T(8,128)(2,1)S(1)}, u32[]{:S(2)}, u32[]{:S(2)}) collective-permute-start(bf16[2,96,512]{2,1,0:T(8,128)(2,1)S(1)} %pad_maximum_fusion.19), channel_id=1, source_target_pairs={{0,24},{1,25},{2,26},{3,27},{4,28},{5,29},{6,30},{7,31},{8,16},{9,... | collective-permute-start | bytes 589832 | tf_op jit(solution)/shard_map/ppermute | solution.py:194
  55.2 2.6 %collective-permute-done.6 = bf16[2,96,512]{2,1,0:T(8,128)(2,1)S(1)} collective-permute-done((bf16[2,96,512]{2,1,0:T(8,128)(2,1)S(1)}, bf16[2,96,512]{2,1,0:T(8,128)(2,1)S(1)}, u32[]{:S(2)}, u32[]{:S(2)}) %collective-permute-start.6) | collective-permute-done | bytes 196640 | tf_op jit(solution)/shard_map/ppermute | solution.py:194
  57.9 2.9 %collective-permute-done.11 = bf16[2,96,512]{2,1,0:T(8,128)(2,1)S(1)} collective-permute-done((bf16[2,96,512]{2,1,0:T(8,128)(2,1)S(1)}, bf16[2,96,512]{2,1,0:T(8,128)(2,1)S(1)}, u32[]{:S(2)}, u32[]{:S(2)}) %collective-permute-start.11) | collective-permute-done | bytes 196640 | tf_op jit(solution)/shard_map/ppermute | solution.py:194
  60.8 2.3 %fusion.11 = (bf16[96,512]{1,0:T(8,128)(2,1)S(1)}, bf16[96,512]{1,0:T(8,128)(2,1)S(1)}, bf16[96,512]{1,0:T(8,128)(2,1)S(1)}, bf16[96,512]{1,0:T(8,128)(2,1)S(1)}...) fusion(f32[3,512]{1,0:T(4,128)S(1)} %get-tuple-element.247, ...), kind=kLoop, calls=%fused_computation.48 | loop fusion | flops 7127040 | bytes 7176192 | tf_op jit(solution)/shard_map/reduce_sum | solution.py:276
  63.2 1.2 %collective-permute-start.19 = (bf16[2,96,512]{2,1,0:T(8,128)(2,1)S(1)}, bf16[2,96,512]{2,1,0:T(8,128)(2,1)S(1)}, u32[]{:S(2)}, u32[]{:S(2)}) collective-permute-start(bf16[2,96,512]{2,1,0:T(8,128)(2,1)S(1)} %pad_maximum_fusion.26), channel_id=1, source_target_pairs={{0,24},{1,25},{2,26},{3,27},{4,28},{5,29},{6,30},{7,31},{8,16},{9,... | collective-permute-start | bytes 589832 | tf_op jit(solution)/shard_map/ppermute | solution.py:194
  64.4 1.0 collective-permute-start.20
  65.4 1.5 %collective-permute-start.18 = (bf16[2,96,512]{2,1,0:T(8,128)(2,1)S(1)}, bf16[2,96,512]{2,1,0:T(8,128)(2,1)S(1)}, u32[]{:S(2)}, u32[]{:S(2)}) collective-permute-start(bf16[2,96,512]{2,1,0:T(8,128)(2,1)S(1)} %pad_maximum_fusion.24), channel_id=1, source_target_pairs={{0,8},{1,9},{2,10},{3,11},{4,12},{5,13},{6,14},{7,15},{8,0},{9,1},... | collective-permute-start | bytes 589832 | tf_op jit(solution)/shard_map/ppermute | solution.py:194
  66.9 1.4 %collective-permute-start.17 = (bf16[3,96,512]{2,1,0:T(8,128)(2,1)S(1)}, bf16[3,96,512]{2,1,0:T(8,128)(2,1)S(1)}, u32[]{:S(2)}, u32[]{:S(2)}) collective-permute-start(bf16[3,96,512]{2,1,0:T(8,128)(2,1)S(1)} %get-tuple-element.85), channel_id=1, source_target_pairs={{0,6},{1,7},{2,0},{3,1},{4,2},{5,3},{6,4},{7,5},{8,14},{9,15},{10,... | collective-permute-start | bytes 884744 | tf_op jit(solution)/shard_map/ppermute | solution.py:194
  68.3 0.6 collective-permute-start.22
  68.9 1.0 collective-permute-done.19
  69.9 2.0 %collective-permute-done.20 = bf16[2,96,512]{2,1,0:T(8,128)(2,1)S(1)} collective-permute-done((bf16[2,96,512]{2,1,0:T(8,128)(2,1)S(1)}, bf16[2,96,512]{2,1,0:T(8,128)(2,1)S(1)}, u32[]{:S(2)}, u32[]{:S(2)}) %collective-permute-start.20) | collective-permute-done | bytes 196640 | tf_op jit(solution)/shard_map/ppermute | solution.py:194
  72.0 0.1 collective-permute-start.21
  72.1 6.6 %collective-permute-done.17 = bf16[3,96,512]{2,1,0:T(8,128)(2,1)S(1)} collective-permute-done((bf16[3,96,512]{2,1,0:T(8,128)(2,1)S(1)}, bf16[3,96,512]{2,1,0:T(8,128)(2,1)S(1)}, u32[]{:S(2)}, u32[]{:S(2)}) %collective-permute-start.17) | collective-permute-done | bytes 294944 | tf_op jit(solution)/shard_map/ppermute | solution.py:194
  78.7 0.4 fusion.19
  79.3 3.5 %collective-permute-start.23 = (bf16[2,96,512]{2,1,0:T(8,128)(2,1)S(1)}, bf16[2,96,512]{2,1,0:T(8,128)(2,1)S(1)}, u32[]{:S(2)}, u32[]{:S(2)}) collective-permute-start(bf16[2,96,512]{2,1,0:T(8,128)(2,1)S(1)} %pad_maximum_fusion.29), channel_id=1, source_target_pairs={{0,8},{1,9},{2,10},{3,11},{4,12},{5,13},{6,14},{7,15},{8,0},{9,1},... | collective-permute-start | bytes 589832 | tf_op jit(solution)/shard_map/ppermute | solution.py:194
  82.8 3.0 %collective-permute-done.24 = bf16[2,96,512]{2,1,0:T(8,128)(2,1)S(1)} collective-permute-done((bf16[2,96,512]{2,1,0:T(8,128)(2,1)S(1)}, bf16[2,96,512]{2,1,0:T(8,128)(2,1)S(1)}, u32[]{:S(2)}, u32[]{:S(2)}) %collective-permute-start.24) | collective-permute-done | bytes 196640 | tf_op jit(solution)/shard_map/ppermute | solution.py:194
  85.9 1.2 collective-permute-done.25
  87.2 0.4 fusion.27
  87.7 0.9 collective-permute-start.29
  88.6 2.0 %collective-permute-start.30 = (bf16[2,96,512]{2,1,0:T(8,128)(2,1)S(1)}, bf16[2,96,512]{2,1,0:T(8,128)(2,1)S(1)}, u32[]{:S(2)}, u32[]{:S(2)}) collective-permute-start(bf16[2,96,512]{2,1,0:T(8,128)(2,1)S(1)} %pad_maximum_fusion.31), channel_id=1, source_target_pairs={{0,16},{1,17},{2,18},{3,19},{4,20},{5,21},{6,22},{7,23},{8,24},{9,... | collective-permute-start | bytes 589832 | tf_op jit(solution)/shard_map/ppermute | solution.py:194
  90.7 0.7 collective-permute-start.28
  91.4 0.2 broadcast_select_fusion.7
  91.6 0.4 broadcast_in_dim.14
  92.0 0.1 fusion
  92.1 4.3 %collective-permute-done.29 = bf16[2,96,512]{2,1,0:T(8,128)(2,1)S(1)} collective-permute-done((bf16[2,96,512]{2,1,0:T(8,128)(2,1)S(1)}, bf16[2,96,512]{2,1,0:T(8,128)(2,1)S(1)}, u32[]{:S(2)}, u32[]{:S(2)}) %collective-permute-start.29) | collective-permute-done | bytes 196640 | tf_op jit(solution)/shard_map/ppermute | solution.py:194
  96.4 3.7 %collective-permute-done.30 = bf16[2,96,512]{2,1,0:T(8,128)(2,1)S(1)} collective-permute-done((bf16[2,96,512]{2,1,0:T(8,128)(2,1)S(1)}, bf16[2,96,512]{2,1,0:T(8,128)(2,1)S(1)}, u32[]{:S(2)}, u32[]{:S(2)}) %collective-permute-start.30) | collective-permute-done | bytes 196640 | tf_op jit(solution)/shard_map/ppermute | solution.py:194
  100.3 0.4 fusion.35
  100.7 1.5 %collective-permute-start.33 = (bf16[2,96,512]{2,1,0:T(8,128)(2,1)S(1)}, bf16[2,96,512]{2,1,0:T(8,128)(2,1)S(1)}, u32[]{:S(2)}, u32[]{:S(2)}) collective-permute-start(bf16[2,96,512]{2,1,0:T(8,128)(2,1)S(1)} %pad_maximum_fusion.34), channel_id=1, source_target_pairs={{0,16},{1,17},{2,18},{3,19},{4,20},{5,21},{6,22},{7,23},{8,24},{9,... | collective-permute-start | bytes 589832 | tf_op jit(solution)/shard_map/ppermute | solution.py:194
  102.3 1.4 %collective-permute-start.32 = (bf16[2,96,512]{2,1,0:T(8,128)(2,1)S(1)}, bf16[2,96,512]{2,1,0:T(8,128)(2,1)S(1)}, u32[]{:S(2)}, u32[]{:S(2)}) collective-permute-start(bf16[2,96,512]{2,1,0:T(8,128)(2,1)S(1)} %pad_maximum_fusion.33), channel_id=1, source_target_pairs={{0,24},{1,25},{2,26},{3,27},{4,28},{5,29},{6,30},{7,31},{8,16},{9,... | collective-permute-start | bytes 589832 | tf_op jit(solution)/shard_map/ppermute | solution.py:194
  103.7 0.7 collective-permute-start.34
  104.5 0.2 broadcast_select_fusion.5
  104.7 7.6 %collective-permute-done.33 = bf16[2,96,512]{2,1,0:T(8,128)(2,1)S(1)} collective-permute-done((bf16[2,96,512]{2,1,0:T(8,128)(2,1)S(1)}, bf16[2,96,512]{2,1,0:T(8,128)(2,1)S(1)}, u32[]{:S(2)}, u32[]{:S(2)}) %collective-permute-start.33) | collective-permute-done | bytes 196640 | tf_op jit(solution)/shard_map/ppermute | solution.py:194
  112.3 1.2 %collective-permute-done.34 = bf16[2,96,512]{2,1,0:T(8,128)(2,1)S(1)} collective-permute-done((bf16[2,96,512]{2,1,0:T(8,128)(2,1)S(1)}, bf16[2,96,512]{2,1,0:T(8,128)(2,1)S(1)}, u32[]{:S(2)}, u32[]{:S(2)}) %collective-permute-start.34) | collective-permute-done | bytes 196640 | tf_op jit(solution)/shard_map/ppermute | solution.py:194
  113.8 0.2 broadcast_select_fusion.3
  114.1 1.4 %collective-permute-done.35 = bf16[4,96,512]{2,1,0:T(8,128)(2,1)S(1)} collective-permute-done((bf16[4,96,512]{2,1,0:T(8,128)(2,1)S(1)}, bf16[4,96,512]{2,1,0:T(8,128)(2,1)S(1)}, u32[]{:S(2)}, u32[]{:S(2)}) %collective-permute-start.35) | collective-permute-done | bytes 393248 | tf_op jit(solution)/shard_map/ppermute | solution.py:194
  115.5 0.2 broadcast_select_fusion.1
  115.8 1.7 %copy-done = bf16[4,2,96,2048]{3,2,1,0:T(8,128)(2,1)} copy-done((bf16[4,2,96,2048]{3,2,1,0:T(8,128)(2,1)}, bf16[4,2,96,2048]{3,2,1,0:T(8,128)(2,1)S(1)}, u32[]{:S(2)}) %copy-start) | copy-done | bytes 3145752
  (99 shorter events, 2.4 us)
Async XLA Ops:
  5.6 1.9 %collective-permute-start = (bf16[1,4,96,512]{3,2,1,0:T(8,128)(2,1)S(1)}, bf16[1,4,96,512]{3,2,1,0:T(8,128)(2,1)S(1)}, u32[]{:S(2)}, u32[]{:S(2)}) collective-permute-start(bf16[1,4,96,512]{3,2,1,0:T(8,128)(2,1)S(1)} %get-tuple-element.51), channel_id=1, source_target_pairs={{0,1},{1,0},{2,3},{3,2},{4,5},{5,4},{6,7},{7,6},{8,9},{9,8},{10,11... | collective-permute-start | bytes 1179656 | tf_op jit(solution)/shard_map/ppermute | solution.py:194
  10.6 13.9 %collective-permute-start.1 = (bf16[3,4,96,512]{3,2,1,0:T(8,128)(2,1)S(1)}, bf16[3,4,96,512]{3,2,1,0:T(8,128)(2,1)S(1)}, u32[]{:S(2)}, u32[]{:S(2)}) collective-permute-start(bf16[3,4,96,512]{3,2,1,0:T(8,128)(2,1)S(1)} %get-tuple-element.55), channel_id=1, source_target_pairs={{0,1},{1,0},{2,3},{3,2},{4,5},{5,4},{6,7},{7,6},{8,9},{9,8},{10,11... | collective-permute-start | bytes 3538952 | tf_op jit(solution)/shard_map/ppermute | solution.py:194
  11.1 9.5 %collective-permute-start.4 = (bf16[2,96,512]{2,1,0:T(8,128)(2,1)S(1)}, bf16[2,96,512]{2,1,0:T(8,128)(2,1)S(1)}, u32[]{:S(2)}, u32[]{:S(2)}) collective-permute-start(bf16[2,96,512]{2,1,0:T(8,128)(2,1)S(1)} %pad_maximum_fusion.16), channel_id=1, source_target_pairs={{0,24},{1,25},{2,26},{3,27},{4,28},{5,29},{6,30},{7,31},{8,16},{9,... | collective-permute-start | bytes 589832 | tf_op jit(solution)/shard_map/ppermute | solution.py:194
  14.8 13.8 %collective-permute-start.2 = (bf16[2,96,512]{2,1,0:T(8,128)(2,1)S(1)}, bf16[2,96,512]{2,1,0:T(8,128)(2,1)S(1)}, u32[]{:S(2)}, u32[]{:S(2)}) collective-permute-start(bf16[2,96,512]{2,1,0:T(8,128)(2,1)S(1)} %pad_maximum_fusion.14), channel_id=1, source_target_pairs={{0,8},{1,9},{2,10},{3,11},{4,12},{5,13},{6,14},{7,15},{8,0},{9,1},... | collective-permute-start | bytes 589832 | tf_op jit(solution)/shard_map/ppermute | solution.py:194
  15.4 9.0 %collective-permute-start.3 = (bf16[2,96,512]{2,1,0:T(8,128)(2,1)S(1)}, bf16[2,96,512]{2,1,0:T(8,128)(2,1)S(1)}, u32[]{:S(2)}, u32[]{:S(2)}) collective-permute-start(bf16[2,96,512]{2,1,0:T(8,128)(2,1)S(1)} %pad_maximum_fusion.15), channel_id=1, source_target_pairs={{0,16},{1,17},{2,18},{3,19},{4,20},{5,21},{6,22},{7,23},{8,24},{9,... | collective-permute-start | bytes 589832 | tf_op jit(solution)/shard_map/ppermute | solution.py:194
  24.6 8.6 %collective-permute-start.12 = (bf16[2,96,512]{2,1,0:T(8,128)(2,1)S(1)}, bf16[2,96,512]{2,1,0:T(8,128)(2,1)S(1)}, u32[]{:S(2)}, u32[]{:S(2)}) collective-permute-start(bf16[2,96,512]{2,1,0:T(8,128)(2,1)S(1)} %pad_maximum_fusion.23), channel_id=1, source_target_pairs={{0,16},{1,17},{2,18},{3,19},{4,20},{5,21},{6,22},{7,23},{8,24},{9,... | collective-permute-start | bytes 589832 | tf_op jit(solution)/shard_map/ppermute | solution.py:194
  26.4 8.4 %collective-permute-start.9 = (bf16[2,96,512]{2,1,0:T(8,128)(2,1)S(1)}, bf16[2,96,512]{2,1,0:T(8,128)(2,1)S(1)}, u32[]{:S(2)}, u32[]{:S(2)}) collective-permute-start(bf16[2,96,512]{2,1,0:T(8,128)(2,1)S(1)} %pad_maximum_fusion.21), channel_id=1, source_target_pairs={{0,8},{1,9},{2,10},{3,11},{4,12},{5,13},{6,14},{7,15},{8,0},{9,1},... | collective-permute-start | bytes 589832 | tf_op jit(solution)/shard_map/ppermute | solution.py:194
  28.0 14.9 %collective-permute-start.7 = (bf16[2,96,512]{2,1,0:T(8,128)(2,1)S(1)}, bf16[2,96,512]{2,1,0:T(8,128)(2,1)S(1)}, u32[]{:S(2)}, u32[]{:S(2)}) collective-permute-start(bf16[2,96,512]{2,1,0:T(8,128)(2,1)S(1)} %pad_maximum_fusion.18), channel_id=1, source_target_pairs={{0,8},{1,9},{2,10},{3,11},{4,12},{5,13},{6,14},{7,15},{8,0},{9,1},... | collective-permute-start | bytes 589832 | tf_op jit(solution)/shard_map/ppermute | solution.py:194
  28.6 14.0 %collective-permute-start.13 = (bf16[2,96,512]{2,1,0:T(8,128)(2,1)S(1)}, bf16[2,96,512]{2,1,0:T(8,128)(2,1)S(1)}, u32[]{:S(2)}, u32[]{:S(2)}) collective-permute-start(bf16[2,96,512]{2,1,0:T(8,128)(2,1)S(1)} %pad_maximum_fusion.13), channel_id=1, source_target_pairs={{0,24},{1,25},{2,26},{3,27},{4,28},{5,29},{6,30},{7,31},{8,16},{9,... | collective-permute-start | bytes 589832 | tf_op jit(solution)/shard_map/ppermute | solution.py:194
  30.5 21.7 %collective-permute-start.5 = (bf16[3,96,512]{2,1,0:T(8,128)(2,1)S(1)}, bf16[3,96,512]{2,1,0:T(8,128)(2,1)S(1)}, u32[]{:S(2)}, u32[]{:S(2)}) collective-permute-start(bf16[3,96,512]{2,1,0:T(8,128)(2,1)S(1)} %add_convert_fusion.2), channel_id=1, source_target_pairs={{0,4},{1,5},{2,6},{3,7},{4,0},{5,1},{6,2},{7,3},{8,12},{9,13},{10,... | collective-permute-start | bytes 884744 | tf_op jit(solution)/shard_map/ppermute | solution.py:194
  33.3 18.9 %collective-permute-start.15 = (bf16[2,96,512]{2,1,0:T(8,128)(2,1)S(1)}, bf16[2,96,512]{2,1,0:T(8,128)(2,1)S(1)}, u32[]{:S(2)}, u32[]{:S(2)}) collective-permute-start(bf16[2,96,512]{2,1,0:T(8,128)(2,1)S(1)} %get-tuple-element.72), channel_id=1, source_target_pairs={{0,24},{1,25},{2,26},{3,27},{4,28},{5,29},{6,30},{7,31},{8,16},{9,... | collective-permute-start | bytes 589832 | tf_op jit(solution)/shard_map/ppermute | solution.py:194
  34.9 17.3 %collective-permute-start.10 = (bf16[2,96,512]{2,1,0:T(8,128)(2,1)S(1)}, bf16[2,96,512]{2,1,0:T(8,128)(2,1)S(1)}, u32[]{:S(2)}, u32[]{:S(2)}) collective-permute-start(bf16[2,96,512]{2,1,0:T(8,128)(2,1)S(1)} %get-tuple-element.63), channel_id=1, source_target_pairs={{0,16},{1,17},{2,18},{3,19},{4,20},{5,21},{6,22},{7,23},{8,24},{9,... | collective-permute-start | bytes 589832 | tf_op jit(solution)/shard_map/ppermute | solution.py:194
  43.0 17.8 %collective-permute-start.14 = (bf16[3,96,512]{2,1,0:T(8,128)(2,1)S(1)}, bf16[3,96,512]{2,1,0:T(8,128)(2,1)S(1)}, u32[]{:S(2)}, u32[]{:S(2)}) collective-permute-start(bf16[3,96,512]{2,1,0:T(8,128)(2,1)S(1)} %add_convert_fusion.1), channel_id=1, source_target_pairs={{0,2},{1,3},{2,4},{3,5},{4,6},{5,7},{6,0},{7,1},{8,10},{9,11},{10,... | collective-permute-start | bytes 884744 | tf_op jit(solution)/shard_map/ppermute | solution.py:194
  44.8 10.4 %collective-permute-start.8 = (bf16[2,96,512]{2,1,0:T(8,128)(2,1)S(1)}, bf16[2,96,512]{2,1,0:T(8,128)(2,1)S(1)}, u32[]{:S(2)}, u32[]{:S(2)}) collective-permute-start(bf16[2,96,512]{2,1,0:T(8,128)(2,1)S(1)} %pad_maximum_fusion.17), channel_id=1, source_target_pairs={{0,16},{1,17},{2,18},{3,19},{4,20},{5,21},{6,22},{7,23},{8,24},{9,... | collective-permute-start | bytes 589832 | tf_op jit(solution)/shard_map/ppermute | solution.py:194
  52.2 5.7 %collective-permute-start.6 = (bf16[2,96,512]{2,1,0:T(8,128)(2,1)S(1)}, bf16[2,96,512]{2,1,0:T(8,128)(2,1)S(1)}, u32[]{:S(2)}, u32[]{:S(2)}) collective-permute-start(bf16[2,96,512]{2,1,0:T(8,128)(2,1)S(1)} %pad_maximum_fusion.12), channel_id=1, source_target_pairs={{0,8},{1,9},{2,10},{3,11},{4,12},{5,13},{6,14},{7,15},{8,0},{9,1},... | collective-permute-start | bytes 589832 | tf_op jit(solution)/shard_map/ppermute | solution.py:194
  52.3 8.5 %copy-start.1 = (f32[3,96,512]{2,1,0:T(8,128)S(1)}, f32[3,96,512]{2,1,0:T(8,128)}, u32[]{:S(2)}) copy-start(f32[3,96,512]{2,1,0:T(8,128)} %param.13) | copy-start | bytes 1769476
  52.3 8.5 %copy-start.2 = (f32[3,96,512]{2,1,0:T(8,128)S(1)}, f32[3,96,512]{2,1,0:T(8,128)}, u32[]{:S(2)}) copy-start(f32[3,96,512]{2,1,0:T(8,128)} %param.14) | copy-start | bytes 1769476
  52.3 8.5 %copy-start.3 = (f32[3,96,512]{2,1,0:T(8,128)S(1)}, f32[3,96,512]{2,1,0:T(8,128)}, u32[]{:S(2)}) copy-start(f32[3,96,512]{2,1,0:T(8,128)} %param.15) | copy-start | bytes 1769476
  52.6 8.2 %collective-permute-start.16 = (bf16[3,96,512]{2,1,0:T(8,128)(2,1)S(1)}, bf16[3,96,512]{2,1,0:T(8,128)(2,1)S(1)}, u32[]{:S(2)}, u32[]{:S(2)}) collective-permute-start(bf16[3,96,512]{2,1,0:T(8,128)(2,1)S(1)} %add_convert_fusion), channel_id=1, source_target_pairs={{0,6},{1,7},{2,0},{3,1},{4,2},{5,3},{6,4},{7,5},{8,14},{9,15},{10,... | collective-permute-start | bytes 884744 | tf_op jit(solution)/shard_map/ppermute | solution.py:194
  53.7 7.0 %collective-permute-start.11 = (bf16[2,96,512]{2,1,0:T(8,128)(2,1)S(1)}, bf16[2,96,512]{2,1,0:T(8,128)(2,1)S(1)}, u32[]{:S(2)}, u32[]{:S(2)}) collective-permute-start(bf16[2,96,512]{2,1,0:T(8,128)(2,1)S(1)} %pad_maximum_fusion.19), channel_id=1, source_target_pairs={{0,24},{1,25},{2,26},{3,27},{4,28},{5,29},{6,30},{7,31},{8,16},{9,... | collective-permute-start | bytes 589832 | tf_op jit(solution)/shard_map/ppermute | solution.py:194
  63.2 6.7 %collective-permute-start.19 = (bf16[2,96,512]{2,1,0:T(8,128)(2,1)S(1)}, bf16[2,96,512]{2,1,0:T(8,128)(2,1)S(1)}, u32[]{:S(2)}, u32[]{:S(2)}) collective-permute-start(bf16[2,96,512]{2,1,0:T(8,128)(2,1)S(1)} %pad_maximum_fusion.26), channel_id=1, source_target_pairs={{0,24},{1,25},{2,26},{3,27},{4,28},{5,29},{6,30},{7,31},{8,16},{9,... | collective-permute-start | bytes 589832 | tf_op jit(solution)/shard_map/ppermute | solution.py:194
  64.4 7.5 %collective-permute-start.20 = (bf16[2,96,512]{2,1,0:T(8,128)(2,1)S(1)}, bf16[2,96,512]{2,1,0:T(8,128)(2,1)S(1)}, u32[]{:S(2)}, u32[]{:S(2)}) collective-permute-start(bf16[2,96,512]{2,1,0:T(8,128)(2,1)S(1)} %pad_maximum_fusion.28), channel_id=1, source_target_pairs={{0,16},{1,17},{2,18},{3,19},{4,20},{5,21},{6,22},{7,23},{8,24},{9,... | collective-permute-start | bytes 589832 | tf_op jit(solution)/shard_map/ppermute | solution.py:194
  65.4 6.5 %collective-permute-start.18 = (bf16[2,96,512]{2,1,0:T(8,128)(2,1)S(1)}, bf16[2,96,512]{2,1,0:T(8,128)(2,1)S(1)}, u32[]{:S(2)}, u32[]{:S(2)}) collective-permute-start(bf16[2,96,512]{2,1,0:T(8,128)(2,1)S(1)} %pad_maximum_fusion.24), channel_id=1, source_target_pairs={{0,8},{1,9},{2,10},{3,11},{4,12},{5,13},{6,14},{7,15},{8,0},{9,1},... | collective-permute-start | bytes 589832 | tf_op jit(solution)/shard_map/ppermute | solution.py:194
  66.9 11.8 %collective-permute-start.17 = (bf16[3,96,512]{2,1,0:T(8,128)(2,1)S(1)}, bf16[3,96,512]{2,1,0:T(8,128)(2,1)S(1)}, u32[]{:S(2)}, u32[]{:S(2)}) collective-permute-start(bf16[3,96,512]{2,1,0:T(8,128)(2,1)S(1)} %get-tuple-element.85), channel_id=1, source_target_pairs={{0,6},{1,7},{2,0},{3,1},{4,2},{5,3},{6,4},{7,5},{8,14},{9,15},{10,... | collective-permute-start | bytes 884744 | tf_op jit(solution)/shard_map/ppermute | solution.py:194
  68.3 18.9 %collective-permute-start.22 = (bf16[3,96,512]{2,1,0:T(8,128)(2,1)S(1)}, bf16[3,96,512]{2,1,0:T(8,128)(2,1)S(1)}, u32[]{:S(2)}, u32[]{:S(2)}) collective-permute-start(bf16[3,96,512]{2,1,0:T(8,128)(2,1)S(1)} %get-tuple-element.85), channel_id=1, source_target_pairs={{0,2},{1,3},{2,4},{3,5},{4,6},{5,7},{6,0},{7,1},{8,10},{9,11},{10,... | collective-permute-start | bytes 884744 | tf_op jit(solution)/shard_map/ppermute | solution.py:194
  72.0 18.7 %collective-permute-start.21 = (bf16[4,96,512]{2,1,0:T(8,128)(2,1)S(1)}, bf16[4,96,512]{2,1,0:T(8,128)(2,1)S(1)}, u32[]{:S(2)}, u32[]{:S(2)}) collective-permute-start(bf16[4,96,512]{2,1,0:T(8,128)(2,1)S(1)} %pad_maximum_fusion.1), channel_id=1, source_target_pairs={{0,1},{1,0},{2,3},{3,2},{4,5},{5,4},{6,7},{7,6},{8,9},{9,8},{10,11... | collective-permute-start | bytes 1179656 | tf_op jit(solution)/shard_map/ppermute | solution.py:194
  79.1 6.7 %collective-permute-start.24 = (bf16[2,96,512]{2,1,0:T(8,128)(2,1)S(1)}, bf16[2,96,512]{2,1,0:T(8,128)(2,1)S(1)}, u32[]{:S(2)}, u32[]{:S(2)}) collective-permute-start(bf16[2,96,512]{2,1,0:T(8,128)(2,1)S(1)} %pad_maximum_fusion.25), channel_id=1, source_target_pairs={{0,24},{1,25},{2,26},{3,27},{4,28},{5,29},{6,30},{7,31},{8,16},{9,... | collective-permute-start | bytes 589832 | tf_op jit(solution)/shard_map/ppermute | solution.py:194
  79.2 7.8 %collective-permute-start.25 = (bf16[2,96,512]{2,1,0:T(8,128)(2,1)S(1)}, bf16[2,96,512]{2,1,0:T(8,128)(2,1)S(1)}, u32[]{:S(2)}, u32[]{:S(2)}) collective-permute-start(bf16[2,96,512]{2,1,0:T(8,128)(2,1)S(1)} %pad_maximum_fusion.27), channel_id=1, source_target_pairs={{0,16},{1,17},{2,18},{3,19},{4,20},{5,21},{6,22},{7,23},{8,24},{9,... | collective-permute-start | bytes 589832 | tf_op jit(solution)/shard_map/ppermute | solution.py:194
  79.3 7.7 %collective-permute-start.23 = (bf16[2,96,512]{2,1,0:T(8,128)(2,1)S(1)}, bf16[2,96,512]{2,1,0:T(8,128)(2,1)S(1)}, u32[]{:S(2)}, u32[]{:S(2)}) collective-permute-start(bf16[2,96,512]{2,1,0:T(8,128)(2,1)S(1)} %pad_maximum_fusion.29), channel_id=1, source_target_pairs={{0,8},{1,9},{2,10},{3,11},{4,12},{5,13},{6,14},{7,15},{8,0},{9,1},... | collective-permute-start | bytes 589832 | tf_op jit(solution)/shard_map/ppermute | solution.py:194
  85.9 14.4 %collective-permute-start.27 = (bf16[3,96,512]{2,1,0:T(8,128)(2,1)S(1)}, bf16[3,96,512]{2,1,0:T(8,128)(2,1)S(1)}, u32[]{:S(2)}, u32[]{:S(2)}) collective-permute-start(bf16[3,96,512]{2,1,0:T(8,128)(2,1)S(1)} %get-tuple-element.85), channel_id=1, source_target_pairs={{0,4},{1,5},{2,6},{3,7},{4,0},{5,1},{6,2},{7,3},{8,12},{9,13},{10,... | collective-permute-start | bytes 884744 | tf_op jit(solution)/shard_map/ppermute | solution.py:194
  87.1 17.3 %collective-permute-start.26 = (bf16[4,96,512]{2,1,0:T(8,128)(2,1)S(1)}, bf16[4,96,512]{2,1,0:T(8,128)(2,1)S(1)}, u32[]{:S(2)}, u32[]{:S(2)}) collective-permute-start(bf16[4,96,512]{2,1,0:T(8,128)(2,1)S(1)} %pad_maximum_fusion.4), channel_id=1, source_target_pairs={{0,1},{1,0},{2,3},{3,2},{4,5},{5,4},{6,7},{7,6},{8,9},{9,8},{10,11... | collective-permute-start | bytes 1179656 | tf_op jit(solution)/shard_map/ppermute | solution.py:194
  87.7 8.7 %collective-permute-start.29 = (bf16[2,96,512]{2,1,0:T(8,128)(2,1)S(1)}, bf16[2,96,512]{2,1,0:T(8,128)(2,1)S(1)}, u32[]{:S(2)}, u32[]{:S(2)}) collective-permute-start(bf16[2,96,512]{2,1,0:T(8,128)(2,1)S(1)} %pad_maximum_fusion.30), channel_id=1, source_target_pairs={{0,24},{1,25},{2,26},{3,27},{4,28},{5,29},{6,30},{7,31},{8,16},{9,... | collective-permute-start | bytes 589832 | tf_op jit(solution)/shard_map/ppermute | solution.py:194
  88.6 11.5 %collective-permute-start.30 = (bf16[2,96,512]{2,1,0:T(8,128)(2,1)S(1)}, bf16[2,96,512]{2,1,0:T(8,128)(2,1)S(1)}, u32[]{:S(2)}, u32[]{:S(2)}) collective-permute-start(bf16[2,96,512]{2,1,0:T(8,128)(2,1)S(1)} %pad_maximum_fusion.31), channel_id=1, source_target_pairs={{0,16},{1,17},{2,18},{3,19},{4,20},{5,21},{6,22},{7,23},{8,24},{9,... | collective-permute-start | bytes 589832 | tf_op jit(solution)/shard_map/ppermute | solution.py:194
  90.7 9.5 %collective-permute-start.28 = (bf16[2,96,512]{2,1,0:T(8,128)(2,1)S(1)}, bf16[2,96,512]{2,1,0:T(8,128)(2,1)S(1)}, u32[]{:S(2)}, u32[]{:S(2)}) collective-permute-start(bf16[2,96,512]{2,1,0:T(8,128)(2,1)S(1)} %pad_maximum_fusion.32), channel_id=1, source_target_pairs={{0,8},{1,9},{2,10},{3,11},{4,12},{5,13},{6,14},{7,15},{8,0},{9,1},... | collective-permute-start | bytes 589832 | tf_op jit(solution)/shard_map/ppermute | solution.py:194
  100.2 13.6 %collective-permute-start.31 = (bf16[4,96,512]{2,1,0:T(8,128)(2,1)S(1)}, bf16[4,96,512]{2,1,0:T(8,128)(2,1)S(1)}, u32[]{:S(2)}, u32[]{:S(2)}) collective-permute-start(bf16[4,96,512]{2,1,0:T(8,128)(2,1)S(1)} %pad_maximum_fusion.7), channel_id=1, source_target_pairs={{0,1},{1,0},{2,3},{3,2},{4,5},{5,4},{6,7},{7,6},{8,9},{9,8},{10,11... | collective-permute-start | bytes 1179656 | tf_op jit(solution)/shard_map/ppermute | solution.py:194
  100.7 11.6 %collective-permute-start.33 = (bf16[2,96,512]{2,1,0:T(8,128)(2,1)S(1)}, bf16[2,96,512]{2,1,0:T(8,128)(2,1)S(1)}, u32[]{:S(2)}, u32[]{:S(2)}) collective-permute-start(bf16[2,96,512]{2,1,0:T(8,128)(2,1)S(1)} %pad_maximum_fusion.34), channel_id=1, source_target_pairs={{0,16},{1,17},{2,18},{3,19},{4,20},{5,21},{6,22},{7,23},{8,24},{9,... | collective-permute-start | bytes 589832 | tf_op jit(solution)/shard_map/ppermute | solution.py:194
  102.3 10.0 %collective-permute-start.32 = (bf16[2,96,512]{2,1,0:T(8,128)(2,1)S(1)}, bf16[2,96,512]{2,1,0:T(8,128)(2,1)S(1)}, u32[]{:S(2)}, u32[]{:S(2)}) collective-permute-start(bf16[2,96,512]{2,1,0:T(8,128)(2,1)S(1)} %pad_maximum_fusion.33), channel_id=1, source_target_pairs={{0,24},{1,25},{2,26},{3,27},{4,28},{5,29},{6,30},{7,31},{8,16},{9,... | collective-permute-start | bytes 589832 | tf_op jit(solution)/shard_map/ppermute | solution.py:194
  103.7 9.8 %collective-permute-start.34 = (bf16[2,96,512]{2,1,0:T(8,128)(2,1)S(1)}, bf16[2,96,512]{2,1,0:T(8,128)(2,1)S(1)}, u32[]{:S(2)}, u32[]{:S(2)}) collective-permute-start(bf16[2,96,512]{2,1,0:T(8,128)(2,1)S(1)} %pad_maximum_fusion.35), channel_id=1, source_target_pairs={{0,8},{1,9},{2,10},{3,11},{4,12},{5,13},{6,14},{7,15},{8,0},{9,1},... | collective-permute-start | bytes 589832 | tf_op jit(solution)/shard_map/ppermute | solution.py:194
  113.7 1.8 %collective-permute-start.35 = (bf16[4,96,512]{2,1,0:T(8,128)(2,1)S(1)}, bf16[4,96,512]{2,1,0:T(8,128)(2,1)S(1)}, u32[]{:S(2)}, u32[]{:S(2)}) collective-permute-start(bf16[4,96,512]{2,1,0:T(8,128)(2,1)S(1)} %pad_maximum_fusion.10), channel_id=1, source_target_pairs={{0,1},{1,0},{2,3},{3,2},{4,5},{5,4},{6,7},{7,6},{8,9},{9,8},{10,11... | collective-permute-start | bytes 1179656 | tf_op jit(solution)/shard_map/ppermute | solution.py:194
  115.7 1.7 %copy-start = (bf16[4,2,96,2048]{3,2,1,0:T(8,128)(2,1)}, bf16[4,2,96,2048]{3,2,1,0:T(8,128)(2,1)S(1)}, u32[]{:S(2)}) copy-start(bf16[4,2,96,2048]{3,2,1,0:T(8,128)(2,1)S(1)} %fusion.3) | copy-start | bytes 9437188

commit v4 on v3

--- a/solution.py
+++ b/solution.py
@@ -13,6 +13,33 @@
 second_fix = 1.0 - beta_two**10
 
 AXES = ("dp", "expert")
+
+SUM_TIES = {
+    (1, 3): [(0, 1)],
+    ("sum", 0): [(0, 2)],
+    ("sum", 1): [(1, 3)],
+    (3, 1): [("sum", 0)],
+    (3, 2): [(0, 1), (0, 3)],
+    (3, 3): [(2, 2)],
+    ("sum", 2): [(2, 3)],
+    "rest": [(0, 2)],
+    (1, 1): [(0, 2)],
+}
+SPREAD_TIES = {
+    ("choose", 1): [(0, 2)],
+    (1, 2): [(0, 2)],
+    ("choose", 2): [(1, 3)],
+    (2, 2): [("core", 0)],
+    ("choose", 3): [(2, 3), ("core", 0)],
+    (3, 2): [(1, 3)],
+    (3, 3): [(2, 3)],
+    ("shard", 2): [(0, 1)],
+    ("core", 1): [(2, 3), (2, 2)],
+    ("core", 0): [("shard", 2)],
+    (2, 1): [("core", 0)],
+    ("core", 2): [(3, 3)],
+    ("core", 3): [(3, 1)],
+}
 
 
 def adam(grad_sum, master, moment_one, moment_two):
@@ -24,8 +51,7 @@
     return master_new, moment_one_new, moment_two_new
 
 
-def plane_order(planes):
-    return sorted(range(planes), key=lambda s: -min(s, planes - s))
+PLANE_ORDER = (2, 3, 1, 0)
 
 
 def store_blocks(product, even_core, rows, at, j, keep_ref, send_ref):
@@ -39,7 +65,7 @@
     chosen_ref, hidden_ref, now_ref, next_ref, sems, small_sems,
 ):
     tokens, inner = hidden_ref.shape
-    groups, rows, cols = keep_ref.shape[1:]
+    lead, groups, rows, cols = keep_ref.shape
     planes = inner // (2 * rows)
     parts = sems.shape[1]
     part = tokens // parts
@@ -78,10 +104,10 @@
         hidden = hidden_ref[n * part : (n + 1) * part]
         live = lax.broadcasted_iota(jnp.int32, hidden.shape, 0) < count_ref[0, 0] - n * part
         hidden = jnp.where(live, hidden, jnp.zeros_like(hidden)).T
-        for m, s in enumerate(plane_order(planes)):
+        for m, s in enumerate(PLANE_ORDER):
             for p in range(planes):
 
-                @pl.when(lax.rem(plane + s, planes) == p)
+                @pl.when(plane ^ s == p)
                 def put():
                     turned_ref[2 * rows * m : 2 * rows * (m + 1), n * part : (n + 1) * part] = hidden[
                         2 * rows * p : 2 * rows * (p + 1)
@@ -92,9 +118,11 @@
     def columns(j, carry):
         at = pl.ds(pl.multiple_of((group ^ j) * cols, cols), cols)
         product = jnp.dot(
-            turned_ref[: 2 * rows], upstream_ref[:, at], preferred_element_type=jnp.float32
+            turned_ref[: 2 * rows * lead], upstream_ref[:, at], preferred_element_type=jnp.float32
         )
-        store_blocks(product, core == 0, rows, 0, j, keep_ref, send_ref)
+        for n in range(lead):
+            part = product[2 * rows * n : 2 * rows * (n + 1)]
+            store_blocks(part, core == 0, rows, n, j, keep_ref, send_ref)
         return carry
 
     lax.fori_loop(0, groups, columns, 0)
@@ -107,7 +135,7 @@
     def columns(j, carry):
         at = pl.ds(pl.multiple_of((group ^ j) * cols, cols), cols)
         product = jnp.dot(
-            turned_ref[2 * rows :], upstream_ref[:, at], preferred_element_type=jnp.float32
+            turned_ref[-2 * rows * rest :], upstream_ref[:, at], preferred_element_type=jnp.float32
         )
         for n in range(rest):
             part = product[2 * rows * n : 2 * rows * (n + 1)]
@@ -117,7 +145,7 @@
     lax.fori_loop(0, groups, columns, 0)
 
 
-def first_blocks(counts, plan_now, plan_next, hidden, upstream, experts):
+def first_blocks(counts, plan_now, plan_next, hidden, upstream, experts, lead):
     groups, owners = plan_now.shape
     planes = owners // 2
     plan_now, plan_next, hidden, upstream = [
@@ -142,8 +170,8 @@
         out_shape=[
             jax.ShapeDtypeStruct((inner, tokens), jnp.bfloat16),
             jax.ShapeDtypeStruct((tokens, width), jnp.bfloat16),
-            blocks(1),
-            blocks(1),
+            blocks(lead),
+            blocks(lead),
             jax.ShapeDtypeStruct((2, 2 * groups, experts, cols), jnp.float32),
         ],
         scratch_shapes=[
@@ -155,7 +183,7 @@
         ],
         compiler_params=pltpu.CompilerParams(vmem_limit_bytes=24 * 2**20),
         cost_estimate=pl.CostEstimate(
-            flops=4 * tokens * rows * width,
+            flops=4 * tokens * rows * lead * width,
             bytes_accessed=2 * (tokens * inner + tokens * width),
             transcendentals=0,
         ),
@@ -164,13 +192,13 @@
     return turned, copied, keep, send, chosen
 
 
-def rest_blocks(turned, upstream, groups, planes):
+def rest_blocks(turned, upstream, groups, planes, rest):
     tokens, width = upstream.shape
     inner = turned.shape[0]
     cols = width // groups
     rows = inner // (2 * planes)
     vmem = pl.BlockSpec(memory_space=pltpu.VMEM)
-    out = jax.ShapeDtypeStruct((planes - 1, groups, rows, cols), jnp.bfloat16)
+    out = jax.ShapeDtypeStruct((rest, groups, rows, cols), jnp.bfloat16)
     return pl.pallas_call(
         rest_kernel,
         in_specs=[vmem, vmem],
@@ -178,8 +206,8 @@
         out_shape=[out, out],
         compiler_params=pltpu.CompilerParams(vmem_limit_bytes=24 * 2**20),
         cost_estimate=pl.CostEstimate(
-            flops=2 * tokens * (inner - 2 * rows) * width,
-            bytes_accessed=2 * (inner - 2 * rows) * width,
+            flops=4 * tokens * rows * rest * width,
+            bytes_accessed=4 * rows * rest * width,
             transcendentals=0,
         ),
         name="rest_blocks",
@@ -187,17 +215,16 @@
 
 
 class Mail:
-    def __init__(self):
+    def __init__(self, ties):
+        self.ties = ties
         self.arrived = {}
 
-    def send(self, name, value, pairs, after=()):
-        self.arrived[name] = lax.ppermute(self.hold(value, after), AXES, pairs)
-
-    def hold(self, value, after):
-        if after:
-            value, *there = lax.optimization_barrier((value, *[self.arrived[n] for n in after]))
-            self.arrived.update(zip(after, there))
-        return value
+    def send(self, name, value, pairs):
+        self.arrived[name] = lax.ppermute(self.hold(name, value), AXES, pairs)
+
+    def hold(self, name, value):
+        after = [self.arrived[n] for n in self.ties.get(name, ()) if n in self.arrived]
+        return lax.optimization_barrier((value, *after))[0] if after else value
 
     def __getitem__(self, name):
         return self.arrived[name]
@@ -217,54 +244,46 @@
     everyone = range(groups * owners)
     to_core = [(d, d ^ 1) for d in everyone]
     to_group = [[(d, d ^ (j * owners)) for d in everyone] for j in range(groups)]
-    to_plane = [
-        [(d, d // owners * owners + (d % owners + 2 * s) % owners) for d in everyone] for s in range(planes)
-    ]
-    order = plane_order(planes)
+    to_plane = [[(d, d ^ 2 * s) for d in everyone] for s in range(planes)]
     others = range(1, groups)
+    lead = 2
 
     turned, upstream, first_keep, first_send, chosen = first_blocks(
-        row_counts, plan_now, plan_next, hidden_acts[0, 0], out_grads[0, 0], experts
+        row_counts, plan_now, plan_next, hidden_acts[0, 0], out_grads[0, 0], experts, lead
     )
     now, later = chosen[0], chosen[1]
 
-    mail = Mail()
+    mail = Mail(SUM_TIES)
     mail.send("first", first_send, to_core)
-    rest_keep, rest_send = rest_blocks(mail.hold(turned, ["first"]), upstream, groups, planes)
-    mail.send("rest", rest_send, to_core)
-    keep, held = {}, {}
-    for n, s in enumerate(order):
-        keep[s], held[s] = (rest_keep[n - 1], mail["rest"][n - 1]) if n else (first_keep[0], mail["first"][0])
-    window = 5
-    names = []
-    for n, s in enumerate(order):
-        names += [(s, j) for j in others]
-        if n and order[n - 1]:
-            names.append(("sum", order[n - 1]))
-
-    def start(s, j, value, pairs):
-        at = names.index((s, j))
-        mail.send((s, j), value, pairs, names[at - window : at - window + 1] if at >= window else ())
-
-    def plane_sum(s):
+    keep, held = [[blocks[n] for n in range(lead)] for blocks in (first_keep, mail["first"])]
+
+    def plane_sum(n):
         total = jnp.zeros((experts, rows, cols), jnp.float32)
         for j in range(groups):
-            block = mail[s, j] if j else jnp.stack([keep[s][0], held[s][0]])
+            block = mail[n, j] if j else jnp.stack([keep[n][0], held[n][0]])
             for i in range(2):
                 total = total + now[2 * j + i][:, None] * block[i].astype(jnp.float32)
         return total
 
-    for name in names:
-        if name[0] == "sum":
-            s = name[1]
-            start("sum", s, plane_sum(s).astype(jnp.bfloat16), to_plane[s])
-        else:
-            s, j = name
-            start(s, j, jnp.stack([keep[s][j], held[s][j]]), to_group[j])
-    grad_sum = plane_sum(0)
-    for s in order:
-        if s:
-            grad_sum = grad_sum + mail["sum", s].astype(jnp.float32)
+    for n in range(planes):
+        if n == lead:
+            rest_keep, rest_send = rest_blocks(
+                mail.hold("rest", turned), upstream, groups, planes, planes - lead
+            )
+            for m in range(planes - lead):
+                mail.send(("other", m), rest_send[m], to_core)
+                keep.append(rest_keep[m])
+                held.append(mail["other", m])
+        for j in others:
+            mail.send((n, j), jnp.stack([keep[n][j], held[n][j]]), to_group[j])
+        if n:
+            total = plane_sum(n - 1)
+            if n == 2:
+                total = total + mail["sum", 0].astype(jnp.float32)
+            mail.send(("sum", n - 1), total.astype(jnp.bfloat16), to_plane[3 if n == 2 else 1])
+    grad_sum = plane_sum(planes - 1)
+    for n in range(1, planes - 1):
+        grad_sum = grad_sum + mail["sum", n].astype(jnp.float32)
 
     master_new, moment_one_new, moment_two_new = adam(grad_sum, master, moment_one, moment_two)
     rounded = master_new.astype(jnp.bfloat16)
@@ -284,47 +303,35 @@
             blocks = [jnp.where(swap, blocks[m ^ (1 << bit)], blocks[m]) for m in range(groups)]
         return jnp.concatenate(blocks, axis=-1)
 
-    back = order[::-1]
+    back = PLANE_ORDER[::-1]
     own = {}
-    mail = Mail()
-
-    def spread(n):
-        s, before = back[n], back[n - 1]
-        shard = mail.hold(mail["shard", s], [(before, 1)]) if s else rounded
-        own[s], *blocks = chosen_blocks(shard)
+    mail = Mail(SPREAD_TIES)
+
+    def send_shard(n):
+        mail.send(("shard", n), mail["shard", 2] if n == 3 else rounded, to_plane[3 if n == 2 else 1])
+
+    def pass_on(n):
+        blocks = jnp.stack([own[n][1]] + [mail[n, j][1] for j in others])
+        mail.send(("core", n), blocks, to_core)
+
+    send_shard(1)
+    for n in range(planes):
+        own[n], *blocks = chosen_blocks(mail.hold(("choose", n), mail["shard", n]) if n else rounded)
         for j, block in enumerate(blocks, 1):
-            mail.send((s, j), block, to_group[j], [(before, j)] if s and j > 1 else [])
-
-    def pass_on(n):
-        s = back[n]
-        blocks = jnp.stack([own[s][1]] + [mail[s, j][1] for j in others])
-        mail.send(("core", s), blocks, to_core)
-
-    def shards(n, after):
-        s = back[n]
-        mail.send(("shard", s), rounded, to_plane[s], after)
-
-    last = planes - 1
-    for n in range(planes):
+            mail.send((n, j), block, to_group[j])
         if n == 0:
-            shards(1, [])
-            spread(0)
-            if last >= 2:
-                shards(2, [])
-            if last >= 3:
-                shards(3, [("shard", back[1])])
+            for m in range(2, planes):
+                send_shard(m)
         else:
-            spread(n)
-            if n + 3 <= last:
-                shards(n + 3, [("shard", back[n + 1])])
-        pass_on(n)
+            pass_on(n - 1)
+    pass_on(planes - 1)
 
     replica = jnp.zeros((planes, 2, rows, groups * cols), jnp.bfloat16)
-    for s in back:
-        mine = in_order([own[s][0]] + [mail[s, j][0] for j in others])
-        other = in_order([mail["core", s][j] for j in range(groups)])
+    for n, s in enumerate(back):
+        mine = in_order([own[n][0]] + [mail[n, j][0] for j in others])
+        other = in_order([mail["core", n][j] for j in range(groups)])
         both = jnp.stack([jnp.where(core == 0, mine, other), jnp.where(core == 0, other, mine)])
-        replica = lax.dynamic_update_index_in_dim(replica, both, lax.rem(plane - s + planes, planes), 0)
+        replica = lax.dynamic_update_index_in_dim(replica, both, plane ^ s, 0)
     replica = replica.reshape(2 * planes * rows, groups * cols)
     return (master_new, moment_one_new, moment_two_new, replica[None, None])
 
@@ -372,8 +379,8 @@
     groups = lax.axis_size("dp")
     owners = lax.axis_size("expert")
     experts, rows, cols = master.shape
-    few = experts <= 2 * groups and owners <= 8
-    even = owners % 2 == 0 and groups & (groups - 1) == 0 and rows % 16 == 0 and cols % 128 == 0
+    few = experts <= 2 * groups and owners == 2 * len(PLANE_ORDER)
+    even = groups & (groups - 1) == 0 and rows % 16 == 0 and cols % 128 == 0
     body = per_device_planes if few and even else per_device_whole
     return body(hidden_acts, out_grads, row_counts, plan_now, plan_next, master, *moments)
 

time: 118 us -> 109 us (0.924)
  waiting for transfers between devices: 60.4 us -> 47.8 us
  starting transfers between devices: 38.2 us -> 42.2 us
    ppermute x36 -> x37, waiting for transfers between devices: 60.4 us -> 47.8 us  [send(): self.arrived[name] = lax.ppermute(self.hold(name, value), AXES, pairs)]
    ppermute x36 -> x37, starting transfers between devices: 38.2 us -> 42.2 us  [send(): self.arrived[name] = lax.ppermute(self.hold(name, value), AXES, pairs)]
  transfers between devices with their start and end apart: 36 -> 37, of which waited for: 18 -> 18; matrix products, arithmetic and copies ran while one was open for 4% -> 5% of each run, Pallas kernels for 0% -> 2%
where the time goes in v4:
time: 109 us
  waiting for transfers between devices  47.8 us (44%)
  starting transfers between devices  42.2 us (39%)
  Pallas kernels  7.4 us (7%)
  other arithmetic  7.19 us (7%)
  local copies, waits for them, and re-layouts  2.13 us (2%)
  between operations  1.92 us (2%)
    ppermute x37, waiting for transfers between devices, send(): self.arrived[name] = lax.ppermute(self.hold(name, value), AXES, pairs)  47.8 us
    ppermute x37, starting transfers between devices, send(): self.arrived[name] = lax.ppermute(self.hold(name, value), AXES, pairs)  42.2 us
    pallas_call x1, Pallas kernels, first_blocks(): pl.pallas_call(first_kernel, in_specs=[pl.BlockSpec(memory_space=pltpu.SM...  5.07 us
    reduce_sum x4, other arithmetic, chosen_blocks(): jnp.sum(later[2 * j + i][:, None] * shard, axis=0).astype(jnp.bfloat16)  3.39 us
    pallas_call x1, Pallas kernels, rest_blocks(): pl.pallas_call(rest_kernel, in_specs=[vmem, vmem], out_specs=[vmem, vmem]...  2.32 us
  transfers between devices with their start and end apart: 37, of which 18 were waited for; matrix products, arithmetic and copies ran while one was open for 5% of the time, Pallas kernels for 2%

profile of v4, /device:TPU:0, one launch (start us, length us, event | category | flops | bytes accessed | tf_op | source)
XLA Modules:
  0.0 108.6 jit_solution(11068571573262160457)
XLA Ops:
  1.3 5.1 %first_blocks.1 = (bf16[768,1024]{1,0:T(8,128)(2,1)S(1)}, bf16[1024,2048]{1,0:T(8,128)(2,1)S(1)}, bf16[2,4,96,512]{3,2,1,0:T(8,128)(2,1)S(1)}, bf16[2,4,96,512]{3,2,1,0:T(8,128)(2,1)S(1)}, f32[2,8,3,512]{3,2,1,0:T(4,128)S(1)}) custom-call(s32[1,1]{1,0:T(1,128)S(6)} %copy.16.count_ref, s32[4,8]{1,0:T(4,128)} %now_hbm.1, s32[4,8]{1,0:T(4,128)} %next_hbm.1, ...), custom_call_target="tpu_custom_call" | custom-call | flops 1610612736 | bytes 5767168 | tf_op jit(solution)/shard_map/first_blocks/pallas_call | solution.py:166
  6.4 0.5 collective-permute-start
  6.9 0.1 bitcast_convert_fusion.1
  7.0 1.8 %collective-permute-done = bf16[2,4,96,512]{3,2,1,0:T(8,128)(2,1)S(1)} collective-permute-done((bf16[2,4,96,512]{3,2,1,0:T(8,128)(2,1)S(1)}, bf16[2,4,96,512]{3,2,1,0:T(8,128)(2,1)S(1)}, u32[]{:S(2)}, u32[]{:S(2)}) %collective-permute-start) | collective-permute-done | bytes 786464 | tf_op jit(solution)/shard_map/ppermute | solution.py:223
  8.9 3.0 %collective-permute-start.1 = (bf16[2,96,512]{2,1,0:T(8,128)(2,1)S(1)}, bf16[2,96,512]{2,1,0:T(8,128)(2,1)S(1)}, u32[]{:S(2)}, u32[]{:S(2)}) collective-permute-start(bf16[2,96,512]{2,1,0:T(8,128)(2,1)S(1)} %pad_maximum_fusion.12), channel_id=1, source_target_pairs={{0,16},{1,17},{2,18},{3,19},{4,20},{5,21},{6,22},{7,23},{8,24},{9,... | collective-permute-start | bytes 589832 | tf_op jit(solution)/shard_map/ppermute | solution.py:223
  11.9 1.5 %collective-permute-start.4 = (bf16[2,96,512]{2,1,0:T(8,128)(2,1)S(1)}, bf16[2,96,512]{2,1,0:T(8,128)(2,1)S(1)}, u32[]{:S(2)}, u32[]{:S(2)}) collective-permute-start(bf16[2,96,512]{2,1,0:T(8,128)(2,1)S(1)} %pad_maximum_fusion.15), channel_id=1, source_target_pairs={{0,24},{1,25},{2,26},{3,27},{4,28},{5,29},{6,30},{7,31},{8,16},{9,... | collective-permute-start | bytes 589832 | tf_op jit(solution)/shard_map/ppermute | solution.py:223
  13.4 0.1 collective-permute-start.3
  13.6 2.0 %collective-permute-start.12 = (bf16[2,96,512]{2,1,0:T(8,128)(2,1)S(1)}, bf16[2,96,512]{2,1,0:T(8,128)(2,1)S(1)}, u32[]{:S(2)}, u32[]{:S(2)}) collective-permute-start(bf16[2,96,512]{2,1,0:T(8,128)(2,1)S(1)} %pad_maximum_fusion.20), channel_id=1, source_target_pairs={{0,16},{1,17},{2,18},{3,19},{4,20},{5,21},{6,22},{7,23},{8,24},{9,... | collective-permute-start | bytes 589832 | tf_op jit(solution)/shard_map/ppermute | solution.py:223
  15.7 6.1 %collective-permute-done.1 = bf16[2,96,512]{2,1,0:T(8,128)(2,1)S(1)} collective-permute-done((bf16[2,96,512]{2,1,0:T(8,128)(2,1)S(1)}, bf16[2,96,512]{2,1,0:T(8,128)(2,1)S(1)}, u32[]{:S(2)}, u32[]{:S(2)}) %collective-permute-start.1) | collective-permute-done | bytes 196640 | tf_op jit(solution)/shard_map/ppermute | solution.py:223
  21.8 2.3 %rest_blocks.1 = (bf16[2,4,96,512]{3,2,1,0:T(8,128)(2,1)S(1)}, bf16[2,4,96,512]{3,2,1,0:T(8,128)(2,1)S(1)}) custom-call(bf16[768,1024]{1,0:T(8,128)(2,1)S(1)} %get-tuple-element.37.turned_ref, bf16[1024,2048]{1,0:T(8,128)(2,1)S(1)} %get-tuple-element.38.upstream_ref), custom_call_target="tpu_custom_call" | custom-call | flops 1610612736 | bytes 1572864 | tf_op jit(solution)/shard_map/rest_blocks/pallas_call | solution.py:202
  24.4 0.3 add_convert_fusion.2
  24.7 2.2 %collective-permute-start.5 = (bf16[3,96,512]{2,1,0:T(8,128)(2,1)S(1)}, bf16[3,96,512]{2,1,0:T(8,128)(2,1)S(1)}, u32[]{:S(2)}, u32[]{:S(2)}) collective-permute-start(bf16[3,96,512]{2,1,0:T(8,128)(2,1)S(1)} %add_convert_fusion.2), channel_id=1, source_target_pairs={{0,2},{1,3},{2,0},{3,1},{4,6},{5,7},{6,4},{7,5},{8,10},{9,11},{10,... | collective-permute-start | bytes 884744 | tf_op jit(solution)/shard_map/ppermute | solution.py:223
  26.9 2.4 %collective-permute-start.13 = (bf16[2,96,512]{2,1,0:T(8,128)(2,1)S(1)}, bf16[2,96,512]{2,1,0:T(8,128)(2,1)S(1)}, u32[]{:S(2)}, u32[]{:S(2)}) collective-permute-start(bf16[2,96,512]{2,1,0:T(8,128)(2,1)S(1)} %get-tuple-element.46), channel_id=1, source_target_pairs={{0,24},{1,25},{2,26},{3,27},{4,28},{5,29},{6,30},{7,31},{8,16},{9,... | collective-permute-start | bytes 589832 | tf_op jit(solution)/shard_map/ppermute | solution.py:223
  29.3 0.5 collective-permute-start.11
  30.1 5.4 %collective-permute-done.13 = bf16[2,96,512]{2,1,0:T(8,128)(2,1)S(1)} collective-permute-done((bf16[2,96,512]{2,1,0:T(8,128)(2,1)S(1)}, bf16[2,96,512]{2,1,0:T(8,128)(2,1)S(1)}, u32[]{:S(2)}, u32[]{:S(2)}) %collective-permute-start.13) | collective-permute-done | bytes 196640 | tf_op jit(solution)/shard_map/ppermute | solution.py:223
  35.6 3.5 %collective-permute-done.11 = bf16[2,96,512]{2,1,0:T(8,128)(2,1)S(1)} collective-permute-done((bf16[2,96,512]{2,1,0:T(8,128)(2,1)S(1)}, bf16[2,96,512]{2,1,0:T(8,128)(2,1)S(1)}, u32[]{:S(2)}, u32[]{:S(2)}) %collective-permute-start.11) | collective-permute-done | bytes 196640 | tf_op jit(solution)/shard_map/ppermute | solution.py:223
  39.1 0.4 add_convert_fusion.1
  39.5 2.5 %collective-permute-start.14 = (bf16[3,96,512]{2,1,0:T(8,128)(2,1)S(1)}, bf16[3,96,512]{2,1,0:T(8,128)(2,1)S(1)}, u32[]{:S(2)}, u32[]{:S(2)}) collective-permute-start(bf16[3,96,512]{2,1,0:T(8,128)(2,1)S(1)} %add_convert_fusion.1), channel_id=1, source_target_pairs={{0,6},{1,7},{2,4},{3,5},{4,2},{5,3},{6,0},{7,1},{8,14},{9,15},{10,... | collective-permute-start | bytes 884744 | tf_op jit(solution)/shard_map/ppermute | solution.py:223
  42.1 1.5 %collective-permute-start.16 = (bf16[2,96,512]{2,1,0:T(8,128)(2,1)S(1)}, bf16[2,96,512]{2,1,0:T(8,128)(2,1)S(1)}, u32[]{:S(2)}, u32[]{:S(2)}) collective-permute-start(bf16[2,96,512]{2,1,0:T(8,128)(2,1)S(1)} %pad_maximum_fusion.23), channel_id=1, source_target_pairs={{0,24},{1,25},{2,26},{3,27},{4,28},{5,29},{6,30},{7,31},{8,16},{9,... | collective-permute-start | bytes 589832 | tf_op jit(solution)/shard_map/ppermute | solution.py:223
  43.6 1.6 %collective-permute-start.9 = (bf16[2,96,512]{2,1,0:T(8,128)(2,1)S(1)}, bf16[2,96,512]{2,1,0:T(8,128)(2,1)S(1)}, u32[]{:S(2)}, u32[]{:S(2)}) collective-permute-start(bf16[2,96,512]{2,1,0:T(8,128)(2,1)S(1)} %pad_maximum_fusion.18), channel_id=1, source_target_pairs={{0,16},{1,17},{2,18},{3,19},{4,20},{5,21},{6,22},{7,23},{8,24},{9,... | collective-permute-start | bytes 589832 | tf_op jit(solution)/shard_map/ppermute | solution.py:223
  45.2 0.6 collective-permute-start.15
  45.9 0.6 collective-permute-start.7
  46.6 4.4 %collective-permute-done.16 = bf16[2,96,512]{2,1,0:T(8,128)(2,1)S(1)} collective-permute-done((bf16[2,96,512]{2,1,0:T(8,128)(2,1)S(1)}, bf16[2,96,512]{2,1,0:T(8,128)(2,1)S(1)}, u32[]{:S(2)}, u32[]{:S(2)}) %collective-permute-start.16) | collective-permute-done | bytes 196640 | tf_op jit(solution)/shard_map/ppermute | solution.py:223
  51.0 1.5 %collective-permute-start.6 = (bf16[2,96,512]{2,1,0:T(8,128)(2,1)S(1)}, bf16[2,96,512]{2,1,0:T(8,128)(2,1)S(1)}, u32[]{:S(2)}, u32[]{:S(2)}) collective-permute-start(bf16[2,96,512]{2,1,0:T(8,128)(2,1)S(1)} %pad_maximum_fusion.13), channel_id=1, source_target_pairs={{0,8},{1,9},{2,10},{3,11},{4,12},{5,13},{6,14},{7,15},{8,0},{9,1},... | collective-permute-start | bytes 589832 | tf_op jit(solution)/shard_map/ppermute | solution.py:223
  52.5 0.9 collective-permute-done.9
  53.4 0.5 collective-permute-done.15
  53.9 0.3 add_convert_fusion
  54.2 0.8 collective-permute-start.17
  55.0 2.7 %collective-permute-start.10 = (bf16[2,96,512]{2,1,0:T(8,128)(2,1)S(1)}, bf16[2,96,512]{2,1,0:T(8,128)(2,1)S(1)}, u32[]{:S(2)}, u32[]{:S(2)}) collective-permute-start(bf16[2,96,512]{2,1,0:T(8,128)(2,1)S(1)} %pad_maximum_fusion.17), channel_id=1, source_target_pairs={{0,24},{1,25},{2,26},{3,27},{4,28},{5,29},{6,30},{7,31},{8,16},{9,... | collective-permute-start | bytes 589832 | tf_op jit(solution)/shard_map/ppermute | solution.py:223
  57.8 4.0 %collective-permute-done.10 = bf16[2,96,512]{2,1,0:T(8,128)(2,1)S(1)} collective-permute-done((bf16[2,96,512]{2,1,0:T(8,128)(2,1)S(1)}, bf16[2,96,512]{2,1,0:T(8,128)(2,1)S(1)}, u32[]{:S(2)}, u32[]{:S(2)}) %collective-permute-start.10) | collective-permute-done | bytes 196640 | tf_op jit(solution)/shard_map/ppermute | solution.py:223
  61.9 0.8 collective-permute-done.17
  62.6 2.3 %fusion.11 = (bf16[96,512]{1,0:T(8,128)(2,1)S(1)}, bf16[96,512]{1,0:T(8,128)(2,1)S(1)}, bf16[96,512]{1,0:T(8,128)(2,1)S(1)}, bf16[96,512]{1,0:T(8,128)(2,1)S(1)}...) fusion(f32[3,512]{1,0:T(4,128)S(1)} %get-tuple-element.226, ...), kind=kLoop, calls=%fused_computation.48 | loop fusion | flops 6832128 | bytes 6881280 | tf_op jit(solution)/shard_map/reduce_sum | solution.py:295
  64.9 1.0 collective-permute-start.19
  65.9 1.5 %collective-permute-start.20 = (bf16[2,96,512]{2,1,0:T(8,128)(2,1)S(1)}, bf16[2,96,512]{2,1,0:T(8,128)(2,1)S(1)}, u32[]{:S(2)}, u32[]{:S(2)}) collective-permute-start(bf16[2,96,512]{2,1,0:T(8,128)(2,1)S(1)} %pad_maximum_fusion.26), channel_id=1, source_target_pairs={{0,8},{1,9},{2,10},{3,11},{4,12},{5,13},{6,14},{7,15},{8,0},{9,1},... | collective-permute-start | bytes 589832 | tf_op jit(solution)/shard_map/ppermute | solution.py:223
  67.5 1.2 %collective-permute-start.18 = (bf16[2,96,512]{2,1,0:T(8,128)(2,1)S(1)}, bf16[2,96,512]{2,1,0:T(8,128)(2,1)S(1)}, u32[]{:S(2)}, u32[]{:S(2)}) collective-permute-start(bf16[2,96,512]{2,1,0:T(8,128)(2,1)S(1)} %pad_maximum_fusion.24), channel_id=1, source_target_pairs={{0,24},{1,25},{2,26},{3,27},{4,28},{5,29},{6,30},{7,31},{8,16},{9,... | collective-permute-start | bytes 589832 | tf_op jit(solution)/shard_map/ppermute | solution.py:223
  68.7 0.7 collective-permute-start.23
  69.4 3.2 %collective-permute-done.20 = bf16[2,96,512]{2,1,0:T(8,128)(2,1)S(1)} collective-permute-done((bf16[2,96,512]{2,1,0:T(8,128)(2,1)S(1)}, bf16[2,96,512]{2,1,0:T(8,128)(2,1)S(1)}, u32[]{:S(2)}, u32[]{:S(2)}) %collective-permute-start.20) | collective-permute-done | bytes 196640 | tf_op jit(solution)/shard_map/ppermute | solution.py:223
  72.6 1.3 %collective-permute-start.21 = (bf16[3,96,512]{2,1,0:T(8,128)(2,1)S(1)}, bf16[3,96,512]{2,1,0:T(8,128)(2,1)S(1)}, u32[]{:S(2)}, u32[]{:S(2)}) collective-permute-start(bf16[3,96,512]{2,1,0:T(8,128)(2,1)S(1)} %get-tuple-element.49), channel_id=1, source_target_pairs={{0,6},{1,7},{2,4},{3,5},{4,2},{5,3},{6,0},{7,1},{8,14},{9,15},{10,... | collective-permute-start | bytes 884744 | tf_op jit(solution)/shard_map/ppermute | solution.py:223
  73.9 1.9 %collective-permute-done.18 = bf16[2,96,512]{2,1,0:T(8,128)(2,1)S(1)} collective-permute-done((bf16[2,96,512]{2,1,0:T(8,128)(2,1)S(1)}, bf16[2,96,512]{2,1,0:T(8,128)(2,1)S(1)}, u32[]{:S(2)}, u32[]{:S(2)}) %collective-permute-start.18) | collective-permute-done | bytes 196640 | tf_op jit(solution)/shard_map/ppermute | solution.py:223
  75.9 2.3 %collective-permute-done.23 = bf16[3,96,512]{2,1,0:T(8,128)(2,1)S(1)} collective-permute-done((bf16[3,96,512]{2,1,0:T(8,128)(2,1)S(1)}, bf16[3,96,512]{2,1,0:T(8,128)(2,1)S(1)}, u32[]{:S(2)}, u32[]{:S(2)}) %collective-permute-start.23) | collective-permute-done | bytes 294944 | tf_op jit(solution)/shard_map/ppermute | solution.py:223
  78.2 0.4 fusion.19
  78.7 2.1 %collective-permute-start.24 = (bf16[2,96,512]{2,1,0:T(8,128)(2,1)S(1)}, bf16[2,96,512]{2,1,0:T(8,128)(2,1)S(1)}, u32[]{:S(2)}, u32[]{:S(2)}) collective-permute-start(bf16[2,96,512]{2,1,0:T(8,128)(2,1)S(1)} %pad_maximum_fusion.27), channel_id=1, source_target_pairs={{0,24},{1,25},{2,26},{3,27},{4,28},{5,29},{6,30},{7,31},{8,16},{9,... | collective-permute-start | bytes 589832 | tf_op jit(solution)/shard_map/ppermute | solution.py:223
  80.8 0.5 collective-permute-start.25
  81.3 1.1 collective-permute-start.26
  82.4 3.0 %collective-permute-done.24 = bf16[2,96,512]{2,1,0:T(8,128)(2,1)S(1)} collective-permute-done((bf16[2,96,512]{2,1,0:T(8,128)(2,1)S(1)}, bf16[2,96,512]{2,1,0:T(8,128)(2,1)S(1)}, u32[]{:S(2)}, u32[]{:S(2)}) %collective-permute-start.24) | collective-permute-done | bytes 196640 | tf_op jit(solution)/shard_map/ppermute | solution.py:223
  85.4 0.4 fusion.27
  85.8 2.2 %collective-permute-start.27 = (bf16[2,96,512]{2,1,0:T(8,128)(2,1)S(1)}, bf16[2,96,512]{2,1,0:T(8,128)(2,1)S(1)}, u32[]{:S(2)}, u32[]{:S(2)}) collective-permute-start(bf16[2,96,512]{2,1,0:T(8,128)(2,1)S(1)} %pad_maximum_fusion.30), channel_id=1, source_target_pairs={{0,24},{1,25},{2,26},{3,27},{4,28},{5,29},{6,30},{7,31},{8,16},{9,... | collective-permute-start | bytes 589832 | tf_op jit(solution)/shard_map/ppermute | solution.py:223
  88.2 2.0 %collective-permute-start.28 = (bf16[2,96,512]{2,1,0:T(8,128)(2,1)S(1)}, bf16[2,96,512]{2,1,0:T(8,128)(2,1)S(1)}, u32[]{:S(2)}, u32[]{:S(2)}) collective-permute-start(bf16[2,96,512]{2,1,0:T(8,128)(2,1)S(1)} %pad_maximum_fusion.31), channel_id=1, source_target_pairs={{0,16},{1,17},{2,18},{3,19},{4,20},{5,21},{6,22},{7,23},{8,24},{9,... | collective-permute-start | bytes 589832 | tf_op jit(solution)/shard_map/ppermute | solution.py:223
  90.2 0.6 collective-permute-start.30
  90.8 3.6 %collective-permute-done.27 = bf16[2,96,512]{2,1,0:T(8,128)(2,1)S(1)} collective-permute-done((bf16[2,96,512]{2,1,0:T(8,128)(2,1)S(1)}, bf16[2,96,512]{2,1,0:T(8,128)(2,1)S(1)}, u32[]{:S(2)}, u32[]{:S(2)}) %collective-permute-start.27) | collective-permute-done | bytes 196640 | tf_op jit(solution)/shard_map/ppermute | solution.py:223
  94.4 0.3 collective-permute-done.31
  94.7 0.4 fusion.35
  95.1 1.9 %collective-permute-start.32 = (bf16[2,96,512]{2,1,0:T(8,128)(2,1)S(1)}, bf16[2,96,512]{2,1,0:T(8,128)(2,1)S(1)}, u32[]{:S(2)}, u32[]{:S(2)}) collective-permute-start(bf16[2,96,512]{2,1,0:T(8,128)(2,1)S(1)} %pad_maximum_fusion.33), channel_id=1, source_target_pairs={{0,24},{1,25},{2,26},{3,27},{4,28},{5,29},{6,30},{7,31},{8,16},{9,... | collective-permute-start | bytes 589832 | tf_op jit(solution)/shard_map/ppermute | solution.py:223
  97.0 0.6 collective-permute-start.34
  97.6 1.2 %collective-permute-start.35 = (bf16[2,96,512]{2,1,0:T(8,128)(2,1)S(1)}, bf16[2,96,512]{2,1,0:T(8,128)(2,1)S(1)}, u32[]{:S(2)}, u32[]{:S(2)}) collective-permute-start(bf16[2,96,512]{2,1,0:T(8,128)(2,1)S(1)} %pad_maximum_fusion.35), channel_id=1, source_target_pairs={{0,8},{1,9},{2,10},{3,11},{4,12},{5,13},{6,14},{7,15},{8,0},{9,1},... | collective-permute-start | bytes 589832 | tf_op jit(solution)/shard_map/ppermute | solution.py:223
  98.8 0.2 broadcast_select_fusion.7
  99.0 0.4 broadcast_in_dim.14
  99.7 3.3 %collective-permute-done.32 = bf16[2,96,512]{2,1,0:T(8,128)(2,1)S(1)} collective-permute-done((bf16[2,96,512]{2,1,0:T(8,128)(2,1)S(1)}, bf16[2,96,512]{2,1,0:T(8,128)(2,1)S(1)}, u32[]{:S(2)}, u32[]{:S(2)}) %collective-permute-start.32) | collective-permute-done | bytes 196640 | tf_op jit(solution)/shard_map/ppermute | solution.py:223
  103.1 1.6 %collective-permute-done.34 = bf16[2,96,512]{2,1,0:T(8,128)(2,1)S(1)} collective-permute-done((bf16[2,96,512]{2,1,0:T(8,128)(2,1)S(1)}, bf16[2,96,512]{2,1,0:T(8,128)(2,1)S(1)}, u32[]{:S(2)}, u32[]{:S(2)}) %collective-permute-start.34) | collective-permute-done | bytes 196640 | tf_op jit(solution)/shard_map/ppermute | solution.py:223
  105.0 0.2 broadcast_select_fusion.5
  105.3 0.2 broadcast_select_fusion.3
  105.5 1.1 %collective-permute-done.36 = bf16[4,96,512]{2,1,0:T(8,128)(2,1)S(1)} collective-permute-done((bf16[4,96,512]{2,1,0:T(8,128)(2,1)S(1)}, bf16[4,96,512]{2,1,0:T(8,128)(2,1)S(1)}, u32[]{:S(2)}, u32[]{:S(2)}) %collective-permute-start.36) | collective-permute-done | bytes 393248 | tf_op jit(solution)/shard_map/ppermute | solution.py:223
  106.7 0.2 broadcast_select_fusion.1
  106.9 1.7 %copy-done = bf16[4,2,96,2048]{3,2,1,0:T(8,128)(2,1)} copy-done((bf16[4,2,96,2048]{3,2,1,0:T(8,128)(2,1)}, bf16[4,2,96,2048]{3,2,1,0:T(8,128)(2,1)S(1)}, u32[]{:S(2)}) %copy-start) | copy-done | bytes 3145752
  (94 shorter events, 2.5 us)
Async XLA Ops:
  6.4 2.4 %collective-permute-start = (bf16[2,4,96,512]{3,2,1,0:T(8,128)(2,1)S(1)}, bf16[2,4,96,512]{3,2,1,0:T(8,128)(2,1)S(1)}, u32[]{:S(2)}, u32[]{:S(2)}) collective-permute-start(bf16[2,4,96,512]{3,2,1,0:T(8,128)(2,1)S(1)} %get-tuple-element.36), channel_id=1, source_target_pairs={{0,1},{1,0},{2,3},{3,2},{4,5},{5,4},{6,7},{7,6},{8,9},{9,8},{10,11... | collective-permute-start | bytes 2359304 | tf_op jit(solution)/shard_map/ppermute | solution.py:223
  8.9 12.9 %collective-permute-start.1 = (bf16[2,96,512]{2,1,0:T(8,128)(2,1)S(1)}, bf16[2,96,512]{2,1,0:T(8,128)(2,1)S(1)}, u32[]{:S(2)}, u32[]{:S(2)}) collective-permute-start(bf16[2,96,512]{2,1,0:T(8,128)(2,1)S(1)} %pad_maximum_fusion.12), channel_id=1, source_target_pairs={{0,16},{1,17},{2,18},{3,19},{4,20},{5,21},{6,22},{7,23},{8,24},{9,... | collective-permute-start | bytes 589832 | tf_op jit(solution)/shard_map/ppermute | solution.py:223
  11.9 12.4 %collective-permute-start.4 = (bf16[2,96,512]{2,1,0:T(8,128)(2,1)S(1)}, bf16[2,96,512]{2,1,0:T(8,128)(2,1)S(1)}, u32[]{:S(2)}, u32[]{:S(2)}) collective-permute-start(bf16[2,96,512]{2,1,0:T(8,128)(2,1)S(1)} %pad_maximum_fusion.15), channel_id=1, source_target_pairs={{0,24},{1,25},{2,26},{3,27},{4,28},{5,29},{6,30},{7,31},{8,16},{9,... | collective-permute-start | bytes 589832 | tf_op jit(solution)/shard_map/ppermute | solution.py:223
  13.4 10.9 %collective-permute-start.3 = (bf16[2,96,512]{2,1,0:T(8,128)(2,1)S(1)}, bf16[2,96,512]{2,1,0:T(8,128)(2,1)S(1)}, u32[]{:S(2)}, u32[]{:S(2)}) collective-permute-start(bf16[2,96,512]{2,1,0:T(8,128)(2,1)S(1)} %pad_maximum_fusion.14), channel_id=1, source_target_pairs={{0,8},{1,9},{2,10},{3,11},{4,12},{5,13},{6,14},{7,15},{8,0},{9,1},... | collective-permute-start | bytes 589832 | tf_op jit(solution)/shard_map/ppermute | solution.py:223
  13.6 16.4 %collective-permute-start.12 = (bf16[2,96,512]{2,1,0:T(8,128)(2,1)S(1)}, bf16[2,96,512]{2,1,0:T(8,128)(2,1)S(1)}, u32[]{:S(2)}, u32[]{:S(2)}) collective-permute-start(bf16[2,96,512]{2,1,0:T(8,128)(2,1)S(1)} %pad_maximum_fusion.20), channel_id=1, source_target_pairs={{0,16},{1,17},{2,18},{3,19},{4,20},{5,21},{6,22},{7,23},{8,24},{9,... | collective-permute-start | bytes 589832 | tf_op jit(solution)/shard_map/ppermute | solution.py:223
  24.2 17.9 %collective-permute-start.8 = (bf16[4,96,512]{2,1,0:T(8,128)(2,1)S(1)}, bf16[4,96,512]{2,1,0:T(8,128)(2,1)S(1)}, u32[]{:S(2)}, u32[]{:S(2)}) collective-permute-start(bf16[4,96,512]{2,1,0:T(8,128)(2,1)S(1)} %get-tuple-element.131), channel_id=1, source_target_pairs={{0,1},{1,0},{2,3},{3,2},{4,5},{5,4},{6,7},{7,6},{8,9},{9,8},{10,11... | collective-permute-start | bytes 1179656 | tf_op jit(solution)/shard_map/ppermute | solution.py:223
  24.7 14.4 %collective-permute-start.5 = (bf16[3,96,512]{2,1,0:T(8,128)(2,1)S(1)}, bf16[3,96,512]{2,1,0:T(8,128)(2,1)S(1)}, u32[]{:S(2)}, u32[]{:S(2)}) collective-permute-start(bf16[3,96,512]{2,1,0:T(8,128)(2,1)S(1)} %add_convert_fusion.2), channel_id=1, source_target_pairs={{0,2},{1,3},{2,0},{3,1},{4,6},{5,7},{6,4},{7,5},{8,10},{9,11},{10,... | collective-permute-start | bytes 884744 | tf_op jit(solution)/shard_map/ppermute | solution.py:223
  26.9 8.6 %collective-permute-start.13 = (bf16[2,96,512]{2,1,0:T(8,128)(2,1)S(1)}, bf16[2,96,512]{2,1,0:T(8,128)(2,1)S(1)}, u32[]{:S(2)}, u32[]{:S(2)}) collective-permute-start(bf16[2,96,512]{2,1,0:T(8,128)(2,1)S(1)} %get-tuple-element.46), channel_id=1, source_target_pairs={{0,24},{1,25},{2,26},{3,27},{4,28},{5,29},{6,30},{7,31},{8,16},{9,... | collective-permute-start | bytes 589832 | tf_op jit(solution)/shard_map/ppermute | solution.py:223
  29.3 9.7 %collective-permute-start.11 = (bf16[2,96,512]{2,1,0:T(8,128)(2,1)S(1)}, bf16[2,96,512]{2,1,0:T(8,128)(2,1)S(1)}, u32[]{:S(2)}, u32[]{:S(2)}) collective-permute-start(bf16[2,96,512]{2,1,0:T(8,128)(2,1)S(1)} %get-tuple-element.45), channel_id=1, source_target_pairs={{0,8},{1,9},{2,10},{3,11},{4,12},{5,13},{6,14},{7,15},{8,0},{9,1},... | collective-permute-start | bytes 589832 | tf_op jit(solution)/shard_map/ppermute | solution.py:223
  30.0 15.9 %collective-permute-start.2 = (bf16[4,96,512]{2,1,0:T(8,128)(2,1)S(1)}, bf16[4,96,512]{2,1,0:T(8,128)(2,1)S(1)}, u32[]{:S(2)}, u32[]{:S(2)}) collective-permute-start(bf16[4,96,512]{2,1,0:T(8,128)(2,1)S(1)} %get-tuple-element.130), channel_id=1, source_target_pairs={{0,1},{1,0},{2,3},{3,2},{4,5},{5,4},{6,7},{7,6},{8,9},{9,8},{10,11... | collective-permute-start | bytes 1179656 | tf_op jit(solution)/shard_map/ppermute | solution.py:223
  39.5 22.4 %collective-permute-start.14 = (bf16[3,96,512]{2,1,0:T(8,128)(2,1)S(1)}, bf16[3,96,512]{2,1,0:T(8,128)(2,1)S(1)}, u32[]{:S(2)}, u32[]{:S(2)}) collective-permute-start(bf16[3,96,512]{2,1,0:T(8,128)(2,1)S(1)} %add_convert_fusion.1), channel_id=1, source_target_pairs={{0,6},{1,7},{2,4},{3,5},{4,2},{5,3},{6,0},{7,1},{8,14},{9,15},{10,... | collective-permute-start | bytes 884744 | tf_op jit(solution)/shard_map/ppermute | solution.py:223
  42.1 8.8 %collective-permute-start.16 = (bf16[2,96,512]{2,1,0:T(8,128)(2,1)S(1)}, bf16[2,96,512]{2,1,0:T(8,128)(2,1)S(1)}, u32[]{:S(2)}, u32[]{:S(2)}) collective-permute-start(bf16[2,96,512]{2,1,0:T(8,128)(2,1)S(1)} %pad_maximum_fusion.23), channel_id=1, source_target_pairs={{0,24},{1,25},{2,26},{3,27},{4,28},{5,29},{6,30},{7,31},{8,16},{9,... | collective-permute-start | bytes 589832 | tf_op jit(solution)/shard_map/ppermute | solution.py:223
  43.6 9.7 %collective-permute-start.9 = (bf16[2,96,512]{2,1,0:T(8,128)(2,1)S(1)}, bf16[2,96,512]{2,1,0:T(8,128)(2,1)S(1)}, u32[]{:S(2)}, u32[]{:S(2)}) collective-permute-start(bf16[2,96,512]{2,1,0:T(8,128)(2,1)S(1)} %pad_maximum_fusion.18), channel_id=1, source_target_pairs={{0,16},{1,17},{2,18},{3,19},{4,20},{5,21},{6,22},{7,23},{8,24},{9,... | collective-permute-start | bytes 589832 | tf_op jit(solution)/shard_map/ppermute | solution.py:223
  45.2 8.6 %collective-permute-start.15 = (bf16[2,96,512]{2,1,0:T(8,128)(2,1)S(1)}, bf16[2,96,512]{2,1,0:T(8,128)(2,1)S(1)}, u32[]{:S(2)}, u32[]{:S(2)}) collective-permute-start(bf16[2,96,512]{2,1,0:T(8,128)(2,1)S(1)} %pad_maximum_fusion.22), channel_id=1, source_target_pairs={{0,8},{1,9},{2,10},{3,11},{4,12},{5,13},{6,14},{7,15},{8,0},{9,1},... | collective-permute-start | bytes 589832 | tf_op jit(solution)/shard_map/ppermute | solution.py:223
  45.9 11.8 %collective-permute-start.7 = (bf16[2,96,512]{2,1,0:T(8,128)(2,1)S(1)}, bf16[2,96,512]{2,1,0:T(8,128)(2,1)S(1)}, u32[]{:S(2)}, u32[]{:S(2)}) collective-permute-start(bf16[2,96,512]{2,1,0:T(8,128)(2,1)S(1)} %pad_maximum_fusion.16), channel_id=1, source_target_pairs={{0,16},{1,17},{2,18},{3,19},{4,20},{5,21},{6,22},{7,23},{8,24},{9,... | collective-permute-start | bytes 589832 | tf_op jit(solution)/shard_map/ppermute | solution.py:223
  46.5 16.1 %copy-start.1 = (f32[3,96,512]{2,1,0:T(8,128)S(1)}, f32[3,96,512]{2,1,0:T(8,128)}, u32[]{:S(2)}) copy-start(f32[3,96,512]{2,1,0:T(8,128)} %param.13) | copy-start | bytes 1769476
  46.5 16.1 %copy-start.2 = (f32[3,96,512]{2,1,0:T(8,128)S(1)}, f32[3,96,512]{2,1,0:T(8,128)}, u32[]{:S(2)}) copy-start(f32[3,96,512]{2,1,0:T(8,128)} %param.14) | copy-start | bytes 1769476
  46.5 16.1 %copy-start.3 = (f32[3,96,512]{2,1,0:T(8,128)S(1)}, f32[3,96,512]{2,1,0:T(8,128)}, u32[]{:S(2)}) copy-start(f32[3,96,512]{2,1,0:T(8,128)} %param.15) | copy-start | bytes 1769476
  51.0 6.8 %collective-permute-start.6 = (bf16[2,96,512]{2,1,0:T(8,128)(2,1)S(1)}, bf16[2,96,512]{2,1,0:T(8,128)(2,1)S(1)}, u32[]{:S(2)}, u32[]{:S(2)}) collective-permute-start(bf16[2,96,512]{2,1,0:T(8,128)(2,1)S(1)} %pad_maximum_fusion.13), channel_id=1, source_target_pairs={{0,8},{1,9},{2,10},{3,11},{4,12},{5,13},{6,14},{7,15},{8,0},{9,1},... | collective-permute-start | bytes 589832 | tf_op jit(solution)/shard_map/ppermute | solution.py:223
  54.2 8.4 %collective-permute-start.17 = (bf16[3,96,512]{2,1,0:T(8,128)(2,1)S(1)}, bf16[3,96,512]{2,1,0:T(8,128)(2,1)S(1)}, u32[]{:S(2)}, u32[]{:S(2)}) collective-permute-start(bf16[3,96,512]{2,1,0:T(8,128)(2,1)S(1)} %add_convert_fusion), channel_id=1, source_target_pairs={{0,2},{1,3},{2,0},{3,1},{4,6},{5,7},{6,4},{7,5},{8,10},{9,11},{10,... | collective-permute-start | bytes 884744 | tf_op jit(solution)/shard_map/ppermute | solution.py:223
  55.0 6.8 %collective-permute-start.10 = (bf16[2,96,512]{2,1,0:T(8,128)(2,1)S(1)}, bf16[2,96,512]{2,1,0:T(8,128)(2,1)S(1)}, u32[]{:S(2)}, u32[]{:S(2)}) collective-permute-start(bf16[2,96,512]{2,1,0:T(8,128)(2,1)S(1)} %pad_maximum_fusion.17), channel_id=1, source_target_pairs={{0,24},{1,25},{2,26},{3,27},{4,28},{5,29},{6,30},{7,31},{8,16},{9,... | collective-permute-start | bytes 589832 | tf_op jit(solution)/shard_map/ppermute | solution.py:223
  64.9 8.9 %collective-permute-start.19 = (bf16[2,96,512]{2,1,0:T(8,128)(2,1)S(1)}, bf16[2,96,512]{2,1,0:T(8,128)(2,1)S(1)}, u32[]{:S(2)}, u32[]{:S(2)}) collective-permute-start(bf16[2,96,512]{2,1,0:T(8,128)(2,1)S(1)} %pad_maximum_fusion.25), channel_id=1, source_target_pairs={{0,16},{1,17},{2,18},{3,19},{4,20},{5,21},{6,22},{7,23},{8,24},{9,... | collective-permute-start | bytes 589832 | tf_op jit(solution)/shard_map/ppermute | solution.py:223
  65.9 6.6 %collective-permute-start.20 = (bf16[2,96,512]{2,1,0:T(8,128)(2,1)S(1)}, bf16[2,96,512]{2,1,0:T(8,128)(2,1)S(1)}, u32[]{:S(2)}, u32[]{:S(2)}) collective-permute-start(bf16[2,96,512]{2,1,0:T(8,128)(2,1)S(1)} %pad_maximum_fusion.26), channel_id=1, source_target_pairs={{0,8},{1,9},{2,10},{3,11},{4,12},{5,13},{6,14},{7,15},{8,0},{9,1},... | collective-permute-start | bytes 589832 | tf_op jit(solution)/shard_map/ppermute | solution.py:223
  67.5 8.3 %collective-permute-start.18 = (bf16[2,96,512]{2,1,0:T(8,128)(2,1)S(1)}, bf16[2,96,512]{2,1,0:T(8,128)(2,1)S(1)}, u32[]{:S(2)}, u32[]{:S(2)}) collective-permute-start(bf16[2,96,512]{2,1,0:T(8,128)(2,1)S(1)} %pad_maximum_fusion.24), channel_id=1, source_target_pairs={{0,24},{1,25},{2,26},{3,27},{4,28},{5,29},{6,30},{7,31},{8,16},{9,... | collective-permute-start | bytes 589832 | tf_op jit(solution)/shard_map/ppermute | solution.py:223
  68.7 9.6 %collective-permute-start.23 = (bf16[3,96,512]{2,1,0:T(8,128)(2,1)S(1)}, bf16[3,96,512]{2,1,0:T(8,128)(2,1)S(1)}, u32[]{:S(2)}, u32[]{:S(2)}) collective-permute-start(bf16[3,96,512]{2,1,0:T(8,128)(2,1)S(1)} %get-tuple-element.49), channel_id=1, source_target_pairs={{0,2},{1,3},{2,0},{3,1},{4,6},{5,7},{6,4},{7,5},{8,10},{9,11},{10,... | collective-permute-start | bytes 884744 | tf_op jit(solution)/shard_map/ppermute | solution.py:223
  72.6 9.8 %collective-permute-start.21 = (bf16[3,96,512]{2,1,0:T(8,128)(2,1)S(1)}, bf16[3,96,512]{2,1,0:T(8,128)(2,1)S(1)}, u32[]{:S(2)}, u32[]{:S(2)}) collective-permute-start(bf16[3,96,512]{2,1,0:T(8,128)(2,1)S(1)} %get-tuple-element.49), channel_id=1, source_target_pairs={{0,6},{1,7},{2,4},{3,5},{4,2},{5,3},{6,0},{7,1},{8,14},{9,15},{10,... | collective-permute-start | bytes 884744 | tf_op jit(solution)/shard_map/ppermute | solution.py:223
  78.7 6.7 %collective-permute-start.24 = (bf16[2,96,512]{2,1,0:T(8,128)(2,1)S(1)}, bf16[2,96,512]{2,1,0:T(8,128)(2,1)S(1)}, u32[]{:S(2)}, u32[]{:S(2)}) collective-permute-start(bf16[2,96,512]{2,1,0:T(8,128)(2,1)S(1)} %pad_maximum_fusion.27), channel_id=1, source_target_pairs={{0,24},{1,25},{2,26},{3,27},{4,28},{5,29},{6,30},{7,31},{8,16},{9,... | collective-permute-start | bytes 589832 | tf_op jit(solution)/shard_map/ppermute | solution.py:223
  80.8 7.1 %collective-permute-start.25 = (bf16[2,96,512]{2,1,0:T(8,128)(2,1)S(1)}, bf16[2,96,512]{2,1,0:T(8,128)(2,1)S(1)}, u32[]{:S(2)}, u32[]{:S(2)}) collective-permute-start(bf16[2,96,512]{2,1,0:T(8,128)(2,1)S(1)} %pad_maximum_fusion.28), channel_id=1, source_target_pairs={{0,16},{1,17},{2,18},{3,19},{4,20},{5,21},{6,22},{7,23},{8,24},{9,... | collective-permute-start | bytes 589832 | tf_op jit(solution)/shard_map/ppermute | solution.py:223
  81.3 6.7 %collective-permute-start.26 = (bf16[2,96,512]{2,1,0:T(8,128)(2,1)S(1)}, bf16[2,96,512]{2,1,0:T(8,128)(2,1)S(1)}, u32[]{:S(2)}, u32[]{:S(2)}) collective-permute-start(bf16[2,96,512]{2,1,0:T(8,128)(2,1)S(1)} %pad_maximum_fusion.29), channel_id=1, source_target_pairs={{0,8},{1,9},{2,10},{3,11},{4,12},{5,13},{6,14},{7,15},{8,0},{9,1},... | collective-permute-start | bytes 589832 | tf_op jit(solution)/shard_map/ppermute | solution.py:223
  82.4 5.8 %collective-permute-start.22 = (bf16[4,96,512]{2,1,0:T(8,128)(2,1)S(1)}, bf16[4,96,512]{2,1,0:T(8,128)(2,1)S(1)}, u32[]{:S(2)}, u32[]{:S(2)}) collective-permute-start(bf16[4,96,512]{2,1,0:T(8,128)(2,1)S(1)} %pad_maximum_fusion.1), channel_id=1, source_target_pairs={{0,1},{1,0},{2,3},{3,2},{4,5},{5,4},{6,7},{7,6},{8,9},{9,8},{10,11... | collective-permute-start | bytes 1179656 | tf_op jit(solution)/shard_map/ppermute | solution.py:223
  85.8 8.6 %collective-permute-start.27 = (bf16[2,96,512]{2,1,0:T(8,128)(2,1)S(1)}, bf16[2,96,512]{2,1,0:T(8,128)(2,1)S(1)}, u32[]{:S(2)}, u32[]{:S(2)}) collective-permute-start(bf16[2,96,512]{2,1,0:T(8,128)(2,1)S(1)} %pad_maximum_fusion.30), channel_id=1, source_target_pairs={{0,24},{1,25},{2,26},{3,27},{4,28},{5,29},{6,30},{7,31},{8,16},{9,... | collective-permute-start | bytes 589832 | tf_op jit(solution)/shard_map/ppermute | solution.py:223
  87.9 6.7 %collective-permute-start.31 = (bf16[3,96,512]{2,1,0:T(8,128)(2,1)S(1)}, bf16[3,96,512]{2,1,0:T(8,128)(2,1)S(1)}, u32[]{:S(2)}, u32[]{:S(2)}) collective-permute-start(bf16[3,96,512]{2,1,0:T(8,128)(2,1)S(1)} %collective-permute-done.21), channel_id=1, source_target_pairs={{0,2},{1,3},{2,0},{3,1},{4,6},{5,7},{6,4},{7,5},{8,10},{9,11},{10,... | collective-permute-start | bytes 884744 | tf_op jit(solution)/shard_map/ppermute | solution.py:223
  88.2 11.3 %collective-permute-start.28 = (bf16[2,96,512]{2,1,0:T(8,128)(2,1)S(1)}, bf16[2,96,512]{2,1,0:T(8,128)(2,1)S(1)}, u32[]{:S(2)}, u32[]{:S(2)}) collective-permute-start(bf16[2,96,512]{2,1,0:T(8,128)(2,1)S(1)} %pad_maximum_fusion.31), channel_id=1, source_target_pairs={{0,16},{1,17},{2,18},{3,19},{4,20},{5,21},{6,22},{7,23},{8,24},{9,... | collective-permute-start | bytes 589832 | tf_op jit(solution)/shard_map/ppermute | solution.py:223
  90.2 9.3 %collective-permute-start.30 = (bf16[2,96,512]{2,1,0:T(8,128)(2,1)S(1)}, bf16[2,96,512]{2,1,0:T(8,128)(2,1)S(1)}, u32[]{:S(2)}, u32[]{:S(2)}) collective-permute-start(bf16[2,96,512]{2,1,0:T(8,128)(2,1)S(1)} %pad_maximum_fusion.32), channel_id=1, source_target_pairs={{0,8},{1,9},{2,10},{3,11},{4,12},{5,13},{6,14},{7,15},{8,0},{9,1},... | collective-permute-start | bytes 589832 | tf_op jit(solution)/shard_map/ppermute | solution.py:223
  95.1 8.0 %collective-permute-start.32 = (bf16[2,96,512]{2,1,0:T(8,128)(2,1)S(1)}, bf16[2,96,512]{2,1,0:T(8,128)(2,1)S(1)}, u32[]{:S(2)}, u32[]{:S(2)}) collective-permute-start(bf16[2,96,512]{2,1,0:T(8,128)(2,1)S(1)} %pad_maximum_fusion.33), channel_id=1, source_target_pairs={{0,24},{1,25},{2,26},{3,27},{4,28},{5,29},{6,30},{7,31},{8,16},{9,... | collective-permute-start | bytes 589832 | tf_op jit(solution)/shard_map/ppermute | solution.py:223
  97.0 7.7 %collective-permute-start.34 = (bf16[2,96,512]{2,1,0:T(8,128)(2,1)S(1)}, bf16[2,96,512]{2,1,0:T(8,128)(2,1)S(1)}, u32[]{:S(2)}, u32[]{:S(2)}) collective-permute-start(bf16[2,96,512]{2,1,0:T(8,128)(2,1)S(1)} %pad_maximum_fusion.34), channel_id=1, source_target_pairs={{0,16},{1,17},{2,18},{3,19},{4,20},{5,21},{6,22},{7,23},{8,24},{9,... | collective-permute-start | bytes 589832 | tf_op jit(solution)/shard_map/ppermute | solution.py:223
  97.6 7.1 %collective-permute-start.35 = (bf16[2,96,512]{2,1,0:T(8,128)(2,1)S(1)}, bf16[2,96,512]{2,1,0:T(8,128)(2,1)S(1)}, u32[]{:S(2)}, u32[]{:S(2)}) collective-permute-start(bf16[2,96,512]{2,1,0:T(8,128)(2,1)S(1)} %pad_maximum_fusion.35), channel_id=1, source_target_pairs={{0,8},{1,9},{2,10},{3,11},{4,12},{5,13},{6,14},{7,15},{8,0},{9,1},... | collective-permute-start | bytes 589832 | tf_op jit(solution)/shard_map/ppermute | solution.py:223
  99.5 5.4 %collective-permute-start.29 = (bf16[4,96,512]{2,1,0:T(8,128)(2,1)S(1)}, bf16[4,96,512]{2,1,0:T(8,128)(2,1)S(1)}, u32[]{:S(2)}, u32[]{:S(2)}) collective-permute-start(bf16[4,96,512]{2,1,0:T(8,128)(2,1)S(1)} %pad_maximum_fusion.4), channel_id=1, source_target_pairs={{0,1},{1,0},{2,3},{3,2},{4,5},{5,4},{6,7},{7,6},{8,9},{9,8},{10,11... | collective-permute-start | bytes 1179656 | tf_op jit(solution)/shard_map/ppermute | solution.py:223
  103.1 2.2 %collective-permute-start.33 = (bf16[4,96,512]{2,1,0:T(8,128)(2,1)S(1)}, bf16[4,96,512]{2,1,0:T(8,128)(2,1)S(1)}, u32[]{:S(2)}, u32[]{:S(2)}) collective-permute-start(bf16[4,96,512]{2,1,0:T(8,128)(2,1)S(1)} %pad_maximum_fusion.7), channel_id=1, source_target_pairs={{0,1},{1,0},{2,3},{3,2},{4,5},{5,4},{6,7},{7,6},{8,9},{9,8},{10,11... | collective-permute-start | bytes 1179656 | tf_op jit(solution)/shard_map/ppermute | solution.py:223
  104.8 1.8 %collective-permute-start.36 = (bf16[4,96,512]{2,1,0:T(8,128)(2,1)S(1)}, bf16[4,96,512]{2,1,0:T(8,128)(2,1)S(1)}, u32[]{:S(2)}, u32[]{:S(2)}) collective-permute-start(bf16[4,96,512]{2,1,0:T(8,128)(2,1)S(1)} %pad_maximum_fusion.10), channel_id=1, source_target_pairs={{0,1},{1,0},{2,3},{3,2},{4,5},{5,4},{6,7},{7,6},{8,9},{9,8},{10,11... | collective-permute-start | bytes 1179656 | tf_op jit(solution)/shard_map/ppermute | solution.py:223
  106.9 1.7 %copy-start = (bf16[4,2,96,2048]{3,2,1,0:T(8,128)(2,1)}, bf16[4,2,96,2048]{3,2,1,0:T(8,128)(2,1)S(1)}, u32[]{:S(2)}) copy-start(bf16[4,2,96,2048]{3,2,1,0:T(8,128)(2,1)S(1)} %fusion.3) | copy-start | bytes 9437188

commit v5 on v4

--- a/solution.py
+++ b/solution.py
@@ -17,17 +17,20 @@
 SUM_TIES = {
     (1, 3): [(0, 1)],
     ("sum", 0): [(0, 2)],
+    (2, 1): [("other", 1)],
+    (2, 3): [("other", 1), (1, 3)],
     ("sum", 1): [(1, 3)],
     (3, 1): [("sum", 0)],
     (3, 2): [(0, 1), (0, 3)],
     (3, 3): [(2, 2)],
     ("sum", 2): [(2, 3)],
     "rest": [(0, 2)],
-    (1, 1): [(0, 2)],
+    (1, 1): [(0, 3)],
 }
 SPREAD_TIES = {
-    ("choose", 1): [(0, 2)],
+    ("choose", 1): [(0, 1)],
     (1, 2): [(0, 2)],
+    (1, 3): [(0, 3)],
     ("choose", 2): [(1, 3)],
     (2, 2): [("core", 0)],
     ("choose", 3): [(2, 3), ("core", 0)],
@@ -37,8 +40,9 @@
     ("core", 1): [(2, 3), (2, 2)],
     ("core", 0): [("shard", 2)],
     (2, 1): [("core", 0)],
-    ("core", 2): [(3, 3)],
+    ("core", 2): [(3, 1)],
     ("core", 3): [(3, 1)],
+    (1, 1): [(0, 1), (0, 2)],
 }
 
 
@@ -246,7 +250,7 @@
     to_group = [[(d, d ^ (j * owners)) for d in everyone] for j in range(groups)]
     to_plane = [[(d, d ^ 2 * s) for d in everyone] for s in range(planes)]
     others = range(1, groups)
-    lead = 2
+    lead = 3
 
     turned, upstream, first_keep, first_send, chosen = first_blocks(
         row_counts, plan_now, plan_next, hidden_acts[0, 0], out_grads[0, 0], experts, lead

time: 109 us -> 104 us (0.954)
  waiting for transfers between devices: 47.8 us -> 40.3 us
  starting transfers between devices: 42.2 us -> 45.3 us
    ppermute x37 -> x36, waiting for transfers between devices: 47.8 us -> 40.3 us  [send(): self.arrived[name] = lax.ppermute(self.hold(name, value), AXES, pairs)]
    ppermute x37 -> x36, starting transfers between devices: 42.2 us -> 45.3 us  [send(): self.arrived[name] = lax.ppermute(self.hold(name, value), AXES, pairs)]
  transfers between devices with their start and end apart: 37 -> 36, of which waited for: 18 -> 18; matrix products, arithmetic and copies ran while one was open for 5% -> 5% of each run, Pallas kernels for 2% -> 1%
where the time goes in v5:
time: 104 us
  starting transfers between devices  45.3 us (44%)
  waiting for transfers between devices  40.3 us (39%)
  Pallas kernels  7.44 us (7%)
  other arithmetic  7.23 us (7%)
  local copies, waits for them, and re-layouts  2.08 us (2%)
  between operations  1.95 us (2%)
    ppermute x36, starting transfers between devices, send(): self.arrived[name] = lax.ppermute(self.hold(name, value), AXES, pairs)  45.3 us
    ppermute x36, waiting for transfers between devices, send(): self.arrived[name] = lax.ppermute(self.hold(name, value), AXES, pairs)  40.3 us
    pallas_call x1, Pallas kernels, first_blocks(): pl.pallas_call(first_kernel, in_specs=[pl.BlockSpec(memory_space=pltpu.SM...  5.88 us
    reduce_sum x4, other arithmetic, chosen_blocks(): jnp.sum(later[2 * j + i][:, None] * shard, axis=0).astype(jnp.bfloat16)  3.39 us
  transfers between devices with their start and end apart: 36, of which 18 were waited for; matrix products, arithmetic and copies ran while one was open for 5% of the time, Pallas kernels for 1%

profile of v5, /device:TPU:0, one launch (start us, length us, event | category | flops | bytes accessed | tf_op | source)
XLA Modules:
  0.0 104.3 jit_solution(15077845509041588556)
XLA Ops:
  1.3 5.9 %first_blocks.1 = (bf16[768,1024]{1,0:T(8,128)(2,1)S(1)}, bf16[1024,2048]{1,0:T(8,128)(2,1)S(1)}, bf16[3,4,96,512]{3,2,1,0:T(8,128)(2,1)S(1)}, bf16[3,4,96,512]{3,2,1,0:T(8,128)(2,1)S(1)}, f32[2,8,3,512]{3,2,1,0:T(4,128)S(1)}) custom-call(s32[1,1]{1,0:T(1,128)S(6)} %copy.16.count_ref, s32[4,8]{1,0:T(4,128)} %now_hbm.1, s32[4,8]{1,0:T(4,128)} %next_hbm.1, ...), custom_call_target="tpu_custom_call" | custom-call | flops 2415919104 | bytes 5767168 | tf_op jit(solution)/shard_map/first_blocks/pallas_call | solution.py:170
  7.2 0.5 collective-permute-start
  7.7 0.1 bitcast_convert_fusion.1
  7.9 2.3 %collective-permute-done = bf16[3,4,96,512]{3,2,1,0:T(8,128)(2,1)S(1)} collective-permute-done((bf16[3,4,96,512]{3,2,1,0:T(8,128)(2,1)S(1)}, bf16[3,4,96,512]{3,2,1,0:T(8,128)(2,1)S(1)}, u32[]{:S(2)}, u32[]{:S(2)}) %collective-permute-start) | collective-permute-done | bytes 1179680 | tf_op jit(solution)/shard_map/ppermute | solution.py:227
  10.3 2.9 %collective-permute-start.3 = (bf16[2,96,512]{2,1,0:T(8,128)(2,1)S(1)}, bf16[2,96,512]{2,1,0:T(8,128)(2,1)S(1)}, u32[]{:S(2)}, u32[]{:S(2)}) collective-permute-start(bf16[2,96,512]{2,1,0:T(8,128)(2,1)S(1)} %pad_maximum_fusion.14), channel_id=1, source_target_pairs={{0,8},{1,9},{2,10},{3,11},{4,12},{5,13},{6,14},{7,15},{8,0},{9,1},... | collective-permute-start | bytes 589832 | tf_op jit(solution)/shard_map/ppermute | solution.py:227
  13.3 1.6 %collective-permute-start.8 = (bf16[2,96,512]{2,1,0:T(8,128)(2,1)S(1)}, bf16[2,96,512]{2,1,0:T(8,128)(2,1)S(1)}, u32[]{:S(2)}, u32[]{:S(2)}) collective-permute-start(bf16[2,96,512]{2,1,0:T(8,128)(2,1)S(1)} %pad_maximum_fusion.18), channel_id=1, source_target_pairs={{0,16},{1,17},{2,18},{3,19},{4,20},{5,21},{6,22},{7,23},{8,24},{9,... | collective-permute-start | bytes 589832 | tf_op jit(solution)/shard_map/ppermute | solution.py:227
  14.9 0.6 collective-permute-start.14
  15.5 1.5 %collective-permute-start.4 = (bf16[2,96,512]{2,1,0:T(8,128)(2,1)S(1)}, bf16[2,96,512]{2,1,0:T(8,128)(2,1)S(1)}, u32[]{:S(2)}, u32[]{:S(2)}) collective-permute-start(bf16[2,96,512]{2,1,0:T(8,128)(2,1)S(1)} %pad_maximum_fusion.15), channel_id=1, source_target_pairs={{0,24},{1,25},{2,26},{3,27},{4,28},{5,29},{6,30},{7,31},{8,16},{9,... | collective-permute-start | bytes 589832 | tf_op jit(solution)/shard_map/ppermute | solution.py:227
  17.0 1.6 %collective-permute-start.1 = (bf16[2,96,512]{2,1,0:T(8,128)(2,1)S(1)}, bf16[2,96,512]{2,1,0:T(8,128)(2,1)S(1)}, u32[]{:S(2)}, u32[]{:S(2)}) collective-permute-start(bf16[2,96,512]{2,1,0:T(8,128)(2,1)S(1)} %pad_maximum_fusion.12), channel_id=1, source_target_pairs={{0,16},{1,17},{2,18},{3,19},{4,20},{5,21},{6,22},{7,23},{8,24},{9,... | collective-permute-start | bytes 589832 | tf_op jit(solution)/shard_map/ppermute | solution.py:227
  18.7 0.2 collective-permute-done.3
  18.9 2.1 %collective-permute-start.11 = (bf16[2,96,512]{2,1,0:T(8,128)(2,1)S(1)}, bf16[2,96,512]{2,1,0:T(8,128)(2,1)S(1)}, u32[]{:S(2)}, u32[]{:S(2)}) collective-permute-start(bf16[2,96,512]{2,1,0:T(8,128)(2,1)S(1)} %pad_maximum_fusion.20), channel_id=1, source_target_pairs={{0,16},{1,17},{2,18},{3,19},{4,20},{5,21},{6,22},{7,23},{8,24},{9,... | collective-permute-start | bytes 589832 | tf_op jit(solution)/shard_map/ppermute | solution.py:227
  21.1 7.1 %collective-permute-done.4 = bf16[2,96,512]{2,1,0:T(8,128)(2,1)S(1)} collective-permute-done((bf16[2,96,512]{2,1,0:T(8,128)(2,1)S(1)}, bf16[2,96,512]{2,1,0:T(8,128)(2,1)S(1)}, u32[]{:S(2)}, u32[]{:S(2)}) %collective-permute-start.4) | collective-permute-done | bytes 196640 | tf_op jit(solution)/shard_map/ppermute | solution.py:227
  28.2 1.4 %collective-permute-start.12 = (bf16[2,96,512]{2,1,0:T(8,128)(2,1)S(1)}, bf16[2,96,512]{2,1,0:T(8,128)(2,1)S(1)}, u32[]{:S(2)}, u32[]{:S(2)}) collective-permute-start(bf16[2,96,512]{2,1,0:T(8,128)(2,1)S(1)} %get-tuple-element.49), channel_id=1, source_target_pairs={{0,24},{1,25},{2,26},{3,27},{4,28},{5,29},{6,30},{7,31},{8,16},{9,... | collective-permute-start | bytes 589832 | tf_op jit(solution)/shard_map/ppermute | solution.py:227
  29.7 0.3 add_convert_fusion.2
  30.1 1.6 %collective-permute-start.5 = (bf16[3,96,512]{2,1,0:T(8,128)(2,1)S(1)}, bf16[3,96,512]{2,1,0:T(8,128)(2,1)S(1)}, u32[]{:S(2)}, u32[]{:S(2)}) collective-permute-start(bf16[3,96,512]{2,1,0:T(8,128)(2,1)S(1)} %add_convert_fusion.2), channel_id=1, source_target_pairs={{0,2},{1,3},{2,0},{3,1},{4,6},{5,7},{6,4},{7,5},{8,10},{9,11},{10,... | collective-permute-start | bytes 884744 | tf_op jit(solution)/shard_map/ppermute | solution.py:227
  31.7 1.6 %rest_blocks.1 = (bf16[1,4,96,512]{3,2,1,0:T(8,128)(2,1)S(1)}, bf16[1,4,96,512]{3,2,1,0:T(8,128)(2,1)S(1)}) custom-call(bf16[768,1024]{1,0:T(8,128)(2,1)S(1)} %get-tuple-element.40.turned_ref, bf16[1024,2048]{1,0:T(8,128)(2,1)S(1)} %get-tuple-element.41.upstream_ref), custom_call_target="tpu_custom_call" | custom-call | flops 805306368 | bytes 786432 | tf_op jit(solution)/shard_map/rest_blocks/pallas_call | solution.py:206
  33.3 0.6 collective-permute-start.10
  34.1 2.8 %collective-permute-done.11 = bf16[2,96,512]{2,1,0:T(8,128)(2,1)S(1)} collective-permute-done((bf16[2,96,512]{2,1,0:T(8,128)(2,1)S(1)}, bf16[2,96,512]{2,1,0:T(8,128)(2,1)S(1)}, u32[]{:S(2)}, u32[]{:S(2)}) %collective-permute-start.11) | collective-permute-done | bytes 196640 | tf_op jit(solution)/shard_map/ppermute | solution.py:227
  37.0 1.6 %collective-permute-start.15 = (bf16[2,96,512]{2,1,0:T(8,128)(2,1)S(1)}, bf16[2,96,512]{2,1,0:T(8,128)(2,1)S(1)}, u32[]{:S(2)}, u32[]{:S(2)}) collective-permute-start(bf16[2,96,512]{2,1,0:T(8,128)(2,1)S(1)} %pad_maximum_fusion.23), channel_id=1, source_target_pairs={{0,24},{1,25},{2,26},{3,27},{4,28},{5,29},{6,30},{7,31},{8,16},{9,... | collective-permute-start | bytes 589832 | tf_op jit(solution)/shard_map/ppermute | solution.py:227
  38.6 0.5 collective-permute-done.10
  39.1 0.4 add_convert_fusion.1
  39.4 3.2 %collective-permute-start.13 = (bf16[3,96,512]{2,1,0:T(8,128)(2,1)S(1)}, bf16[3,96,512]{2,1,0:T(8,128)(2,1)S(1)}, u32[]{:S(2)}, u32[]{:S(2)}) collective-permute-start(bf16[3,96,512]{2,1,0:T(8,128)(2,1)S(1)} %add_convert_fusion.1), channel_id=1, source_target_pairs={{0,6},{1,7},{2,4},{3,5},{4,2},{5,3},{6,0},{7,1},{8,14},{9,15},{10,... | collective-permute-start | bytes 884744 | tf_op jit(solution)/shard_map/ppermute | solution.py:227
  42.7 1.5 %collective-permute-done.15 = bf16[2,96,512]{2,1,0:T(8,128)(2,1)S(1)} collective-permute-done((bf16[2,96,512]{2,1,0:T(8,128)(2,1)S(1)}, bf16[2,96,512]{2,1,0:T(8,128)(2,1)S(1)}, u32[]{:S(2)}, u32[]{:S(2)}) %collective-permute-start.15) | collective-permute-done | bytes 196640 | tf_op jit(solution)/shard_map/ppermute | solution.py:227
  44.2 0.3 add_convert_fusion
  44.6 1.1 %collective-permute-start.16 = (bf16[3,96,512]{2,1,0:T(8,128)(2,1)S(1)}, bf16[3,96,512]{2,1,0:T(8,128)(2,1)S(1)}, u32[]{:S(2)}, u32[]{:S(2)}) collective-permute-start(bf16[3,96,512]{2,1,0:T(8,128)(2,1)S(1)} %add_convert_fusion), channel_id=1, source_target_pairs={{0,2},{1,3},{2,0},{3,1},{4,6},{5,7},{6,4},{7,5},{8,10},{9,11},{10,... | collective-permute-start | bytes 884744 | tf_op jit(solution)/shard_map/ppermute | solution.py:227
  45.8 1.5 %collective-permute-start.9 = (bf16[2,96,512]{2,1,0:T(8,128)(2,1)S(1)}, bf16[2,96,512]{2,1,0:T(8,128)(2,1)S(1)}, u32[]{:S(2)}, u32[]{:S(2)}) collective-permute-start(bf16[2,96,512]{2,1,0:T(8,128)(2,1)S(1)} %pad_maximum_fusion.17), channel_id=1, source_target_pairs={{0,24},{1,25},{2,26},{3,27},{4,28},{5,29},{6,30},{7,31},{8,16},{9,... | collective-permute-start | bytes 589832 | tf_op jit(solution)/shard_map/ppermute | solution.py:227
  47.3 1.6 %collective-permute-start.7 = (bf16[2,96,512]{2,1,0:T(8,128)(2,1)S(1)}, bf16[2,96,512]{2,1,0:T(8,128)(2,1)S(1)}, u32[]{:S(2)}, u32[]{:S(2)}) collective-permute-start(bf16[2,96,512]{2,1,0:T(8,128)(2,1)S(1)} %pad_maximum_fusion.16), channel_id=1, source_target_pairs={{0,16},{1,17},{2,18},{3,19},{4,20},{5,21},{6,22},{7,23},{8,24},{9,... | collective-permute-start | bytes 589832 | tf_op jit(solution)/shard_map/ppermute | solution.py:227
  48.9 0.6 collective-permute-start.6
  49.5 3.8 %collective-permute-done.9 = bf16[2,96,512]{2,1,0:T(8,128)(2,1)S(1)} collective-permute-done((bf16[2,96,512]{2,1,0:T(8,128)(2,1)S(1)}, bf16[2,96,512]{2,1,0:T(8,128)(2,1)S(1)}, u32[]{:S(2)}, u32[]{:S(2)}) %collective-permute-start.9) | collective-permute-done | bytes 196640 | tf_op jit(solution)/shard_map/ppermute | solution.py:227
  53.4 1.9 %collective-permute-done.7 = bf16[2,96,512]{2,1,0:T(8,128)(2,1)S(1)} collective-permute-done((bf16[2,96,512]{2,1,0:T(8,128)(2,1)S(1)}, bf16[2,96,512]{2,1,0:T(8,128)(2,1)S(1)}, u32[]{:S(2)}, u32[]{:S(2)}) %collective-permute-start.7) | collective-permute-done | bytes 196640 | tf_op jit(solution)/shard_map/ppermute | solution.py:227
  55.3 0.4 collective-permute-done.6
  55.8 2.3 %fusion.11 = (bf16[96,512]{1,0:T(8,128)(2,1)S(1)}, bf16[96,512]{1,0:T(8,128)(2,1)S(1)}, bf16[96,512]{1,0:T(8,128)(2,1)S(1)}, bf16[96,512]{1,0:T(8,128)(2,1)S(1)}...) fusion(f32[3,512]{1,0:T(4,128)S(1)} %get-tuple-element.230, ...), kind=kLoop, calls=%fused_computation.48 | loop fusion | flops 6832128 | bytes 6881280 | tf_op jit(solution)/shard_map/reduce_sum | solution.py:299
  58.2 1.5 %collective-permute-start.18 = (bf16[2,96,512]{2,1,0:T(8,128)(2,1)S(1)}, bf16[2,96,512]{2,1,0:T(8,128)(2,1)S(1)}, u32[]{:S(2)}, u32[]{:S(2)}) collective-permute-start(bf16[2,96,512]{2,1,0:T(8,128)(2,1)S(1)} %pad_maximum_fusion.25), channel_id=1, source_target_pairs={{0,16},{1,17},{2,18},{3,19},{4,20},{5,21},{6,22},{7,23},{8,24},{9,... | collective-permute-start | bytes 589832 | tf_op jit(solution)/shard_map/ppermute | solution.py:227
  59.7 0.5 collective-permute-start.19
  60.2 1.7 %collective-permute-start.17 = (bf16[2,96,512]{2,1,0:T(8,128)(2,1)S(1)}, bf16[2,96,512]{2,1,0:T(8,128)(2,1)S(1)}, u32[]{:S(2)}, u32[]{:S(2)}) collective-permute-start(bf16[2,96,512]{2,1,0:T(8,128)(2,1)S(1)} %pad_maximum_fusion.24), channel_id=1, source_target_pairs={{0,24},{1,25},{2,26},{3,27},{4,28},{5,29},{6,30},{7,31},{8,16},{9,... | collective-permute-start | bytes 589832 | tf_op jit(solution)/shard_map/ppermute | solution.py:227
  61.9 1.3 %collective-permute-start.22 = (bf16[3,96,512]{2,1,0:T(8,128)(2,1)S(1)}, bf16[3,96,512]{2,1,0:T(8,128)(2,1)S(1)}, u32[]{:S(2)}, u32[]{:S(2)}) collective-permute-start(bf16[3,96,512]{2,1,0:T(8,128)(2,1)S(1)} %get-tuple-element.53), channel_id=1, source_target_pairs={{0,2},{1,3},{2,0},{3,1},{4,6},{5,7},{6,4},{7,5},{8,10},{9,11},{10,... | collective-permute-start | bytes 884744 | tf_op jit(solution)/shard_map/ppermute | solution.py:227
  63.2 3.8 %collective-permute-done.19 = bf16[2,96,512]{2,1,0:T(8,128)(2,1)S(1)} collective-permute-done((bf16[2,96,512]{2,1,0:T(8,128)(2,1)S(1)}, bf16[2,96,512]{2,1,0:T(8,128)(2,1)S(1)}, u32[]{:S(2)}, u32[]{:S(2)}) %collective-permute-start.19) | collective-permute-done | bytes 196640 | tf_op jit(solution)/shard_map/ppermute | solution.py:227
  67.0 2.9 %collective-permute-start.20 = (bf16[3,96,512]{2,1,0:T(8,128)(2,1)S(1)}, bf16[3,96,512]{2,1,0:T(8,128)(2,1)S(1)}, u32[]{:S(2)}, u32[]{:S(2)}) collective-permute-start(bf16[3,96,512]{2,1,0:T(8,128)(2,1)S(1)} %get-tuple-element.53), channel_id=1, source_target_pairs={{0,6},{1,7},{2,4},{3,5},{4,2},{5,3},{6,0},{7,1},{8,14},{9,15},{10,... | collective-permute-start | bytes 884744 | tf_op jit(solution)/shard_map/ppermute | solution.py:227
  70.1 0.3 collective-permute-done.22
  70.4 0.4 fusion.19
  70.8 1.6 %collective-permute-start.23 = (bf16[2,96,512]{2,1,0:T(8,128)(2,1)S(1)}, bf16[2,96,512]{2,1,0:T(8,128)(2,1)S(1)}, u32[]{:S(2)}, u32[]{:S(2)}) collective-permute-start(bf16[2,96,512]{2,1,0:T(8,128)(2,1)S(1)} %pad_maximum_fusion.27), channel_id=1, source_target_pairs={{0,24},{1,25},{2,26},{3,27},{4,28},{5,29},{6,30},{7,31},{8,16},{9,... | collective-permute-start | bytes 589832 | tf_op jit(solution)/shard_map/ppermute | solution.py:227
  72.4 2.3 %collective-permute-start.24 = (bf16[2,96,512]{2,1,0:T(8,128)(2,1)S(1)}, bf16[2,96,512]{2,1,0:T(8,128)(2,1)S(1)}, u32[]{:S(2)}, u32[]{:S(2)}) collective-permute-start(bf16[2,96,512]{2,1,0:T(8,128)(2,1)S(1)} %pad_maximum_fusion.28), channel_id=1, source_target_pairs={{0,16},{1,17},{2,18},{3,19},{4,20},{5,21},{6,22},{7,23},{8,24},{9,... | collective-permute-start | bytes 589832 | tf_op jit(solution)/shard_map/ppermute | solution.py:227
  74.8 2.4 %collective-permute-done.20 = bf16[3,96,512]{2,1,0:T(8,128)(2,1)S(1)} collective-permute-done((bf16[3,96,512]{2,1,0:T(8,128)(2,1)S(1)}, bf16[3,96,512]{2,1,0:T(8,128)(2,1)S(1)}, u32[]{:S(2)}, u32[]{:S(2)}) %collective-permute-start.20) | collective-permute-done | bytes 294944 | tf_op jit(solution)/shard_map/ppermute | solution.py:227
  77.2 0.5 collective-permute-done.23
  77.7 0.4 fusion.27
  78.1 1.5 %collective-permute-start.26 = (bf16[2,96,512]{2,1,0:T(8,128)(2,1)S(1)}, bf16[2,96,512]{2,1,0:T(8,128)(2,1)S(1)}, u32[]{:S(2)}, u32[]{:S(2)}) collective-permute-start(bf16[2,96,512]{2,1,0:T(8,128)(2,1)S(1)} %pad_maximum_fusion.30), channel_id=1, source_target_pairs={{0,24},{1,25},{2,26},{3,27},{4,28},{5,29},{6,30},{7,31},{8,16},{9,... | collective-permute-start | bytes 589832 | tf_op jit(solution)/shard_map/ppermute | solution.py:227
  79.6 2.0 %collective-permute-start.30 = (bf16[3,96,512]{2,1,0:T(8,128)(2,1)S(1)}, bf16[3,96,512]{2,1,0:T(8,128)(2,1)S(1)}, u32[]{:S(2)}, u32[]{:S(2)}) collective-permute-start(bf16[3,96,512]{2,1,0:T(8,128)(2,1)S(1)} %collective-permute-done.20), channel_id=1, source_target_pairs={{0,2},{1,3},{2,0},{3,1},{4,6},{5,7},{6,4},{7,5},{8,10},{9,11},{10,... | collective-permute-start | bytes 884744 | tf_op jit(solution)/shard_map/ppermute | solution.py:227
  81.8 0.5 collective-permute-start.27
  82.3 1.5 %collective-permute-start.29 = (bf16[2,96,512]{2,1,0:T(8,128)(2,1)S(1)}, bf16[2,96,512]{2,1,0:T(8,128)(2,1)S(1)}, u32[]{:S(2)}, u32[]{:S(2)}) collective-permute-start(bf16[2,96,512]{2,1,0:T(8,128)(2,1)S(1)} %pad_maximum_fusion.32), channel_id=1, source_target_pairs={{0,8},{1,9},{2,10},{3,11},{4,12},{5,13},{6,14},{7,15},{8,0},{9,1},... | collective-permute-start | bytes 589832 | tf_op jit(solution)/shard_map/ppermute | solution.py:227
  83.9 2.2 %collective-permute-done.26 = bf16[2,96,512]{2,1,0:T(8,128)(2,1)S(1)} collective-permute-done((bf16[2,96,512]{2,1,0:T(8,128)(2,1)S(1)}, bf16[2,96,512]{2,1,0:T(8,128)(2,1)S(1)}, u32[]{:S(2)}, u32[]{:S(2)}) %collective-permute-start.26) | collective-permute-done | bytes 196640 | tf_op jit(solution)/shard_map/ppermute | solution.py:227
  86.1 2.9 %collective-permute-done.30 = bf16[3,96,512]{2,1,0:T(8,128)(2,1)S(1)} collective-permute-done((bf16[3,96,512]{2,1,0:T(8,128)(2,1)S(1)}, bf16[3,96,512]{2,1,0:T(8,128)(2,1)S(1)}, u32[]{:S(2)}, u32[]{:S(2)}) %collective-permute-start.30) | collective-permute-done | bytes 294944 | tf_op jit(solution)/shard_map/ppermute | solution.py:227
  89.0 0.4 fusion.35
  89.4 1.0 collective-permute-start.31
  90.4 1.1 %collective-permute-start.34 = (bf16[2,96,512]{2,1,0:T(8,128)(2,1)S(1)}, bf16[2,96,512]{2,1,0:T(8,128)(2,1)S(1)}, u32[]{:S(2)}, u32[]{:S(2)}) collective-permute-start(bf16[2,96,512]{2,1,0:T(8,128)(2,1)S(1)} %pad_maximum_fusion.35), channel_id=1, source_target_pairs={{0,16},{1,17},{2,18},{3,19},{4,20},{5,21},{6,22},{7,23},{8,24},{9,... | collective-permute-start | bytes 589832 | tf_op jit(solution)/shard_map/ppermute | solution.py:227
  91.5 1.6 %collective-permute-start.33 = (bf16[2,96,512]{2,1,0:T(8,128)(2,1)S(1)}, bf16[2,96,512]{2,1,0:T(8,128)(2,1)S(1)}, u32[]{:S(2)}, u32[]{:S(2)}) collective-permute-start(bf16[2,96,512]{2,1,0:T(8,128)(2,1)S(1)} %pad_maximum_fusion.34), channel_id=1, source_target_pairs={{0,24},{1,25},{2,26},{3,27},{4,28},{5,29},{6,30},{7,31},{8,16},{9,... | collective-permute-start | bytes 589832 | tf_op jit(solution)/shard_map/ppermute | solution.py:227
  93.1 0.2 broadcast_select_fusion.7
  93.3 0.4 broadcast_in_dim.14
  94.0 3.2 %collective-permute-done.31 = bf16[2,96,512]{2,1,0:T(8,128)(2,1)S(1)} collective-permute-done((bf16[2,96,512]{2,1,0:T(8,128)(2,1)S(1)}, bf16[2,96,512]{2,1,0:T(8,128)(2,1)S(1)}, u32[]{:S(2)}, u32[]{:S(2)}) %collective-permute-start.31) | collective-permute-done | bytes 196640 | tf_op jit(solution)/shard_map/ppermute | solution.py:227
  97.3 3.1 %collective-permute-done.34 = bf16[2,96,512]{2,1,0:T(8,128)(2,1)S(1)} collective-permute-done((bf16[2,96,512]{2,1,0:T(8,128)(2,1)S(1)}, bf16[2,96,512]{2,1,0:T(8,128)(2,1)S(1)}, u32[]{:S(2)}, u32[]{:S(2)}) %collective-permute-start.34) | collective-permute-done | bytes 196640 | tf_op jit(solution)/shard_map/ppermute | solution.py:227
  100.7 0.2 broadcast_select_fusion.5
  101.0 0.2 broadcast_select_fusion.3
  101.2 1.1 %collective-permute-done.35 = bf16[4,96,512]{2,1,0:T(8,128)(2,1)S(1)} collective-permute-done((bf16[4,96,512]{2,1,0:T(8,128)(2,1)S(1)}, bf16[4,96,512]{2,1,0:T(8,128)(2,1)S(1)}, u32[]{:S(2)}, u32[]{:S(2)}) %collective-permute-start.35) | collective-permute-done | bytes 393248 | tf_op jit(solution)/shard_map/ppermute | solution.py:227
  102.4 0.2 broadcast_select_fusion.1
  102.6 1.7 %copy-done = bf16[4,2,96,2048]{3,2,1,0:T(8,128)(2,1)} copy-done((bf16[4,2,96,2048]{3,2,1,0:T(8,128)(2,1)}, bf16[4,2,96,2048]{3,2,1,0:T(8,128)(2,1)S(1)}, u32[]{:S(2)}) %copy-start) | copy-done | bytes 3145752
  (90 shorter events, 2.5 us)
Async XLA Ops:
  7.2 3.0 %collective-permute-start = (bf16[3,4,96,512]{3,2,1,0:T(8,128)(2,1)S(1)}, bf16[3,4,96,512]{3,2,1,0:T(8,128)(2,1)S(1)}, u32[]{:S(2)}, u32[]{:S(2)}) collective-permute-start(bf16[3,4,96,512]{3,2,1,0:T(8,128)(2,1)S(1)} %get-tuple-element.39), channel_id=1, source_target_pairs={{0,1},{1,0},{2,3},{3,2},{4,5},{5,4},{6,7},{7,6},{8,9},{9,8},{10,11... | collective-permute-start | bytes 3538952 | tf_op jit(solution)/shard_map/ppermute | solution.py:227
  10.3 8.6 %collective-permute-start.3 = (bf16[2,96,512]{2,1,0:T(8,128)(2,1)S(1)}, bf16[2,96,512]{2,1,0:T(8,128)(2,1)S(1)}, u32[]{:S(2)}, u32[]{:S(2)}) collective-permute-start(bf16[2,96,512]{2,1,0:T(8,128)(2,1)S(1)} %pad_maximum_fusion.14), channel_id=1, source_target_pairs={{0,8},{1,9},{2,10},{3,11},{4,12},{5,13},{6,14},{7,15},{8,0},{9,1},... | collective-permute-start | bytes 589832 | tf_op jit(solution)/shard_map/ppermute | solution.py:227
  13.3 20.0 %collective-permute-start.8 = (bf16[2,96,512]{2,1,0:T(8,128)(2,1)S(1)}, bf16[2,96,512]{2,1,0:T(8,128)(2,1)S(1)}, u32[]{:S(2)}, u32[]{:S(2)}) collective-permute-start(bf16[2,96,512]{2,1,0:T(8,128)(2,1)S(1)} %pad_maximum_fusion.18), channel_id=1, source_target_pairs={{0,16},{1,17},{2,18},{3,19},{4,20},{5,21},{6,22},{7,23},{8,24},{9,... | collective-permute-start | bytes 589832 | tf_op jit(solution)/shard_map/ppermute | solution.py:227
  14.9 19.0 %collective-permute-start.14 = (bf16[2,96,512]{2,1,0:T(8,128)(2,1)S(1)}, bf16[2,96,512]{2,1,0:T(8,128)(2,1)S(1)}, u32[]{:S(2)}, u32[]{:S(2)}) collective-permute-start(bf16[2,96,512]{2,1,0:T(8,128)(2,1)S(1)} %pad_maximum_fusion.22), channel_id=1, source_target_pairs={{0,8},{1,9},{2,10},{3,11},{4,12},{5,13},{6,14},{7,15},{8,0},{9,1},... | collective-permute-start | bytes 589832 | tf_op jit(solution)/shard_map/ppermute | solution.py:227
  15.5 12.7 %collective-permute-start.4 = (bf16[2,96,512]{2,1,0:T(8,128)(2,1)S(1)}, bf16[2,96,512]{2,1,0:T(8,128)(2,1)S(1)}, u32[]{:S(2)}, u32[]{:S(2)}) collective-permute-start(bf16[2,96,512]{2,1,0:T(8,128)(2,1)S(1)} %pad_maximum_fusion.15), channel_id=1, source_target_pairs={{0,24},{1,25},{2,26},{3,27},{4,28},{5,29},{6,30},{7,31},{8,16},{9,... | collective-permute-start | bytes 589832 | tf_op jit(solution)/shard_map/ppermute | solution.py:227
  17.0 12.6 %collective-permute-start.1 = (bf16[2,96,512]{2,1,0:T(8,128)(2,1)S(1)}, bf16[2,96,512]{2,1,0:T(8,128)(2,1)S(1)}, u32[]{:S(2)}, u32[]{:S(2)}) collective-permute-start(bf16[2,96,512]{2,1,0:T(8,128)(2,1)S(1)} %pad_maximum_fusion.12), channel_id=1, source_target_pairs={{0,16},{1,17},{2,18},{3,19},{4,20},{5,21},{6,22},{7,23},{8,24},{9,... | collective-permute-start | bytes 589832 | tf_op jit(solution)/shard_map/ppermute | solution.py:227
  18.9 17.9 %collective-permute-start.11 = (bf16[2,96,512]{2,1,0:T(8,128)(2,1)S(1)}, bf16[2,96,512]{2,1,0:T(8,128)(2,1)S(1)}, u32[]{:S(2)}, u32[]{:S(2)}) collective-permute-start(bf16[2,96,512]{2,1,0:T(8,128)(2,1)S(1)} %pad_maximum_fusion.20), channel_id=1, source_target_pairs={{0,16},{1,17},{2,18},{3,19},{4,20},{5,21},{6,22},{7,23},{8,24},{9,... | collective-permute-start | bytes 589832 | tf_op jit(solution)/shard_map/ppermute | solution.py:227
  28.2 8.8 %collective-permute-start.12 = (bf16[2,96,512]{2,1,0:T(8,128)(2,1)S(1)}, bf16[2,96,512]{2,1,0:T(8,128)(2,1)S(1)}, u32[]{:S(2)}, u32[]{:S(2)}) collective-permute-start(bf16[2,96,512]{2,1,0:T(8,128)(2,1)S(1)} %get-tuple-element.49), channel_id=1, source_target_pairs={{0,24},{1,25},{2,26},{3,27},{4,28},{5,29},{6,30},{7,31},{8,16},{9,... | collective-permute-start | bytes 589832 | tf_op jit(solution)/shard_map/ppermute | solution.py:227
  30.1 9.0 %collective-permute-start.5 = (bf16[3,96,512]{2,1,0:T(8,128)(2,1)S(1)}, bf16[3,96,512]{2,1,0:T(8,128)(2,1)S(1)}, u32[]{:S(2)}, u32[]{:S(2)}) collective-permute-start(bf16[3,96,512]{2,1,0:T(8,128)(2,1)S(1)} %add_convert_fusion.2), channel_id=1, source_target_pairs={{0,2},{1,3},{2,0},{3,1},{4,6},{5,7},{6,4},{7,5},{8,10},{9,11},{10,... | collective-permute-start | bytes 884744 | tf_op jit(solution)/shard_map/ppermute | solution.py:227
  33.3 5.7 %collective-permute-start.10 = (bf16[2,96,512]{2,1,0:T(8,128)(2,1)S(1)}, bf16[2,96,512]{2,1,0:T(8,128)(2,1)S(1)}, u32[]{:S(2)}, u32[]{:S(2)}) collective-permute-start(bf16[2,96,512]{2,1,0:T(8,128)(2,1)S(1)} %get-tuple-element.48), channel_id=1, source_target_pairs={{0,8},{1,9},{2,10},{3,11},{4,12},{5,13},{6,14},{7,15},{8,0},{9,1},... | collective-permute-start | bytes 589832 | tf_op jit(solution)/shard_map/ppermute | solution.py:227
  33.9 11.7 %collective-permute-start.2 = (bf16[4,96,512]{2,1,0:T(8,128)(2,1)S(1)}, bf16[4,96,512]{2,1,0:T(8,128)(2,1)S(1)}, u32[]{:S(2)}, u32[]{:S(2)}) collective-permute-start(bf16[4,96,512]{2,1,0:T(8,128)(2,1)S(1)} %bitcast.350), channel_id=1, source_target_pairs={{0,1},{1,0},{2,3},{3,2},{4,5},{5,4},{6,7},{7,6},{8,9},{9,8},{10,11... | collective-permute-start | bytes 1179656 | tf_op jit(solution)/shard_map/ppermute | solution.py:227
  37.0 7.2 %collective-permute-start.15 = (bf16[2,96,512]{2,1,0:T(8,128)(2,1)S(1)}, bf16[2,96,512]{2,1,0:T(8,128)(2,1)S(1)}, u32[]{:S(2)}, u32[]{:S(2)}) collective-permute-start(bf16[2,96,512]{2,1,0:T(8,128)(2,1)S(1)} %pad_maximum_fusion.23), channel_id=1, source_target_pairs={{0,24},{1,25},{2,26},{3,27},{4,28},{5,29},{6,30},{7,31},{8,16},{9,... | collective-permute-start | bytes 589832 | tf_op jit(solution)/shard_map/ppermute | solution.py:227
  39.4 16.3 %collective-permute-start.13 = (bf16[3,96,512]{2,1,0:T(8,128)(2,1)S(1)}, bf16[3,96,512]{2,1,0:T(8,128)(2,1)S(1)}, u32[]{:S(2)}, u32[]{:S(2)}) collective-permute-start(bf16[3,96,512]{2,1,0:T(8,128)(2,1)S(1)} %add_convert_fusion.1), channel_id=1, source_target_pairs={{0,6},{1,7},{2,4},{3,5},{4,2},{5,3},{6,0},{7,1},{8,14},{9,15},{10,... | collective-permute-start | bytes 884744 | tf_op jit(solution)/shard_map/ppermute | solution.py:227
  44.6 11.2 %collective-permute-start.16 = (bf16[3,96,512]{2,1,0:T(8,128)(2,1)S(1)}, bf16[3,96,512]{2,1,0:T(8,128)(2,1)S(1)}, u32[]{:S(2)}, u32[]{:S(2)}) collective-permute-start(bf16[3,96,512]{2,1,0:T(8,128)(2,1)S(1)} %add_convert_fusion), channel_id=1, source_target_pairs={{0,2},{1,3},{2,0},{3,1},{4,6},{5,7},{6,4},{7,5},{8,10},{9,11},{10,... | collective-permute-start | bytes 884744 | tf_op jit(solution)/shard_map/ppermute | solution.py:227
  45.7 10.1 %copy-start.1 = (f32[3,96,512]{2,1,0:T(8,128)S(1)}, f32[3,96,512]{2,1,0:T(8,128)}, u32[]{:S(2)}) copy-start(f32[3,96,512]{2,1,0:T(8,128)} %param.13) | copy-start | bytes 1769476
  45.7 10.1 %copy-start.2 = (f32[3,96,512]{2,1,0:T(8,128)S(1)}, f32[3,96,512]{2,1,0:T(8,128)}, u32[]{:S(2)}) copy-start(f32[3,96,512]{2,1,0:T(8,128)} %param.14) | copy-start | bytes 1769476
  45.7 10.1 %copy-start.3 = (f32[3,96,512]{2,1,0:T(8,128)S(1)}, f32[3,96,512]{2,1,0:T(8,128)}, u32[]{:S(2)}) copy-start(f32[3,96,512]{2,1,0:T(8,128)} %param.15) | copy-start | bytes 1769476
  45.8 7.6 %collective-permute-start.9 = (bf16[2,96,512]{2,1,0:T(8,128)(2,1)S(1)}, bf16[2,96,512]{2,1,0:T(8,128)(2,1)S(1)}, u32[]{:S(2)}, u32[]{:S(2)}) collective-permute-start(bf16[2,96,512]{2,1,0:T(8,128)(2,1)S(1)} %pad_maximum_fusion.17), channel_id=1, source_target_pairs={{0,24},{1,25},{2,26},{3,27},{4,28},{5,29},{6,30},{7,31},{8,16},{9,... | collective-permute-start | bytes 589832 | tf_op jit(solution)/shard_map/ppermute | solution.py:227
  47.3 8.0 %collective-permute-start.7 = (bf16[2,96,512]{2,1,0:T(8,128)(2,1)S(1)}, bf16[2,96,512]{2,1,0:T(8,128)(2,1)S(1)}, u32[]{:S(2)}, u32[]{:S(2)}) collective-permute-start(bf16[2,96,512]{2,1,0:T(8,128)(2,1)S(1)} %pad_maximum_fusion.16), channel_id=1, source_target_pairs={{0,16},{1,17},{2,18},{3,19},{4,20},{5,21},{6,22},{7,23},{8,24},{9,... | collective-permute-start | bytes 589832 | tf_op jit(solution)/shard_map/ppermute | solution.py:227
  48.9 6.9 %collective-permute-start.6 = (bf16[2,96,512]{2,1,0:T(8,128)(2,1)S(1)}, bf16[2,96,512]{2,1,0:T(8,128)(2,1)S(1)}, u32[]{:S(2)}, u32[]{:S(2)}) collective-permute-start(bf16[2,96,512]{2,1,0:T(8,128)(2,1)S(1)} %pad_maximum_fusion.13), channel_id=1, source_target_pairs={{0,8},{1,9},{2,10},{3,11},{4,12},{5,13},{6,14},{7,15},{8,0},{9,1},... | collective-permute-start | bytes 589832 | tf_op jit(solution)/shard_map/ppermute | solution.py:227
  58.2 11.8 %collective-permute-start.18 = (bf16[2,96,512]{2,1,0:T(8,128)(2,1)S(1)}, bf16[2,96,512]{2,1,0:T(8,128)(2,1)S(1)}, u32[]{:S(2)}, u32[]{:S(2)}) collective-permute-start(bf16[2,96,512]{2,1,0:T(8,128)(2,1)S(1)} %pad_maximum_fusion.25), channel_id=1, source_target_pairs={{0,16},{1,17},{2,18},{3,19},{4,20},{5,21},{6,22},{7,23},{8,24},{9,... | collective-permute-start | bytes 589832 | tf_op jit(solution)/shard_map/ppermute | solution.py:227
  59.7 7.4 %collective-permute-start.19 = (bf16[2,96,512]{2,1,0:T(8,128)(2,1)S(1)}, bf16[2,96,512]{2,1,0:T(8,128)(2,1)S(1)}, u32[]{:S(2)}, u32[]{:S(2)}) collective-permute-start(bf16[2,96,512]{2,1,0:T(8,128)(2,1)S(1)} %pad_maximum_fusion.26), channel_id=1, source_target_pairs={{0,8},{1,9},{2,10},{3,11},{4,12},{5,13},{6,14},{7,15},{8,0},{9,1},... | collective-permute-start | bytes 589832 | tf_op jit(solution)/shard_map/ppermute | solution.py:227
  60.2 9.7 %collective-permute-start.17 = (bf16[2,96,512]{2,1,0:T(8,128)(2,1)S(1)}, bf16[2,96,512]{2,1,0:T(8,128)(2,1)S(1)}, u32[]{:S(2)}, u32[]{:S(2)}) collective-permute-start(bf16[2,96,512]{2,1,0:T(8,128)(2,1)S(1)} %pad_maximum_fusion.24), channel_id=1, source_target_pairs={{0,24},{1,25},{2,26},{3,27},{4,28},{5,29},{6,30},{7,31},{8,16},{9,... | collective-permute-start | bytes 589832 | tf_op jit(solution)/shard_map/ppermute | solution.py:227
  61.9 8.5 %collective-permute-start.22 = (bf16[3,96,512]{2,1,0:T(8,128)(2,1)S(1)}, bf16[3,96,512]{2,1,0:T(8,128)(2,1)S(1)}, u32[]{:S(2)}, u32[]{:S(2)}) collective-permute-start(bf16[3,96,512]{2,1,0:T(8,128)(2,1)S(1)} %get-tuple-element.53), channel_id=1, source_target_pairs={{0,2},{1,3},{2,0},{3,1},{4,6},{5,7},{6,4},{7,5},{8,10},{9,11},{10,... | collective-permute-start | bytes 884744 | tf_op jit(solution)/shard_map/ppermute | solution.py:227
  67.0 10.1 %collective-permute-start.20 = (bf16[3,96,512]{2,1,0:T(8,128)(2,1)S(1)}, bf16[3,96,512]{2,1,0:T(8,128)(2,1)S(1)}, u32[]{:S(2)}, u32[]{:S(2)}) collective-permute-start(bf16[3,96,512]{2,1,0:T(8,128)(2,1)S(1)} %get-tuple-element.53), channel_id=1, source_target_pairs={{0,6},{1,7},{2,4},{3,5},{4,2},{5,3},{6,0},{7,1},{8,14},{9,15},{10,... | collective-permute-start | bytes 884744 | tf_op jit(solution)/shard_map/ppermute | solution.py:227
  70.8 6.9 %collective-permute-start.23 = (bf16[2,96,512]{2,1,0:T(8,128)(2,1)S(1)}, bf16[2,96,512]{2,1,0:T(8,128)(2,1)S(1)}, u32[]{:S(2)}, u32[]{:S(2)}) collective-permute-start(bf16[2,96,512]{2,1,0:T(8,128)(2,1)S(1)} %pad_maximum_fusion.27), channel_id=1, source_target_pairs={{0,24},{1,25},{2,26},{3,27},{4,28},{5,29},{6,30},{7,31},{8,16},{9,... | collective-permute-start | bytes 589832 | tf_op jit(solution)/shard_map/ppermute | solution.py:227
  72.4 9.2 %collective-permute-start.24 = (bf16[2,96,512]{2,1,0:T(8,128)(2,1)S(1)}, bf16[2,96,512]{2,1,0:T(8,128)(2,1)S(1)}, u32[]{:S(2)}, u32[]{:S(2)}) collective-permute-start(bf16[2,96,512]{2,1,0:T(8,128)(2,1)S(1)} %pad_maximum_fusion.28), channel_id=1, source_target_pairs={{0,16},{1,17},{2,18},{3,19},{4,20},{5,21},{6,22},{7,23},{8,24},{9,... | collective-permute-start | bytes 589832 | tf_op jit(solution)/shard_map/ppermute | solution.py:227
  74.7 6.9 %collective-permute-start.25 = (bf16[2,96,512]{2,1,0:T(8,128)(2,1)S(1)}, bf16[2,96,512]{2,1,0:T(8,128)(2,1)S(1)}, u32[]{:S(2)}, u32[]{:S(2)}) collective-permute-start(bf16[2,96,512]{2,1,0:T(8,128)(2,1)S(1)} %pad_maximum_fusion.29), channel_id=1, source_target_pairs={{0,8},{1,9},{2,10},{3,11},{4,12},{5,13},{6,14},{7,15},{8,0},{9,1},... | collective-permute-start | bytes 589832 | tf_op jit(solution)/shard_map/ppermute | solution.py:227
  77.2 4.6 %collective-permute-start.21 = (bf16[4,96,512]{2,1,0:T(8,128)(2,1)S(1)}, bf16[4,96,512]{2,1,0:T(8,128)(2,1)S(1)}, u32[]{:S(2)}, u32[]{:S(2)}) collective-permute-start(bf16[4,96,512]{2,1,0:T(8,128)(2,1)S(1)} %pad_maximum_fusion.1), channel_id=1, source_target_pairs={{0,1},{1,0},{2,3},{3,2},{4,5},{5,4},{6,7},{7,6},{8,9},{9,8},{10,11... | collective-permute-start | bytes 1179656 | tf_op jit(solution)/shard_map/ppermute | solution.py:227
  78.1 8.0 %collective-permute-start.26 = (bf16[2,96,512]{2,1,0:T(8,128)(2,1)S(1)}, bf16[2,96,512]{2,1,0:T(8,128)(2,1)S(1)}, u32[]{:S(2)}, u32[]{:S(2)}) collective-permute-start(bf16[2,96,512]{2,1,0:T(8,128)(2,1)S(1)} %pad_maximum_fusion.30), channel_id=1, source_target_pairs={{0,24},{1,25},{2,26},{3,27},{4,28},{5,29},{6,30},{7,31},{8,16},{9,... | collective-permute-start | bytes 589832 | tf_op jit(solution)/shard_map/ppermute | solution.py:227
  79.6 9.4 %collective-permute-start.30 = (bf16[3,96,512]{2,1,0:T(8,128)(2,1)S(1)}, bf16[3,96,512]{2,1,0:T(8,128)(2,1)S(1)}, u32[]{:S(2)}, u32[]{:S(2)}) collective-permute-start(bf16[3,96,512]{2,1,0:T(8,128)(2,1)S(1)} %collective-permute-done.20), channel_id=1, source_target_pairs={{0,2},{1,3},{2,0},{3,1},{4,6},{5,7},{6,4},{7,5},{8,10},{9,11},{10,... | collective-permute-start | bytes 884744 | tf_op jit(solution)/shard_map/ppermute | solution.py:227
  81.8 12.0 %collective-permute-start.27 = (bf16[2,96,512]{2,1,0:T(8,128)(2,1)S(1)}, bf16[2,96,512]{2,1,0:T(8,128)(2,1)S(1)}, u32[]{:S(2)}, u32[]{:S(2)}) collective-permute-start(bf16[2,96,512]{2,1,0:T(8,128)(2,1)S(1)} %pad_maximum_fusion.31), channel_id=1, source_target_pairs={{0,16},{1,17},{2,18},{3,19},{4,20},{5,21},{6,22},{7,23},{8,24},{9,... | collective-permute-start | bytes 589832 | tf_op jit(solution)/shard_map/ppermute | solution.py:227
  82.3 11.5 %collective-permute-start.29 = (bf16[2,96,512]{2,1,0:T(8,128)(2,1)S(1)}, bf16[2,96,512]{2,1,0:T(8,128)(2,1)S(1)}, u32[]{:S(2)}, u32[]{:S(2)}) collective-permute-start(bf16[2,96,512]{2,1,0:T(8,128)(2,1)S(1)} %pad_maximum_fusion.32), channel_id=1, source_target_pairs={{0,8},{1,9},{2,10},{3,11},{4,12},{5,13},{6,14},{7,15},{8,0},{9,1},... | collective-permute-start | bytes 589832 | tf_op jit(solution)/shard_map/ppermute | solution.py:227
  89.4 7.9 %collective-permute-start.31 = (bf16[2,96,512]{2,1,0:T(8,128)(2,1)S(1)}, bf16[2,96,512]{2,1,0:T(8,128)(2,1)S(1)}, u32[]{:S(2)}, u32[]{:S(2)}) collective-permute-start(bf16[2,96,512]{2,1,0:T(8,128)(2,1)S(1)} %pad_maximum_fusion.33), channel_id=1, source_target_pairs={{0,8},{1,9},{2,10},{3,11},{4,12},{5,13},{6,14},{7,15},{8,0},{9,1},... | collective-permute-start | bytes 589832 | tf_op jit(solution)/shard_map/ppermute | solution.py:227
  90.4 9.9 %collective-permute-start.34 = (bf16[2,96,512]{2,1,0:T(8,128)(2,1)S(1)}, bf16[2,96,512]{2,1,0:T(8,128)(2,1)S(1)}, u32[]{:S(2)}, u32[]{:S(2)}) collective-permute-start(bf16[2,96,512]{2,1,0:T(8,128)(2,1)S(1)} %pad_maximum_fusion.35), channel_id=1, source_target_pairs={{0,16},{1,17},{2,18},{3,19},{4,20},{5,21},{6,22},{7,23},{8,24},{9,... | collective-permute-start | bytes 589832 | tf_op jit(solution)/shard_map/ppermute | solution.py:227
  91.5 8.8 %collective-permute-start.33 = (bf16[2,96,512]{2,1,0:T(8,128)(2,1)S(1)}, bf16[2,96,512]{2,1,0:T(8,128)(2,1)S(1)}, u32[]{:S(2)}, u32[]{:S(2)}) collective-permute-start(bf16[2,96,512]{2,1,0:T(8,128)(2,1)S(1)} %pad_maximum_fusion.34), channel_id=1, source_target_pairs={{0,24},{1,25},{2,26},{3,27},{4,28},{5,29},{6,30},{7,31},{8,16},{9,... | collective-permute-start | bytes 589832 | tf_op jit(solution)/shard_map/ppermute | solution.py:227
  93.8 6.8 %collective-permute-start.28 = (bf16[4,96,512]{2,1,0:T(8,128)(2,1)S(1)}, bf16[4,96,512]{2,1,0:T(8,128)(2,1)S(1)}, u32[]{:S(2)}, u32[]{:S(2)}) collective-permute-start(bf16[4,96,512]{2,1,0:T(8,128)(2,1)S(1)} %pad_maximum_fusion.4), channel_id=1, source_target_pairs={{0,1},{1,0},{2,3},{3,2},{4,5},{5,4},{6,7},{7,6},{8,9},{9,8},{10,11... | collective-permute-start | bytes 1179656 | tf_op jit(solution)/shard_map/ppermute | solution.py:227
  97.2 3.7 %collective-permute-start.32 = (bf16[4,96,512]{2,1,0:T(8,128)(2,1)S(1)}, bf16[4,96,512]{2,1,0:T(8,128)(2,1)S(1)}, u32[]{:S(2)}, u32[]{:S(2)}) collective-permute-start(bf16[4,96,512]{2,1,0:T(8,128)(2,1)S(1)} %pad_maximum_fusion.7), channel_id=1, source_target_pairs={{0,1},{1,0},{2,3},{3,2},{4,5},{5,4},{6,7},{7,6},{8,9},{9,8},{10,11... | collective-permute-start | bytes 1179656 | tf_op jit(solution)/shard_map/ppermute | solution.py:227
  100.5 1.8 %collective-permute-start.35 = (bf16[4,96,512]{2,1,0:T(8,128)(2,1)S(1)}, bf16[4,96,512]{2,1,0:T(8,128)(2,1)S(1)}, u32[]{:S(2)}, u32[]{:S(2)}) collective-permute-start(bf16[4,96,512]{2,1,0:T(8,128)(2,1)S(1)} %pad_maximum_fusion.10), channel_id=1, source_target_pairs={{0,1},{1,0},{2,3},{3,2},{4,5},{5,4},{6,7},{7,6},{8,9},{9,8},{10,11... | collective-permute-start | bytes 1179656 | tf_op jit(solution)/shard_map/ppermute | solution.py:227
  102.6 1.7 %copy-start = (bf16[4,2,96,2048]{3,2,1,0:T(8,128)(2,1)}, bf16[4,2,96,2048]{3,2,1,0:T(8,128)(2,1)S(1)}, u32[]{:S(2)}) copy-start(bf16[4,2,96,2048]{3,2,1,0:T(8,128)(2,1)S(1)} %fusion.3) | copy-start | bytes 9437188

commit v6 on v5

--- a/solution.py
+++ b/solution.py
@@ -17,8 +17,7 @@
 SUM_TIES = {
     (1, 3): [(0, 1)],
     ("sum", 0): [(0, 2)],
-    (2, 1): [("other", 1)],
-    (2, 3): [("other", 1), (1, 3)],
+    (2, 3): [(1, 3)],
     ("sum", 1): [(1, 3)],
     (3, 1): [("sum", 0)],
     (3, 2): [(0, 1), (0, 3)],
@@ -66,12 +65,12 @@
 
 def first_kernel(
     count_ref, now_hbm, next_hbm, hidden_hbm, upstream_hbm, turned_ref, upstream_ref, keep_ref, send_ref,
-    chosen_ref, hidden_ref, now_ref, next_ref, sems, small_sems,
+    chosen_ref, hidden_ref, now_ref, next_ref, sems, column_sems, small_sems,
 ):
     tokens, inner = hidden_ref.shape
     lead, groups, rows, cols = keep_ref.shape
     planes = inner // (2 * rows)
-    parts = sems.shape[1]
+    parts = sems.shape[0]
     part = tokens // parts
     group, owner = lax.axis_index("dp"), lax.axis_index("expert")
     plane, core = owner >> 1, owner & 1
@@ -82,18 +81,21 @@
     ]
     for copy in smalls:
         copy.start()
-    copies = []
-    for n in range(parts):
-        at = pl.ds(n * part, part)
-        copies.append(
-            [
-                pltpu.make_async_copy(hidden_hbm.at[at], hidden_ref.at[at], sems.at[0, n]),
-                pltpu.make_async_copy(upstream_hbm.at[at], upstream_ref.at[at], sems.at[1, n]),
-            ]
+    copies = [
+        pltpu.make_async_copy(
+            hidden_hbm.at[pl.ds(n * part, part)], hidden_ref.at[pl.ds(n * part, part)], sems.at[n]
         )
-    for kind in range(2):
-        for copy in copies:
-            copy[kind].start()
+        for n in range(parts)
+    ]
+    for copy in copies:
+        copy.start()
+
+    def column_copy(j):
+        at = pl.ds(pl.multiple_of((group ^ j) * cols, cols), cols)
+        return pltpu.make_async_copy(upstream_hbm.at[:, at], upstream_ref.at[:, at], column_sems.at[j])
+
+    for j in range(groups):
+        column_copy(j).start()
 
     for copy in smalls:
         copy.wait()
@@ -104,22 +106,17 @@
             chosen_ref[n, near] = jnp.where(names == named, 1.0, 0.0)
 
     for n in range(parts):
-        copies[n][0].wait()
+        copies[n].wait()
         hidden = hidden_ref[n * part : (n + 1) * part]
         live = lax.broadcasted_iota(jnp.int32, hidden.shape, 0) < count_ref[0, 0] - n * part
         hidden = jnp.where(live, hidden, jnp.zeros_like(hidden)).T
-        for m, s in enumerate(PLANE_ORDER):
-            for p in range(planes):
-
-                @pl.when(plane ^ s == p)
-                def put():
-                    turned_ref[2 * rows * m : 2 * rows * (m + 1), n * part : (n + 1) * part] = hidden[
-                        2 * rows * p : 2 * rows * (p + 1)
-                    ]
-    for n in range(parts):
-        copies[n][1].wait()
+        for p in range(planes):
+            position = sum(jnp.where(plane ^ s == p, m, 0) for m, s in enumerate(PLANE_ORDER))
+            at = pl.ds(pl.multiple_of(position * 2 * rows, 2 * rows), 2 * rows)
+            turned_ref[at, n * part : (n + 1) * part] = hidden[2 * rows * p : 2 * rows * (p + 1)]
 
     def columns(j, carry):
+        column_copy(j).wait()
         at = pl.ds(pl.multiple_of((group ^ j) * cols, cols), cols)
         product = jnp.dot(
             turned_ref[: 2 * rows * lead], upstream_ref[:, at], preferred_element_type=jnp.float32
@@ -182,7 +179,8 @@
             pltpu.VMEM((tokens, inner), jnp.bfloat16),
             pltpu.SMEM(plan_now.shape, jnp.int32),
             pltpu.SMEM(plan_next.shape, jnp.int32),
-            pltpu.SemaphoreType.DMA((2, parts)),
+            pltpu.SemaphoreType.DMA((parts,)),
+            pltpu.SemaphoreType.DMA((groups,)),
             pltpu.SemaphoreType.DMA((2,)),
         ],
         compiler_params=pltpu.CompilerParams(vmem_limit_bytes=24 * 2**20),

time: 104 us -> 104 us (level)
  transfers between devices with their start and end apart: 36 -> 36, of which waited for: 18 -> 18; matrix products, arithmetic and copies ran while one was open for 5% -> 5% of each run, Pallas kernels for 1% -> 2%
where the time goes in v6:
time: 104 us
  starting transfers between devices  45.2 us (43%)
  waiting for transfers between devices  40.3 us (39%)
  Pallas kernels  7.28 us (7%)
  other arithmetic  7.23 us (7%)
  local copies, waits for them, and re-layouts  2.08 us (2%)
  between operations  1.95 us (2%)
    ppermute x36, starting transfers between devices, send(): self.arrived[name] = lax.ppermute(self.hold(name, value), AXES, pairs)  45.2 us
    ppermute x36, waiting for transfers between devices, send(): self.arrived[name] = lax.ppermute(self.hold(name, value), AXES, pairs)  40.3 us
    pallas_call x1, Pallas kernels, first_blocks(): pl.pallas_call(first_kernel, in_specs=[pl.BlockSpec(memory_space=pltpu.SM...  5.71 us
    reduce_sum x4, other arithmetic, chosen_blocks(): jnp.sum(later[2 * j + i][:, None] * shard, axis=0).astype(jnp.bfloat16)  3.39 us
  transfers between devices with their start and end apart: 36, of which 18 were waited for; matrix products, arithmetic and copies ran while one was open for 5% of the time, Pallas kernels for 2%

profile of v6, /device:TPU:0, one launch (start us, length us, event | category | flops | bytes accessed | tf_op | source)
XLA Modules:
  0.0 104.1 jit_solution(10276782647034870417)
XLA Ops:
  1.3 5.7 %first_blocks.1 = (bf16[768,1024]{1,0:T(8,128)(2,1)S(1)}, bf16[1024,2048]{1,0:T(8,128)(2,1)S(1)}, bf16[3,4,96,512]{3,2,1,0:T(8,128)(2,1)S(1)}, bf16[3,4,96,512]{3,2,1,0:T(8,128)(2,1)S(1)}, f32[2,8,3,512]{3,2,1,0:T(4,128)S(1)}) custom-call(s32[1,1]{1,0:T(1,128)S(6)} %copy.16.count_ref, s32[4,8]{1,0:T(4,128)} %now_hbm.1, s32[4,8]{1,0:T(4,128)} %next_hbm.1, ...), custom_call_target="tpu_custom_call" | custom-call | flops 2415919104 | bytes 5767168 | tf_op jit(solution)/shard_map/first_blocks/pallas_call | solution.py:167
  7.0 0.5 collective-permute-start
  7.5 0.1 bitcast_convert_fusion.1
  7.7 2.3 %collective-permute-done = bf16[3,4,96,512]{3,2,1,0:T(8,128)(2,1)S(1)} collective-permute-done((bf16[3,4,96,512]{3,2,1,0:T(8,128)(2,1)S(1)}, bf16[3,4,96,512]{3,2,1,0:T(8,128)(2,1)S(1)}, u32[]{:S(2)}, u32[]{:S(2)}) %collective-permute-start) | collective-permute-done | bytes 1179680 | tf_op jit(solution)/shard_map/ppermute | solution.py:225
  10.2 2.9 %collective-permute-start.3 = (bf16[2,96,512]{2,1,0:T(8,128)(2,1)S(1)}, bf16[2,96,512]{2,1,0:T(8,128)(2,1)S(1)}, u32[]{:S(2)}, u32[]{:S(2)}) collective-permute-start(bf16[2,96,512]{2,1,0:T(8,128)(2,1)S(1)} %pad_maximum_fusion.14), channel_id=1, source_target_pairs={{0,8},{1,9},{2,10},{3,11},{4,12},{5,13},{6,14},{7,15},{8,0},{9,1},... | collective-permute-start | bytes 589832 | tf_op jit(solution)/shard_map/ppermute | solution.py:225
  13.1 1.6 %collective-permute-start.8 = (bf16[2,96,512]{2,1,0:T(8,128)(2,1)S(1)}, bf16[2,96,512]{2,1,0:T(8,128)(2,1)S(1)}, u32[]{:S(2)}, u32[]{:S(2)}) collective-permute-start(bf16[2,96,512]{2,1,0:T(8,128)(2,1)S(1)} %pad_maximum_fusion.18), channel_id=1, source_target_pairs={{0,16},{1,17},{2,18},{3,19},{4,20},{5,21},{6,22},{7,23},{8,24},{9,... | collective-permute-start | bytes 589832 | tf_op jit(solution)/shard_map/ppermute | solution.py:225
  14.7 0.6 collective-permute-start.14
  15.3 1.5 %collective-permute-start.4 = (bf16[2,96,512]{2,1,0:T(8,128)(2,1)S(1)}, bf16[2,96,512]{2,1,0:T(8,128)(2,1)S(1)}, u32[]{:S(2)}, u32[]{:S(2)}) collective-permute-start(bf16[2,96,512]{2,1,0:T(8,128)(2,1)S(1)} %pad_maximum_fusion.15), channel_id=1, source_target_pairs={{0,24},{1,25},{2,26},{3,27},{4,28},{5,29},{6,30},{7,31},{8,16},{9,... | collective-permute-start | bytes 589832 | tf_op jit(solution)/shard_map/ppermute | solution.py:225
  16.9 1.6 %collective-permute-start.1 = (bf16[2,96,512]{2,1,0:T(8,128)(2,1)S(1)}, bf16[2,96,512]{2,1,0:T(8,128)(2,1)S(1)}, u32[]{:S(2)}, u32[]{:S(2)}) collective-permute-start(bf16[2,96,512]{2,1,0:T(8,128)(2,1)S(1)} %pad_maximum_fusion.12), channel_id=1, source_target_pairs={{0,16},{1,17},{2,18},{3,19},{4,20},{5,21},{6,22},{7,23},{8,24},{9,... | collective-permute-start | bytes 589832 | tf_op jit(solution)/shard_map/ppermute | solution.py:225
  18.6 0.2 collective-permute-done.3
  18.8 2.1 %collective-permute-start.11 = (bf16[2,96,512]{2,1,0:T(8,128)(2,1)S(1)}, bf16[2,96,512]{2,1,0:T(8,128)(2,1)S(1)}, u32[]{:S(2)}, u32[]{:S(2)}) collective-permute-start(bf16[2,96,512]{2,1,0:T(8,128)(2,1)S(1)} %pad_maximum_fusion.20), channel_id=1, source_target_pairs={{0,16},{1,17},{2,18},{3,19},{4,20},{5,21},{6,22},{7,23},{8,24},{9,... | collective-permute-start | bytes 589832 | tf_op jit(solution)/shard_map/ppermute | solution.py:225
  20.9 7.1 %collective-permute-done.4 = bf16[2,96,512]{2,1,0:T(8,128)(2,1)S(1)} collective-permute-done((bf16[2,96,512]{2,1,0:T(8,128)(2,1)S(1)}, bf16[2,96,512]{2,1,0:T(8,128)(2,1)S(1)}, u32[]{:S(2)}, u32[]{:S(2)}) %collective-permute-start.4) | collective-permute-done | bytes 196640 | tf_op jit(solution)/shard_map/ppermute | solution.py:225
  28.0 1.4 %collective-permute-start.12 = (bf16[2,96,512]{2,1,0:T(8,128)(2,1)S(1)}, bf16[2,96,512]{2,1,0:T(8,128)(2,1)S(1)}, u32[]{:S(2)}, u32[]{:S(2)}) collective-permute-start(bf16[2,96,512]{2,1,0:T(8,128)(2,1)S(1)} %get-tuple-element.49), channel_id=1, source_target_pairs={{0,24},{1,25},{2,26},{3,27},{4,28},{5,29},{6,30},{7,31},{8,16},{9,... | collective-permute-start | bytes 589832 | tf_op jit(solution)/shard_map/ppermute | solution.py:225
  29.6 0.3 add_convert_fusion.2
  29.9 1.6 %collective-permute-start.5 = (bf16[3,96,512]{2,1,0:T(8,128)(2,1)S(1)}, bf16[3,96,512]{2,1,0:T(8,128)(2,1)S(1)}, u32[]{:S(2)}, u32[]{:S(2)}) collective-permute-start(bf16[3,96,512]{2,1,0:T(8,128)(2,1)S(1)} %add_convert_fusion.2), channel_id=1, source_target_pairs={{0,2},{1,3},{2,0},{3,1},{4,6},{5,7},{6,4},{7,5},{8,10},{9,11},{10,... | collective-permute-start | bytes 884744 | tf_op jit(solution)/shard_map/ppermute | solution.py:225
  31.5 1.6 %rest_blocks.1 = (bf16[1,4,96,512]{3,2,1,0:T(8,128)(2,1)S(1)}, bf16[1,4,96,512]{3,2,1,0:T(8,128)(2,1)S(1)}) custom-call(bf16[768,1024]{1,0:T(8,128)(2,1)S(1)} %get-tuple-element.40.turned_ref, bf16[1024,2048]{1,0:T(8,128)(2,1)S(1)} %get-tuple-element.41.upstream_ref), custom_call_target="tpu_custom_call" | custom-call | flops 805306368 | bytes 786432 | tf_op jit(solution)/shard_map/rest_blocks/pallas_call | solution.py:204
  33.1 0.6 collective-permute-start.10
  33.9 2.8 %collective-permute-done.11 = bf16[2,96,512]{2,1,0:T(8,128)(2,1)S(1)} collective-permute-done((bf16[2,96,512]{2,1,0:T(8,128)(2,1)S(1)}, bf16[2,96,512]{2,1,0:T(8,128)(2,1)S(1)}, u32[]{:S(2)}, u32[]{:S(2)}) %collective-permute-start.11) | collective-permute-done | bytes 196640 | tf_op jit(solution)/shard_map/ppermute | solution.py:225
  36.8 1.6 %collective-permute-start.15 = (bf16[2,96,512]{2,1,0:T(8,128)(2,1)S(1)}, bf16[2,96,512]{2,1,0:T(8,128)(2,1)S(1)}, u32[]{:S(2)}, u32[]{:S(2)}) collective-permute-start(bf16[2,96,512]{2,1,0:T(8,128)(2,1)S(1)} %pad_maximum_fusion.23), channel_id=1, source_target_pairs={{0,24},{1,25},{2,26},{3,27},{4,28},{5,29},{6,30},{7,31},{8,16},{9,... | collective-permute-start | bytes 589832 | tf_op jit(solution)/shard_map/ppermute | solution.py:225
  38.4 0.5 collective-permute-done.10
  38.9 0.4 add_convert_fusion.1
  39.3 3.2 %collective-permute-start.13 = (bf16[3,96,512]{2,1,0:T(8,128)(2,1)S(1)}, bf16[3,96,512]{2,1,0:T(8,128)(2,1)S(1)}, u32[]{:S(2)}, u32[]{:S(2)}) collective-permute-start(bf16[3,96,512]{2,1,0:T(8,128)(2,1)S(1)} %add_convert_fusion.1), channel_id=1, source_target_pairs={{0,6},{1,7},{2,4},{3,5},{4,2},{5,3},{6,0},{7,1},{8,14},{9,15},{10,... | collective-permute-start | bytes 884744 | tf_op jit(solution)/shard_map/ppermute | solution.py:225
  42.5 1.5 %collective-permute-done.15 = bf16[2,96,512]{2,1,0:T(8,128)(2,1)S(1)} collective-permute-done((bf16[2,96,512]{2,1,0:T(8,128)(2,1)S(1)}, bf16[2,96,512]{2,1,0:T(8,128)(2,1)S(1)}, u32[]{:S(2)}, u32[]{:S(2)}) %collective-permute-start.15) | collective-permute-done | bytes 196640 | tf_op jit(solution)/shard_map/ppermute | solution.py:225
  44.1 0.3 add_convert_fusion
  44.4 1.1 %collective-permute-start.16 = (bf16[3,96,512]{2,1,0:T(8,128)(2,1)S(1)}, bf16[3,96,512]{2,1,0:T(8,128)(2,1)S(1)}, u32[]{:S(2)}, u32[]{:S(2)}) collective-permute-start(bf16[3,96,512]{2,1,0:T(8,128)(2,1)S(1)} %add_convert_fusion), channel_id=1, source_target_pairs={{0,2},{1,3},{2,0},{3,1},{4,6},{5,7},{6,4},{7,5},{8,10},{9,11},{10,... | collective-permute-start | bytes 884744 | tf_op jit(solution)/shard_map/ppermute | solution.py:225
  45.6 1.5 %collective-permute-start.9 = (bf16[2,96,512]{2,1,0:T(8,128)(2,1)S(1)}, bf16[2,96,512]{2,1,0:T(8,128)(2,1)S(1)}, u32[]{:S(2)}, u32[]{:S(2)}) collective-permute-start(bf16[2,96,512]{2,1,0:T(8,128)(2,1)S(1)} %pad_maximum_fusion.17), channel_id=1, source_target_pairs={{0,24},{1,25},{2,26},{3,27},{4,28},{5,29},{6,30},{7,31},{8,16},{9,... | collective-permute-start | bytes 589832 | tf_op jit(solution)/shard_map/ppermute | solution.py:225
  47.1 1.6 %collective-permute-start.7 = (bf16[2,96,512]{2,1,0:T(8,128)(2,1)S(1)}, bf16[2,96,512]{2,1,0:T(8,128)(2,1)S(1)}, u32[]{:S(2)}, u32[]{:S(2)}) collective-permute-start(bf16[2,96,512]{2,1,0:T(8,128)(2,1)S(1)} %pad_maximum_fusion.16), channel_id=1, source_target_pairs={{0,16},{1,17},{2,18},{3,19},{4,20},{5,21},{6,22},{7,23},{8,24},{9,... | collective-permute-start | bytes 589832 | tf_op jit(solution)/shard_map/ppermute | solution.py:225
  48.7 0.6 collective-permute-start.6
  49.3 3.8 %collective-permute-done.9 = bf16[2,96,512]{2,1,0:T(8,128)(2,1)S(1)} collective-permute-done((bf16[2,96,512]{2,1,0:T(8,128)(2,1)S(1)}, bf16[2,96,512]{2,1,0:T(8,128)(2,1)S(1)}, u32[]{:S(2)}, u32[]{:S(2)}) %collective-permute-start.9) | collective-permute-done | bytes 196640 | tf_op jit(solution)/shard_map/ppermute | solution.py:225
  53.2 1.9 %collective-permute-done.7 = bf16[2,96,512]{2,1,0:T(8,128)(2,1)S(1)} collective-permute-done((bf16[2,96,512]{2,1,0:T(8,128)(2,1)S(1)}, bf16[2,96,512]{2,1,0:T(8,128)(2,1)S(1)}, u32[]{:S(2)}, u32[]{:S(2)}) %collective-permute-start.7) | collective-permute-done | bytes 196640 | tf_op jit(solution)/shard_map/ppermute | solution.py:225
  55.1 0.4 collective-permute-done.6
  55.7 2.3 %fusion.11 = (bf16[96,512]{1,0:T(8,128)(2,1)S(1)}, bf16[96,512]{1,0:T(8,128)(2,1)S(1)}, bf16[96,512]{1,0:T(8,128)(2,1)S(1)}, bf16[96,512]{1,0:T(8,128)(2,1)S(1)}...) fusion(f32[3,512]{1,0:T(4,128)S(1)} %get-tuple-element.230, ...), kind=kLoop, calls=%fused_computation.48 | loop fusion | flops 6832128 | bytes 6881280 | tf_op jit(solution)/shard_map/reduce_sum | solution.py:297
  58.0 1.5 %collective-permute-start.18 = (bf16[2,96,512]{2,1,0:T(8,128)(2,1)S(1)}, bf16[2,96,512]{2,1,0:T(8,128)(2,1)S(1)}, u32[]{:S(2)}, u32[]{:S(2)}) collective-permute-start(bf16[2,96,512]{2,1,0:T(8,128)(2,1)S(1)} %pad_maximum_fusion.25), channel_id=1, source_target_pairs={{0,16},{1,17},{2,18},{3,19},{4,20},{5,21},{6,22},{7,23},{8,24},{9,... | collective-permute-start | bytes 589832 | tf_op jit(solution)/shard_map/ppermute | solution.py:225
  59.5 0.5 collective-permute-start.19
  60.1 1.6 %collective-permute-start.17 = (bf16[2,96,512]{2,1,0:T(8,128)(2,1)S(1)}, bf16[2,96,512]{2,1,0:T(8,128)(2,1)S(1)}, u32[]{:S(2)}, u32[]{:S(2)}) collective-permute-start(bf16[2,96,512]{2,1,0:T(8,128)(2,1)S(1)} %pad_maximum_fusion.24), channel_id=1, source_target_pairs={{0,24},{1,25},{2,26},{3,27},{4,28},{5,29},{6,30},{7,31},{8,16},{9,... | collective-permute-start | bytes 589832 | tf_op jit(solution)/shard_map/ppermute | solution.py:225
  61.7 1.3 %collective-permute-start.22 = (bf16[3,96,512]{2,1,0:T(8,128)(2,1)S(1)}, bf16[3,96,512]{2,1,0:T(8,128)(2,1)S(1)}, u32[]{:S(2)}, u32[]{:S(2)}) collective-permute-start(bf16[3,96,512]{2,1,0:T(8,128)(2,1)S(1)} %get-tuple-element.53), channel_id=1, source_target_pairs={{0,2},{1,3},{2,0},{3,1},{4,6},{5,7},{6,4},{7,5},{8,10},{9,11},{10,... | collective-permute-start | bytes 884744 | tf_op jit(solution)/shard_map/ppermute | solution.py:225
  63.0 3.9 %collective-permute-done.19 = bf16[2,96,512]{2,1,0:T(8,128)(2,1)S(1)} collective-permute-done((bf16[2,96,512]{2,1,0:T(8,128)(2,1)S(1)}, bf16[2,96,512]{2,1,0:T(8,128)(2,1)S(1)}, u32[]{:S(2)}, u32[]{:S(2)}) %collective-permute-start.19) | collective-permute-done | bytes 196640 | tf_op jit(solution)/shard_map/ppermute | solution.py:225
  66.9 2.9 %collective-permute-start.20 = (bf16[3,96,512]{2,1,0:T(8,128)(2,1)S(1)}, bf16[3,96,512]{2,1,0:T(8,128)(2,1)S(1)}, u32[]{:S(2)}, u32[]{:S(2)}) collective-permute-start(bf16[3,96,512]{2,1,0:T(8,128)(2,1)S(1)} %get-tuple-element.53), channel_id=1, source_target_pairs={{0,6},{1,7},{2,4},{3,5},{4,2},{5,3},{6,0},{7,1},{8,14},{9,15},{10,... | collective-permute-start | bytes 884744 | tf_op jit(solution)/shard_map/ppermute | solution.py:225
  69.9 0.3 collective-permute-done.22
  70.2 0.4 fusion.19
  70.6 1.6 %collective-permute-start.23 = (bf16[2,96,512]{2,1,0:T(8,128)(2,1)S(1)}, bf16[2,96,512]{2,1,0:T(8,128)(2,1)S(1)}, u32[]{:S(2)}, u32[]{:S(2)}) collective-permute-start(bf16[2,96,512]{2,1,0:T(8,128)(2,1)S(1)} %pad_maximum_fusion.27), channel_id=1, source_target_pairs={{0,24},{1,25},{2,26},{3,27},{4,28},{5,29},{6,30},{7,31},{8,16},{9,... | collective-permute-start | bytes 589832 | tf_op jit(solution)/shard_map/ppermute | solution.py:225
  72.2 2.3 %collective-permute-start.24 = (bf16[2,96,512]{2,1,0:T(8,128)(2,1)S(1)}, bf16[2,96,512]{2,1,0:T(8,128)(2,1)S(1)}, u32[]{:S(2)}, u32[]{:S(2)}) collective-permute-start(bf16[2,96,512]{2,1,0:T(8,128)(2,1)S(1)} %pad_maximum_fusion.28), channel_id=1, source_target_pairs={{0,16},{1,17},{2,18},{3,19},{4,20},{5,21},{6,22},{7,23},{8,24},{9,... | collective-permute-start | bytes 589832 | tf_op jit(solution)/shard_map/ppermute | solution.py:225
  74.6 2.4 %collective-permute-done.20 = bf16[3,96,512]{2,1,0:T(8,128)(2,1)S(1)} collective-permute-done((bf16[3,96,512]{2,1,0:T(8,128)(2,1)S(1)}, bf16[3,96,512]{2,1,0:T(8,128)(2,1)S(1)}, u32[]{:S(2)}, u32[]{:S(2)}) %collective-permute-start.20) | collective-permute-done | bytes 294944 | tf_op jit(solution)/shard_map/ppermute | solution.py:225
  77.0 0.5 collective-permute-done.23
  77.5 0.4 fusion.27
  77.9 1.4 %collective-permute-start.26 = (bf16[2,96,512]{2,1,0:T(8,128)(2,1)S(1)}, bf16[2,96,512]{2,1,0:T(8,128)(2,1)S(1)}, u32[]{:S(2)}, u32[]{:S(2)}) collective-permute-start(bf16[2,96,512]{2,1,0:T(8,128)(2,1)S(1)} %pad_maximum_fusion.30), channel_id=1, source_target_pairs={{0,24},{1,25},{2,26},{3,27},{4,28},{5,29},{6,30},{7,31},{8,16},{9,... | collective-permute-start | bytes 589832 | tf_op jit(solution)/shard_map/ppermute | solution.py:225
  79.4 2.0 %collective-permute-start.30 = (bf16[3,96,512]{2,1,0:T(8,128)(2,1)S(1)}, bf16[3,96,512]{2,1,0:T(8,128)(2,1)S(1)}, u32[]{:S(2)}, u32[]{:S(2)}) collective-permute-start(bf16[3,96,512]{2,1,0:T(8,128)(2,1)S(1)} %collective-permute-done.20), channel_id=1, source_target_pairs={{0,2},{1,3},{2,0},{3,1},{4,6},{5,7},{6,4},{7,5},{8,10},{9,11},{10,... | collective-permute-start | bytes 884744 | tf_op jit(solution)/shard_map/ppermute | solution.py:225
  81.6 0.6 collective-permute-start.27
  82.2 1.5 %collective-permute-start.29 = (bf16[2,96,512]{2,1,0:T(8,128)(2,1)S(1)}, bf16[2,96,512]{2,1,0:T(8,128)(2,1)S(1)}, u32[]{:S(2)}, u32[]{:S(2)}) collective-permute-start(bf16[2,96,512]{2,1,0:T(8,128)(2,1)S(1)} %pad_maximum_fusion.32), channel_id=1, source_target_pairs={{0,8},{1,9},{2,10},{3,11},{4,12},{5,13},{6,14},{7,15},{8,0},{9,1},... | collective-permute-start | bytes 589832 | tf_op jit(solution)/shard_map/ppermute | solution.py:225
  83.7 2.2 %collective-permute-done.26 = bf16[2,96,512]{2,1,0:T(8,128)(2,1)S(1)} collective-permute-done((bf16[2,96,512]{2,1,0:T(8,128)(2,1)S(1)}, bf16[2,96,512]{2,1,0:T(8,128)(2,1)S(1)}, u32[]{:S(2)}, u32[]{:S(2)}) %collective-permute-start.26) | collective-permute-done | bytes 196640 | tf_op jit(solution)/shard_map/ppermute | solution.py:225
  85.9 2.9 %collective-permute-done.30 = bf16[3,96,512]{2,1,0:T(8,128)(2,1)S(1)} collective-permute-done((bf16[3,96,512]{2,1,0:T(8,128)(2,1)S(1)}, bf16[3,96,512]{2,1,0:T(8,128)(2,1)S(1)}, u32[]{:S(2)}, u32[]{:S(2)}) %collective-permute-start.30) | collective-permute-done | bytes 294944 | tf_op jit(solution)/shard_map/ppermute | solution.py:225
  88.8 0.4 fusion.35
  89.2 1.0 collective-permute-start.31
  90.2 1.1 %collective-permute-start.34 = (bf16[2,96,512]{2,1,0:T(8,128)(2,1)S(1)}, bf16[2,96,512]{2,1,0:T(8,128)(2,1)S(1)}, u32[]{:S(2)}, u32[]{:S(2)}) collective-permute-start(bf16[2,96,512]{2,1,0:T(8,128)(2,1)S(1)} %pad_maximum_fusion.35), channel_id=1, source_target_pairs={{0,16},{1,17},{2,18},{3,19},{4,20},{5,21},{6,22},{7,23},{8,24},{9,... | collective-permute-start | bytes 589832 | tf_op jit(solution)/shard_map/ppermute | solution.py:225
  91.4 1.6 %collective-permute-start.33 = (bf16[2,96,512]{2,1,0:T(8,128)(2,1)S(1)}, bf16[2,96,512]{2,1,0:T(8,128)(2,1)S(1)}, u32[]{:S(2)}, u32[]{:S(2)}) collective-permute-start(bf16[2,96,512]{2,1,0:T(8,128)(2,1)S(1)} %pad_maximum_fusion.34), channel_id=1, source_target_pairs={{0,24},{1,25},{2,26},{3,27},{4,28},{5,29},{6,30},{7,31},{8,16},{9,... | collective-permute-start | bytes 589832 | tf_op jit(solution)/shard_map/ppermute | solution.py:225
  93.0 0.2 broadcast_select_fusion.7
  93.1 0.4 broadcast_in_dim.14
  93.8 3.2 %collective-permute-done.31 = bf16[2,96,512]{2,1,0:T(8,128)(2,1)S(1)} collective-permute-done((bf16[2,96,512]{2,1,0:T(8,128)(2,1)S(1)}, bf16[2,96,512]{2,1,0:T(8,128)(2,1)S(1)}, u32[]{:S(2)}, u32[]{:S(2)}) %collective-permute-start.31) | collective-permute-done | bytes 196640 | tf_op jit(solution)/shard_map/ppermute | solution.py:225
  97.1 3.1 %collective-permute-done.34 = bf16[2,96,512]{2,1,0:T(8,128)(2,1)S(1)} collective-permute-done((bf16[2,96,512]{2,1,0:T(8,128)(2,1)S(1)}, bf16[2,96,512]{2,1,0:T(8,128)(2,1)S(1)}, u32[]{:S(2)}, u32[]{:S(2)}) %collective-permute-start.34) | collective-permute-done | bytes 196640 | tf_op jit(solution)/shard_map/ppermute | solution.py:225
  100.5 0.2 broadcast_select_fusion.5
  100.8 0.2 broadcast_select_fusion.3
  101.0 1.1 %collective-permute-done.35 = bf16[4,96,512]{2,1,0:T(8,128)(2,1)S(1)} collective-permute-done((bf16[4,96,512]{2,1,0:T(8,128)(2,1)S(1)}, bf16[4,96,512]{2,1,0:T(8,128)(2,1)S(1)}, u32[]{:S(2)}, u32[]{:S(2)}) %collective-permute-start.35) | collective-permute-done | bytes 393248 | tf_op jit(solution)/shard_map/ppermute | solution.py:225
  102.2 0.2 broadcast_select_fusion.1
  102.4 1.7 %copy-done = bf16[4,2,96,2048]{3,2,1,0:T(8,128)(2,1)} copy-done((bf16[4,2,96,2048]{3,2,1,0:T(8,128)(2,1)}, bf16[4,2,96,2048]{3,2,1,0:T(8,128)(2,1)S(1)}, u32[]{:S(2)}) %copy-start) | copy-done | bytes 3145752
  (90 shorter events, 2.5 us)
Async XLA Ops:
  7.0 3.0 %collective-permute-start = (bf16[3,4,96,512]{3,2,1,0:T(8,128)(2,1)S(1)}, bf16[3,4,96,512]{3,2,1,0:T(8,128)(2,1)S(1)}, u32[]{:S(2)}, u32[]{:S(2)}) collective-permute-start(bf16[3,4,96,512]{3,2,1,0:T(8,128)(2,1)S(1)} %get-tuple-element.39), channel_id=1, source_target_pairs={{0,1},{1,0},{2,3},{3,2},{4,5},{5,4},{6,7},{7,6},{8,9},{9,8},{10,11... | collective-permute-start | bytes 3538952 | tf_op jit(solution)/shard_map/ppermute | solution.py:225
  10.2 8.6 %collective-permute-start.3 = (bf16[2,96,512]{2,1,0:T(8,128)(2,1)S(1)}, bf16[2,96,512]{2,1,0:T(8,128)(2,1)S(1)}, u32[]{:S(2)}, u32[]{:S(2)}) collective-permute-start(bf16[2,96,512]{2,1,0:T(8,128)(2,1)S(1)} %pad_maximum_fusion.14), channel_id=1, source_target_pairs={{0,8},{1,9},{2,10},{3,11},{4,12},{5,13},{6,14},{7,15},{8,0},{9,1},... | collective-permute-start | bytes 589832 | tf_op jit(solution)/shard_map/ppermute | solution.py:225
  13.1 20.0 %collective-permute-start.8 = (bf16[2,96,512]{2,1,0:T(8,128)(2,1)S(1)}, bf16[2,96,512]{2,1,0:T(8,128)(2,1)S(1)}, u32[]{:S(2)}, u32[]{:S(2)}) collective-permute-start(bf16[2,96,512]{2,1,0:T(8,128)(2,1)S(1)} %pad_maximum_fusion.18), channel_id=1, source_target_pairs={{0,16},{1,17},{2,18},{3,19},{4,20},{5,21},{6,22},{7,23},{8,24},{9,... | collective-permute-start | bytes 589832 | tf_op jit(solution)/shard_map/ppermute | solution.py:225
  14.7 19.0 %collective-permute-start.14 = (bf16[2,96,512]{2,1,0:T(8,128)(2,1)S(1)}, bf16[2,96,512]{2,1,0:T(8,128)(2,1)S(1)}, u32[]{:S(2)}, u32[]{:S(2)}) collective-permute-start(bf16[2,96,512]{2,1,0:T(8,128)(2,1)S(1)} %pad_maximum_fusion.22), channel_id=1, source_target_pairs={{0,8},{1,9},{2,10},{3,11},{4,12},{5,13},{6,14},{7,15},{8,0},{9,1},... | collective-permute-start | bytes 589832 | tf_op jit(solution)/shard_map/ppermute | solution.py:225
  15.3 12.7 %collective-permute-start.4 = (bf16[2,96,512]{2,1,0:T(8,128)(2,1)S(1)}, bf16[2,96,512]{2,1,0:T(8,128)(2,1)S(1)}, u32[]{:S(2)}, u32[]{:S(2)}) collective-permute-start(bf16[2,96,512]{2,1,0:T(8,128)(2,1)S(1)} %pad_maximum_fusion.15), channel_id=1, source_target_pairs={{0,24},{1,25},{2,26},{3,27},{4,28},{5,29},{6,30},{7,31},{8,16},{9,... | collective-permute-start | bytes 589832 | tf_op jit(solution)/shard_map/ppermute | solution.py:225
  16.9 12.6 %collective-permute-start.1 = (bf16[2,96,512]{2,1,0:T(8,128)(2,1)S(1)}, bf16[2,96,512]{2,1,0:T(8,128)(2,1)S(1)}, u32[]{:S(2)}, u32[]{:S(2)}) collective-permute-start(bf16[2,96,512]{2,1,0:T(8,128)(2,1)S(1)} %pad_maximum_fusion.12), channel_id=1, source_target_pairs={{0,16},{1,17},{2,18},{3,19},{4,20},{5,21},{6,22},{7,23},{8,24},{9,... | collective-permute-start | bytes 589832 | tf_op jit(solution)/shard_map/ppermute | solution.py:225
  18.8 17.9 %collective-permute-start.11 = (bf16[2,96,512]{2,1,0:T(8,128)(2,1)S(1)}, bf16[2,96,512]{2,1,0:T(8,128)(2,1)S(1)}, u32[]{:S(2)}, u32[]{:S(2)}) collective-permute-start(bf16[2,96,512]{2,1,0:T(8,128)(2,1)S(1)} %pad_maximum_fusion.20), channel_id=1, source_target_pairs={{0,16},{1,17},{2,18},{3,19},{4,20},{5,21},{6,22},{7,23},{8,24},{9,... | collective-permute-start | bytes 589832 | tf_op jit(solution)/shard_map/ppermute | solution.py:225
  28.0 8.8 %collective-permute-start.12 = (bf16[2,96,512]{2,1,0:T(8,128)(2,1)S(1)}, bf16[2,96,512]{2,1,0:T(8,128)(2,1)S(1)}, u32[]{:S(2)}, u32[]{:S(2)}) collective-permute-start(bf16[2,96,512]{2,1,0:T(8,128)(2,1)S(1)} %get-tuple-element.49), channel_id=1, source_target_pairs={{0,24},{1,25},{2,26},{3,27},{4,28},{5,29},{6,30},{7,31},{8,16},{9,... | collective-permute-start | bytes 589832 | tf_op jit(solution)/shard_map/ppermute | solution.py:225
  29.9 9.0 %collective-permute-start.5 = (bf16[3,96,512]{2,1,0:T(8,128)(2,1)S(1)}, bf16[3,96,512]{2,1,0:T(8,128)(2,1)S(1)}, u32[]{:S(2)}, u32[]{:S(2)}) collective-permute-start(bf16[3,96,512]{2,1,0:T(8,128)(2,1)S(1)} %add_convert_fusion.2), channel_id=1, source_target_pairs={{0,2},{1,3},{2,0},{3,1},{4,6},{5,7},{6,4},{7,5},{8,10},{9,11},{10,... | collective-permute-start | bytes 884744 | tf_op jit(solution)/shard_map/ppermute | solution.py:225
  33.1 5.7 %collective-permute-start.10 = (bf16[2,96,512]{2,1,0:T(8,128)(2,1)S(1)}, bf16[2,96,512]{2,1,0:T(8,128)(2,1)S(1)}, u32[]{:S(2)}, u32[]{:S(2)}) collective-permute-start(bf16[2,96,512]{2,1,0:T(8,128)(2,1)S(1)} %get-tuple-element.48), channel_id=1, source_target_pairs={{0,8},{1,9},{2,10},{3,11},{4,12},{5,13},{6,14},{7,15},{8,0},{9,1},... | collective-permute-start | bytes 589832 | tf_op jit(solution)/shard_map/ppermute | solution.py:225
  33.8 11.7 %collective-permute-start.2 = (bf16[4,96,512]{2,1,0:T(8,128)(2,1)S(1)}, bf16[4,96,512]{2,1,0:T(8,128)(2,1)S(1)}, u32[]{:S(2)}, u32[]{:S(2)}) collective-permute-start(bf16[4,96,512]{2,1,0:T(8,128)(2,1)S(1)} %bitcast.350), channel_id=1, source_target_pairs={{0,1},{1,0},{2,3},{3,2},{4,5},{5,4},{6,7},{7,6},{8,9},{9,8},{10,11... | collective-permute-start | bytes 1179656 | tf_op jit(solution)/shard_map/ppermute | solution.py:225
  36.8 7.2 %collective-permute-start.15 = (bf16[2,96,512]{2,1,0:T(8,128)(2,1)S(1)}, bf16[2,96,512]{2,1,0:T(8,128)(2,1)S(1)}, u32[]{:S(2)}, u32[]{:S(2)}) collective-permute-start(bf16[2,96,512]{2,1,0:T(8,128)(2,1)S(1)} %pad_maximum_fusion.23), channel_id=1, source_target_pairs={{0,24},{1,25},{2,26},{3,27},{4,28},{5,29},{6,30},{7,31},{8,16},{9,... | collective-permute-start | bytes 589832 | tf_op jit(solution)/shard_map/ppermute | solution.py:225
  39.3 16.3 %collective-permute-start.13 = (bf16[3,96,512]{2,1,0:T(8,128)(2,1)S(1)}, bf16[3,96,512]{2,1,0:T(8,128)(2,1)S(1)}, u32[]{:S(2)}, u32[]{:S(2)}) collective-permute-start(bf16[3,96,512]{2,1,0:T(8,128)(2,1)S(1)} %add_convert_fusion.1), channel_id=1, source_target_pairs={{0,6},{1,7},{2,4},{3,5},{4,2},{5,3},{6,0},{7,1},{8,14},{9,15},{10,... | collective-permute-start | bytes 884744 | tf_op jit(solution)/shard_map/ppermute | solution.py:225
  44.4 11.2 %collective-permute-start.16 = (bf16[3,96,512]{2,1,0:T(8,128)(2,1)S(1)}, bf16[3,96,512]{2,1,0:T(8,128)(2,1)S(1)}, u32[]{:S(2)}, u32[]{:S(2)}) collective-permute-start(bf16[3,96,512]{2,1,0:T(8,128)(2,1)S(1)} %add_convert_fusion), channel_id=1, source_target_pairs={{0,2},{1,3},{2,0},{3,1},{4,6},{5,7},{6,4},{7,5},{8,10},{9,11},{10,... | collective-permute-start | bytes 884744 | tf_op jit(solution)/shard_map/ppermute | solution.py:225
  45.5 10.1 %copy-start.1 = (f32[3,96,512]{2,1,0:T(8,128)S(1)}, f32[3,96,512]{2,1,0:T(8,128)}, u32[]{:S(2)}) copy-start(f32[3,96,512]{2,1,0:T(8,128)} %param.13) | copy-start | bytes 1769476
  45.5 10.1 %copy-start.2 = (f32[3,96,512]{2,1,0:T(8,128)S(1)}, f32[3,96,512]{2,1,0:T(8,128)}, u32[]{:S(2)}) copy-start(f32[3,96,512]{2,1,0:T(8,128)} %param.14) | copy-start | bytes 1769476
  45.5 10.1 %copy-start.3 = (f32[3,96,512]{2,1,0:T(8,128)S(1)}, f32[3,96,512]{2,1,0:T(8,128)}, u32[]{:S(2)}) copy-start(f32[3,96,512]{2,1,0:T(8,128)} %param.15) | copy-start | bytes 1769476
  45.6 7.5 %collective-permute-start.9 = (bf16[2,96,512]{2,1,0:T(8,128)(2,1)S(1)}, bf16[2,96,512]{2,1,0:T(8,128)(2,1)S(1)}, u32[]{:S(2)}, u32[]{:S(2)}) collective-permute-start(bf16[2,96,512]{2,1,0:T(8,128)(2,1)S(1)} %pad_maximum_fusion.17), channel_id=1, source_target_pairs={{0,24},{1,25},{2,26},{3,27},{4,28},{5,29},{6,30},{7,31},{8,16},{9,... | collective-permute-start | bytes 589832 | tf_op jit(solution)/shard_map/ppermute | solution.py:225
  47.1 8.0 %collective-permute-start.7 = (bf16[2,96,512]{2,1,0:T(8,128)(2,1)S(1)}, bf16[2,96,512]{2,1,0:T(8,128)(2,1)S(1)}, u32[]{:S(2)}, u32[]{:S(2)}) collective-permute-start(bf16[2,96,512]{2,1,0:T(8,128)(2,1)S(1)} %pad_maximum_fusion.16), channel_id=1, source_target_pairs={{0,16},{1,17},{2,18},{3,19},{4,20},{5,21},{6,22},{7,23},{8,24},{9,... | collective-permute-start | bytes 589832 | tf_op jit(solution)/shard_map/ppermute | solution.py:225
  48.7 6.9 %collective-permute-start.6 = (bf16[2,96,512]{2,1,0:T(8,128)(2,1)S(1)}, bf16[2,96,512]{2,1,0:T(8,128)(2,1)S(1)}, u32[]{:S(2)}, u32[]{:S(2)}) collective-permute-start(bf16[2,96,512]{2,1,0:T(8,128)(2,1)S(1)} %pad_maximum_fusion.13), channel_id=1, source_target_pairs={{0,8},{1,9},{2,10},{3,11},{4,12},{5,13},{6,14},{7,15},{8,0},{9,1},... | collective-permute-start | bytes 589832 | tf_op jit(solution)/shard_map/ppermute | solution.py:225
  58.0 11.8 %collective-permute-start.18 = (bf16[2,96,512]{2,1,0:T(8,128)(2,1)S(1)}, bf16[2,96,512]{2,1,0:T(8,128)(2,1)S(1)}, u32[]{:S(2)}, u32[]{:S(2)}) collective-permute-start(bf16[2,96,512]{2,1,0:T(8,128)(2,1)S(1)} %pad_maximum_fusion.25), channel_id=1, source_target_pairs={{0,16},{1,17},{2,18},{3,19},{4,20},{5,21},{6,22},{7,23},{8,24},{9,... | collective-permute-start | bytes 589832 | tf_op jit(solution)/shard_map/ppermute | solution.py:225
  59.5 7.4 %collective-permute-start.19 = (bf16[2,96,512]{2,1,0:T(8,128)(2,1)S(1)}, bf16[2,96,512]{2,1,0:T(8,128)(2,1)S(1)}, u32[]{:S(2)}, u32[]{:S(2)}) collective-permute-start(bf16[2,96,512]{2,1,0:T(8,128)(2,1)S(1)} %pad_maximum_fusion.26), channel_id=1, source_target_pairs={{0,8},{1,9},{2,10},{3,11},{4,12},{5,13},{6,14},{7,15},{8,0},{9,1},... | collective-permute-start | bytes 589832 | tf_op jit(solution)/shard_map/ppermute | solution.py:225
  60.1 9.7 %collective-permute-start.17 = (bf16[2,96,512]{2,1,0:T(8,128)(2,1)S(1)}, bf16[2,96,512]{2,1,0:T(8,128)(2,1)S(1)}, u32[]{:S(2)}, u32[]{:S(2)}) collective-permute-start(bf16[2,96,512]{2,1,0:T(8,128)(2,1)S(1)} %pad_maximum_fusion.24), channel_id=1, source_target_pairs={{0,24},{1,25},{2,26},{3,27},{4,28},{5,29},{6,30},{7,31},{8,16},{9,... | collective-permute-start | bytes 589832 | tf_op jit(solution)/shard_map/ppermute | solution.py:225
  61.7 8.5 %collective-permute-start.22 = (bf16[3,96,512]{2,1,0:T(8,128)(2,1)S(1)}, bf16[3,96,512]{2,1,0:T(8,128)(2,1)S(1)}, u32[]{:S(2)}, u32[]{:S(2)}) collective-permute-start(bf16[3,96,512]{2,1,0:T(8,128)(2,1)S(1)} %get-tuple-element.53), channel_id=1, source_target_pairs={{0,2},{1,3},{2,0},{3,1},{4,6},{5,7},{6,4},{7,5},{8,10},{9,11},{10,... | collective-permute-start | bytes 884744 | tf_op jit(solution)/shard_map/ppermute | solution.py:225
  66.9 10.1 %collective-permute-start.20 = (bf16[3,96,512]{2,1,0:T(8,128)(2,1)S(1)}, bf16[3,96,512]{2,1,0:T(8,128)(2,1)S(1)}, u32[]{:S(2)}, u32[]{:S(2)}) collective-permute-start(bf16[3,96,512]{2,1,0:T(8,128)(2,1)S(1)} %get-tuple-element.53), channel_id=1, source_target_pairs={{0,6},{1,7},{2,4},{3,5},{4,2},{5,3},{6,0},{7,1},{8,14},{9,15},{10,... | collective-permute-start | bytes 884744 | tf_op jit(solution)/shard_map/ppermute | solution.py:225
  70.6 6.9 %collective-permute-start.23 = (bf16[2,96,512]{2,1,0:T(8,128)(2,1)S(1)}, bf16[2,96,512]{2,1,0:T(8,128)(2,1)S(1)}, u32[]{:S(2)}, u32[]{:S(2)}) collective-permute-start(bf16[2,96,512]{2,1,0:T(8,128)(2,1)S(1)} %pad_maximum_fusion.27), channel_id=1, source_target_pairs={{0,24},{1,25},{2,26},{3,27},{4,28},{5,29},{6,30},{7,31},{8,16},{9,... | collective-permute-start | bytes 589832 | tf_op jit(solution)/shard_map/ppermute | solution.py:225
  72.2 9.2 %collective-permute-start.24 = (bf16[2,96,512]{2,1,0:T(8,128)(2,1)S(1)}, bf16[2,96,512]{2,1,0:T(8,128)(2,1)S(1)}, u32[]{:S(2)}, u32[]{:S(2)}) collective-permute-start(bf16[2,96,512]{2,1,0:T(8,128)(2,1)S(1)} %pad_maximum_fusion.28), channel_id=1, source_target_pairs={{0,16},{1,17},{2,18},{3,19},{4,20},{5,21},{6,22},{7,23},{8,24},{9,... | collective-permute-start | bytes 589832 | tf_op jit(solution)/shard_map/ppermute | solution.py:225
  74.5 6.9 %collective-permute-start.25 = (bf16[2,96,512]{2,1,0:T(8,128)(2,1)S(1)}, bf16[2,96,512]{2,1,0:T(8,128)(2,1)S(1)}, u32[]{:S(2)}, u32[]{:S(2)}) collective-permute-start(bf16[2,96,512]{2,1,0:T(8,128)(2,1)S(1)} %pad_maximum_fusion.29), channel_id=1, source_target_pairs={{0,8},{1,9},{2,10},{3,11},{4,12},{5,13},{6,14},{7,15},{8,0},{9,1},... | collective-permute-start | bytes 589832 | tf_op jit(solution)/shard_map/ppermute | solution.py:225
  77.0 4.6 %collective-permute-start.21 = (bf16[4,96,512]{2,1,0:T(8,128)(2,1)S(1)}, bf16[4,96,512]{2,1,0:T(8,128)(2,1)S(1)}, u32[]{:S(2)}, u32[]{:S(2)}) collective-permute-start(bf16[4,96,512]{2,1,0:T(8,128)(2,1)S(1)} %pad_maximum_fusion.1), channel_id=1, source_target_pairs={{0,1},{1,0},{2,3},{3,2},{4,5},{5,4},{6,7},{7,6},{8,9},{9,8},{10,11... | collective-permute-start | bytes 1179656 | tf_op jit(solution)/shard_map/ppermute | solution.py:225
  77.9 8.0 %collective-permute-start.26 = (bf16[2,96,512]{2,1,0:T(8,128)(2,1)S(1)}, bf16[2,96,512]{2,1,0:T(8,128)(2,1)S(1)}, u32[]{:S(2)}, u32[]{:S(2)}) collective-permute-start(bf16[2,96,512]{2,1,0:T(8,128)(2,1)S(1)} %pad_maximum_fusion.30), channel_id=1, source_target_pairs={{0,24},{1,25},{2,26},{3,27},{4,28},{5,29},{6,30},{7,31},{8,16},{9,... | collective-permute-start | bytes 589832 | tf_op jit(solution)/shard_map/ppermute | solution.py:225
  79.4 9.4 %collective-permute-start.30 = (bf16[3,96,512]{2,1,0:T(8,128)(2,1)S(1)}, bf16[3,96,512]{2,1,0:T(8,128)(2,1)S(1)}, u32[]{:S(2)}, u32[]{:S(2)}) collective-permute-start(bf16[3,96,512]{2,1,0:T(8,128)(2,1)S(1)} %collective-permute-done.20), channel_id=1, source_target_pairs={{0,2},{1,3},{2,0},{3,1},{4,6},{5,7},{6,4},{7,5},{8,10},{9,11},{10,... | collective-permute-start | bytes 884744 | tf_op jit(solution)/shard_map/ppermute | solution.py:225
  81.6 12.0 %collective-permute-start.27 = (bf16[2,96,512]{2,1,0:T(8,128)(2,1)S(1)}, bf16[2,96,512]{2,1,0:T(8,128)(2,1)S(1)}, u32[]{:S(2)}, u32[]{:S(2)}) collective-permute-start(bf16[2,96,512]{2,1,0:T(8,128)(2,1)S(1)} %pad_maximum_fusion.31), channel_id=1, source_target_pairs={{0,16},{1,17},{2,18},{3,19},{4,20},{5,21},{6,22},{7,23},{8,24},{9,... | collective-permute-start | bytes 589832 | tf_op jit(solution)/shard_map/ppermute | solution.py:225
  82.2 11.5 %collective-permute-start.29 = (bf16[2,96,512]{2,1,0:T(8,128)(2,1)S(1)}, bf16[2,96,512]{2,1,0:T(8,128)(2,1)S(1)}, u32[]{:S(2)}, u32[]{:S(2)}) collective-permute-start(bf16[2,96,512]{2,1,0:T(8,128)(2,1)S(1)} %pad_maximum_fusion.32), channel_id=1, source_target_pairs={{0,8},{1,9},{2,10},{3,11},{4,12},{5,13},{6,14},{7,15},{8,0},{9,1},... | collective-permute-start | bytes 589832 | tf_op jit(solution)/shard_map/ppermute | solution.py:225
  89.2 7.9 %collective-permute-start.31 = (bf16[2,96,512]{2,1,0:T(8,128)(2,1)S(1)}, bf16[2,96,512]{2,1,0:T(8,128)(2,1)S(1)}, u32[]{:S(2)}, u32[]{:S(2)}) collective-permute-start(bf16[2,96,512]{2,1,0:T(8,128)(2,1)S(1)} %pad_maximum_fusion.33), channel_id=1, source_target_pairs={{0,8},{1,9},{2,10},{3,11},{4,12},{5,13},{6,14},{7,15},{8,0},{9,1},... | collective-permute-start | bytes 589832 | tf_op jit(solution)/shard_map/ppermute | solution.py:225
  90.2 9.9 %collective-permute-start.34 = (bf16[2,96,512]{2,1,0:T(8,128)(2,1)S(1)}, bf16[2,96,512]{2,1,0:T(8,128)(2,1)S(1)}, u32[]{:S(2)}, u32[]{:S(2)}) collective-permute-start(bf16[2,96,512]{2,1,0:T(8,128)(2,1)S(1)} %pad_maximum_fusion.35), channel_id=1, source_target_pairs={{0,16},{1,17},{2,18},{3,19},{4,20},{5,21},{6,22},{7,23},{8,24},{9,... | collective-permute-start | bytes 589832 | tf_op jit(solution)/shard_map/ppermute | solution.py:225
  91.4 8.8 %collective-permute-start.33 = (bf16[2,96,512]{2,1,0:T(8,128)(2,1)S(1)}, bf16[2,96,512]{2,1,0:T(8,128)(2,1)S(1)}, u32[]{:S(2)}, u32[]{:S(2)}) collective-permute-start(bf16[2,96,512]{2,1,0:T(8,128)(2,1)S(1)} %pad_maximum_fusion.34), channel_id=1, source_target_pairs={{0,24},{1,25},{2,26},{3,27},{4,28},{5,29},{6,30},{7,31},{8,16},{9,... | collective-permute-start | bytes 589832 | tf_op jit(solution)/shard_map/ppermute | solution.py:225
  93.6 6.8 %collective-permute-start.28 = (bf16[4,96,512]{2,1,0:T(8,128)(2,1)S(1)}, bf16[4,96,512]{2,1,0:T(8,128)(2,1)S(1)}, u32[]{:S(2)}, u32[]{:S(2)}) collective-permute-start(bf16[4,96,512]{2,1,0:T(8,128)(2,1)S(1)} %pad_maximum_fusion.4), channel_id=1, source_target_pairs={{0,1},{1,0},{2,3},{3,2},{4,5},{5,4},{6,7},{7,6},{8,9},{9,8},{10,11... | collective-permute-start | bytes 1179656 | tf_op jit(solution)/shard_map/ppermute | solution.py:225
  97.1 3.6 %collective-permute-start.32 = (bf16[4,96,512]{2,1,0:T(8,128)(2,1)S(1)}, bf16[4,96,512]{2,1,0:T(8,128)(2,1)S(1)}, u32[]{:S(2)}, u32[]{:S(2)}) collective-permute-start(bf16[4,96,512]{2,1,0:T(8,128)(2,1)S(1)} %pad_maximum_fusion.7), channel_id=1, source_target_pairs={{0,1},{1,0},{2,3},{3,2},{4,5},{5,4},{6,7},{7,6},{8,9},{9,8},{10,11... | collective-permute-start | bytes 1179656 | tf_op jit(solution)/shard_map/ppermute | solution.py:225
  100.3 1.8 %collective-permute-start.35 = (bf16[4,96,512]{2,1,0:T(8,128)(2,1)S(1)}, bf16[4,96,512]{2,1,0:T(8,128)(2,1)S(1)}, u32[]{:S(2)}, u32[]{:S(2)}) collective-permute-start(bf16[4,96,512]{2,1,0:T(8,128)(2,1)S(1)} %pad_maximum_fusion.10), channel_id=1, source_target_pairs={{0,1},{1,0},{2,3},{3,2},{4,5},{5,4},{6,7},{7,6},{8,9},{9,8},{10,11... | collective-permute-start | bytes 1179656 | tf_op jit(solution)/shard_map/ppermute | solution.py:225
  102.4 1.7 %copy-start = (bf16[4,2,96,2048]{3,2,1,0:T(8,128)(2,1)}, bf16[4,2,96,2048]{3,2,1,0:T(8,128)(2,1)S(1)}, u32[]{:S(2)}) copy-start(bf16[4,2,96,2048]{3,2,1,0:T(8,128)(2,1)S(1)} %fusion.3) | copy-start | bytes 9437188
